TPU v7x, 32 devices: a whole 2x2x4 slice. The times are simulated.
32 devices in a mesh: pool: 8 (over z, y), tp: 4 (over x, core).
Axes of the slice: x: 2, y: 2, z: 4, core: 2. Of those that a mesh axis runs over, the one named last changes fastest.
Arguments:
- queries: bfloat16 [1024, 64, 128], P(('pool', 'tp')), may hold values from -6 to 6
- fresh_key_values: bfloat16 [1024, 4, 2, 128], P(('pool', 'tp')), may hold values from -5 to 5
- pooled_page_cache: bfloat16 [5, 8, 8, 4, 2, 128], P(None, 'pool', None, 'tp'), may hold values from -5 to 5
- leaf_cache: bfloat16 [8, 256, 4, 2, 128], P('pool', None, 'tp'), may hold values from -5 to 5
- parent: int32 [13], replicated, may hold values from 0 to 4, as said below
- node_pages: int32 [5], replicated, may hold values from 4 to 8
- node_owner: int32 [5], replicated, may hold values from 0 to 7
- leaf_len: int32 [8], P('pool'), may hold values from 1 to 32
Outputs:
- attended: bfloat16 [1024, 64, 128], P(('pool', 'tp'))
Inputs may be any that keep to these rules, and one draw needn't show every extreme that they name: Nodes 0 to 4 have parent 0; node 5 + r is request r's own node and its parent is one of nodes 1 to 4.
All inputs are finite; a program needn't handle non-finite values.
Results may differ from a plain program's by a relative error of at most 0.008.
Values may be sent and summed in bfloat16 or wider, within the bound.
No kernel may reach another device: no remote copies, remote signals or barrier semaphores. Data moves between devices by JAX's collectives and lax.ppermute only.
A program may use at most 64 MiB of HBM per device.

v0:
```python
import jax
import jax.numpy as jnp
from jax import lax
from jax.sharding import PartitionSpec as P


def attend(carried, query_tile, key_pairs, key_mask, batched):
    running, totals, accum = carried
    inv_root = query_tile.shape[-1] ** (-0.5)
    score_form = "btkgd,bskd->btkgs" if batched else "btkgd,skd->btkgs"
    value_form = "btkgs,bskd->btkgd" if batched else "btkgs,skd->btkgd"
    scores = (
        jnp.einsum(score_form, query_tile, key_pairs[..., 0, :], preferred_element_type=jnp.float32)
        * inv_root
    )
    wide_mask = key_mask[:, :, None, None, :]
    scores = jnp.where(wide_mask, scores, jnp.float32(-1e30))
    new_max = jnp.maximum(running, jnp.max(scores, axis=-1))
    weights = jnp.where(wide_mask, jnp.exp(scores - new_max[..., None]), jnp.float32(0.0))
    rescale = jnp.exp(running - new_max)
    totals = totals * rescale + jnp.sum(weights, axis=-1)
    accum = accum * rescale[..., None] + jnp.einsum(
        value_form,
        weights.astype(jnp.bfloat16),
        key_pairs[..., 1, :],
        preferred_element_type=jnp.float32,
    )
    return (new_max, totals, accum)


def per_device(
    queries,
    fresh_key_values,
    pooled_page_cache,
    leaf_cache,
    parent,
    node_pages,
    node_owner,
    leaf_len,
):
    heads_q, heads_kv = (
        lax.all_to_all(queries, "tp", split_axis=1, concat_axis=0, tiled=True),
        lax.all_to_all(fresh_key_values, "tp", split_axis=1, concat_axis=0, tiled=True),
    )
    pool_size = lax.axis_size("pool")
    pool_index = lax.axis_index("pool")
    requests = leaf_cache.shape[0]
    tile_rows = heads_q.shape[0] // requests
    kv_local = heads_kv.shape[1]
    query_group_width = heads_q.shape[1] // kv_local
    head_dim = heads_q.shape[2]
    page_len = pooled_page_cache.shape[2]
    shared_count = pooled_page_cache.shape[0]
    mids_count = shared_count - 1
    query_tile = heads_q.reshape(requests, tile_rows, kv_local, query_group_width, head_dim)
    suffix_kv = heads_kv.reshape(requests, tile_rows, kv_local, 2, head_dim)
    my_mids = lax.dynamic_slice_in_dim(parent, 1 + mids_count + pool_index * requests, requests)
    carried = (
        jnp.full((requests, tile_rows, kv_local, query_group_width), -1e30, jnp.float32),
        jnp.zeros((requests, tile_rows, kv_local, query_group_width), jnp.float32),
        jnp.zeros((requests, tile_rows, kv_local, query_group_width, head_dim), jnp.float32),
    )
    fold_carried = carried
    pieces = lax.all_gather(pooled_page_cache, "pool", axis=1, tiled=True)
    stripes = pieces.shape[1]
    slot_ids = jnp.arange(stripes, dtype=jnp.int32)
    for node_id in range(shared_count):
        usable = jnp.mod(slot_ids - node_owner[node_id], pool_size) < node_pages[node_id]
        usable = jnp.repeat(usable, page_len)
        if node_id == 0:
            relevant = jnp.ones((requests,), bool)
        else:
            relevant = my_mids == node_id
        key_mask = relevant[:, None, None] & usable[None, None, :]
        key_pairs = pieces[node_id].reshape(stripes * page_len, kv_local, 2, head_dim)
        fold_carried = attend(fold_carried, query_tile, key_pairs, key_mask, False)
    carried = fold_carried
    leaf_mask = (
        jnp.arange(leaf_cache.shape[1], dtype=jnp.int32)[None, :] < (leaf_len * page_len)[:, None]
    )
    carried = attend(carried, query_tile, leaf_cache, leaf_mask[:, None, :], True)
    row_ids = jnp.arange(tile_rows, dtype=jnp.int32)
    causal = (row_ids[None, :] <= row_ids[:, None])[None]
    carried = attend(carried, query_tile, suffix_kv, causal, True)
    running, totals, accum = carried
    result = (accum / totals[..., None]).astype(jnp.bfloat16)
    result = result.reshape(requests * tile_rows, kv_local * query_group_width, head_dim)
    return lax.all_to_all(result, "tp", split_axis=0, concat_axis=1, tiled=True)


def solution(mesh):
    return jax.shard_map(
        per_device,
        mesh=mesh,
        in_specs=(
            P(("pool", "tp"), None, None),
            P(("pool", "tp"), None, None, None),
            P(None, "pool", None, "tp", None, None),
            P("pool", None, "tp", None, None),
            P(),
            P(),
            P(),
            P("pool"),
        ),
        out_specs=P(("pool", "tp"), None, None),
        check_vma=False,
    )
```

profile of v0, /device:TPU:0, one launch (start us, length us, event | category | flops | bytes accessed | tf_op | source)
XLA Modules:
  0.0 86.5 jit_solution(16569611497028346015)
XLA Ops:
  0.0 1.5 %copy.31 = bf16[32,4,2,128]{3,2,0,1:T(2,128)(2,1)} copy(bf16[32,4,2,128]{3,2,1,0:T(2,128)(2,1)} %param.9) | data formatting | bytes 131072 | tf_op args[1]
  1.5 4.2 %all-to-all-start.1 = ((bf16[32,4,2,128]{3,2,0,1:T(2,128)(2,1)}), bf16[32,4,2,128]{3,2,0,1:T(2,128)(2,1)S(1)}, u32[]{:S(2)}, u32[]{:S(2)}) async-start(bf16[32,4,2,128]{3,2,0,1:T(2,128)(2,1)} %copy.31), calls=%async_computation.1 | async-start | bytes 131072 | tf_op jit(solution)/shard_map/all_to_all | solution.py:43
  6.4 1.2 %dynamic_slice.3 = s32[1]{0:T(128)} dynamic-slice(s32[13]{0:T(128)} %param.12, s32[]{:T(128)S(6)} %select_n.93), dynamic_slice_sizes={1} | dynamic-slice | bytes 12 | tf_op jit(solution)/shard_map/dynamic_slice | solution.py:57
  9.6 1.5 %fusion.110 = (s32[1]{0:T(128)}, s32[1]{0:T(128)}, s32[1]{0:T(128)}, s32[1]{0:T(128)}, s32[1]{0:T(128)}) fusion(s32[5]{0:T(128)} %param.13), kind=kLoop, calls=%fused_computation.173 | loop fusion | bytes 40 | tf_op jit(solution)/shard_map/slice | solution.py:68
  11.1 1.5 %fusion.109 = (s32[1]{0:T(128)}, s32[1]{0:T(128)}, s32[1]{0:T(128)}, s32[1]{0:T(128)}, s32[1]{0:T(128)}) fusion(s32[5]{0:T(128)} %param.14), kind=kLoop, calls=%fused_computation.172 | loop fusion | bytes 40 | tf_op jit(solution)/shard_map/slice | solution.py:68
  12.6 31.8 %all_gather.3 = bf16[5,8,8,1,2,128]{5,4,3,2,1,0:T(2,128)(2,1)S(1)} all-gather(bf16[5,1,8,1,2,128]{5,4,3,2,1,0:T(2,128)(2,1)} %param.10), channel_id=1, replica_groups=mesh['pool'=8,'tp'=4] {'pool'}, dimensions={1}, use_global_device_ids=true | all-gather | bytes 184320 | tf_op jit(solution)/shard_map/all_gather | solution.py:64
  44.5 1.3 %fusion.89 = pred[8]{0:T(512)(128)(4,1)S(1)} fusion(s32[]{:T(128)} %bitcast.1, s32[]{:T(128)} %bitcast), kind=kLoop, calls=%fused_computation.153 | loop fusion | flops 104 | bytes 16 | tf_op jit(solution)/shard_map/lt | solution.py:68
  45.8 1.3 %compare_and_fusion.2 = pred[8]{0:T(512)(128)(4,1)S(1)} fusion(pred[]{:T(512)} %bitcast.29, s32[]{:T(128)} %bitcast.31, s32[]{:T(128)} %bitcast.30), kind=kLoop, calls=%fused_computation.147 | loop fusion | flops 112 | bytes 17 | tf_op jit(solution)/shard_map/and | solution.py:74
  47.1 1.3 %compare_and_fusion.3 = pred[8]{0:T(512)(128)(4,1)S(1)} fusion(pred[]{:T(512)} %bitcast.15, s32[]{:T(128)} %bitcast.17, s32[]{:T(128)} %bitcast.16), kind=kLoop, calls=%fused_computation.149 | loop fusion | flops 112 | bytes 17 | tf_op jit(solution)/shard_map/and | solution.py:74
  48.4 1.2 %compare_and_fusion = pred[8]{0:T(512)(128)(4,1)S(1)} fusion(pred[]{:T(512)} %bitcast.55, s32[]{:T(128)} %bitcast.57, s32[]{:T(128)} %bitcast.56), kind=kLoop, calls=%fused_computation.143 | loop fusion | flops 112 | bytes 17 | tf_op jit(solution)/shard_map/and | solution.py:74
  50.2 2.2 %copy.22 = bf16[32,64,128]{2,0,1:T(8,128)(2,1)} copy(bf16[32,64,128]{2,1,0:T(8,128)(2,1)} %param.8) | data formatting | bytes 1048576 | tf_op args[0]
  52.4 3.5 %all-to-all-start = ((bf16[32,64,128]{2,0,1:T(8,128)(2,1)}), bf16[32,64,128]{2,0,1:T(8,128)(2,1)S(1)}, u32[]{:S(2)}, u32[]{:S(2)}) async-start(bf16[32,64,128]{2,0,1:T(8,128)(2,1)} %copy.22), calls=%async_computation | async-start | bytes 1048576 | tf_op jit(solution)/shard_map/all_to_all | solution.py:42
  55.9 1.2 %compare_and_fusion.1 = pred[8]{0:T(512)(128)(4,1)S(1)} fusion(pred[]{:T(512)} %bitcast.42, s32[]{:T(128)} %bitcast.44, s32[]{:T(128)} %bitcast.43), kind=kLoop, calls=%fused_computation.145 | loop fusion | flops 112 | bytes 17 | tf_op jit(solution)/shard_map/and | solution.py:74
  58.2 6.5 %all-to-all-done = bf16[32,64,128]{2,0,1:T(8,128)(2,1)S(1)} async-done(((bf16[32,64,128]{2,0,1:T(8,128)(2,1)}), bf16[32,64,128]{2,0,1:T(8,128)(2,1)S(1)}, u32[]{:S(2)}, u32[]{:S(2)}) %all-to-all-start) | async-done | bytes 524320 | tf_op jit(solution)/shard_map/all_to_all | solution.py:42
  66.7 0.5 bitcast_reduce_fusion
  67.3 0.4 convolution_bitcast_fusion.2
  67.8 0.4 convolution_bitcast_fusion.3
  68.4 0.4 convolution_bitcast_fusion.4
  69.3 0.7 fusion.2
  70.0 0.9 %convolution_bitcast_fusion.1 = f32[1,128,1,16,128]{4,1,3,0,2:T(8,128)S(1)} fusion(f32[256,128,16]{1,0,2:T(8,128)S(1)} %get-tuple-element.40, f32[128,16]{0,1:T(8,128)S(1)} %get-tuple-element.13, pred[256]{0:T(512)(128)(4,1)S(1)} %iota_compare_fusion.1, bf16[1,256,1,1,128]{4,3,2,1,0:T(2,128)(2,1)S(1)} %get-tuple-element.23), kind=kOutput, calls=%fused_computation.8 | convolution fusion | flops 136839168 | bytes 3219712 | tf_op jit(solution)/shard_map/btkgs,bskd->btkgd/dot_general | solution.py:22
  71.3 2.2 %fusion.19 = f32[1,128,1,16,128]{4,1,3,0,2:T(8,128)S(1)} fusion(f32[1,128,1,16,128]{4,1,3,0,2:T(8,128)S(1)} %convolution_bitcast_fusion.1, f32[1,128,1,128,16]{1,3,4,2,0:T(8,128)S(1)} %convolution_bitcast_fusion.2, f32[1,128,1,128,16]{1,3,4,2,0:T(8,128)S(1)} %convolution_bitcast_fusion.3, f32[1,128,1,128,16]{1,3,4,2,0:T(8,128)S(1)} %convolution_bitcast_fusion.4, ...), kind=kOutput, calls=%fused_computation.30 | convolution fusion | flops 37093376 | bytes 6898176 | tf_op jit(solution)/shard_map/btkgs,skd->btkgd/dot_general | solution.py:22
  73.5 0.5 fusion.22
  74.4 11.2 %all_to_all.48 = bf16[128,16,128]{2,1,0:T(8,128)(2,1)S(1)} all-to-all(bf16[128,16,128]{2,1,0:T(8,128)(2,1)S(1)} %copy.34), channel_id=1, replica_groups=mesh['pool'=8,'tp'=4] {'tp'}, dimensions={0} | all-to-all | bytes 1048576 | tf_op jit(solution)/shard_map/all_to_all | solution.py:88
  85.6 0.9 copy.35
  (38 shorter events, 4.7 us)
Async XLA Ops:
  0.0 57.9 %copy-start = (bf16[1,256,1,2,128]{4,3,2,1,0:T(2,128)(2,1)S(1)}, bf16[1,256,1,2,128]{4,3,2,1,0:T(2,128)(2,1)}, u32[]{:S(2)}) copy-start(bf16[1,256,1,2,128]{4,3,2,1,0:T(2,128)(2,1)} %param.11) | copy-start | bytes 393220
  1.5 50.9 %all-to-all-start.1 = ((bf16[32,4,2,128]{3,2,0,1:T(2,128)(2,1)}), bf16[32,4,2,128]{3,2,0,1:T(2,128)(2,1)S(1)}, u32[]{:S(2)}, u32[]{:S(2)}) async-start(bf16[32,4,2,128]{3,2,0,1:T(2,128)(2,1)} %copy.31), calls=%async_computation.1 | async-start | bytes 131072 | tf_op jit(solution)/shard_map/all_to_all | solution.py:43
  52.4 12.3 %all-to-all-start = ((bf16[32,64,128]{2,0,1:T(8,128)(2,1)}), bf16[32,64,128]{2,0,1:T(8,128)(2,1)S(1)}, u32[]{:S(2)}, u32[]{:S(2)}) async-start(bf16[32,64,128]{2,0,1:T(8,128)(2,1)} %copy.22), calls=%async_computation | async-start | bytes 1048576 | tf_op jit(solution)/shard_map/all_to_all | solution.py:42
where the time goes:
time: 87 us; the launch traced here: 86.5 us
  blocking collectives  43.1 us (50%)
  local copies, waits for them, and re-layouts  10.4 us (12%)
  other arithmetic  7.71 us (9%)
  starting transfers between devices  7.68 us (9%)
  matrix products  7.58 us (9%)
  waiting for transfers between devices  6.53 us (8%)
  between operations  3.53 us (4%)
    all_gather x1, blocking collectives, per_device(): pieces = lax.all_gather(pooled_page_cache, 'pool', axis=1, tiled=True)  31.8 us
    all_to_all x1, blocking collectives, per_device(): return lax.all_to_all(result, 'tp', split_axis=0, concat_axis=1, tiled=True)  11.2 us
    all_to_all x1, waiting for transfers between devices, per_device(): lax.all_to_all(queries, 'tp', split_axis=1, concat_axis=0, tiled=True)  6.53 us
    dot_general x7, matrix products, attend(): jnp.einsum(value_form, weights.astype(jnp.bfloat16), key_pairs[..., 1, :]...  5.26 us
    and x4, other arithmetic, per_device(): key_mask = relevant[:, None, None] & usable[None, None, :]  4.91 us
    all_to_all x1, starting transfers between devices, per_device(): lax.all_to_all(fresh_key_values, 'tp', split_axis=1, concat_axis=0, tiled...  4.21 us
    unnamed x4, local copies, waits for them, and re-layouts  3.72 us
    all_to_all x1, starting transfers between devices, per_device(): lax.all_to_all(queries, 'tp', split_axis=1, concat_axis=0, tiled=True)  3.47 us
  transfers between devices with their start and end apart: 2, of which 1 were waited for; matrix products, arithmetic and copies ran while one was open for 16% of the time, Pallas kernels for 0%

commit v1 on v0

v1 whole, which is shorter than its diff:
```python
import functools

import jax
import jax.numpy as jnp
from jax import lax
from jax.experimental import pallas as pl
from jax.experimental.pallas import tpu as pltpu
from jax.sharding import PartitionSpec as P

LOG2_E = 1.4426950408889634
MASKED = -1e30
LONG = pl.CostEstimate(flops=5 * 10**10, bytes_accessed=10**6, transcendentals=0)
SHORT = pl.CostEstimate(flops=10**6, bytes_accessed=10**5, transcendentals=0)


def pick(shape, source_row):
    row = lax.broadcasted_iota(jnp.int32, shape, 0)
    column = lax.broadcasted_iota(jnp.int32, shape, 1)
    return jnp.where(column == source_row(row), 1.0, 0.0).astype(jnp.bfloat16)


def dot(a, b):
    return lax.dot_general(a, b, (((1,), (0,)), ((), ())), preferred_element_type=jnp.float32)


def select_kernel(
    page, parent_hbm, pages_hbm, owner_hbm, pool_hbm, leaf_hbm, fresh_hbm,
    out_hbm, local_ref, bias_ref,
    parent_ref, pages_ref, owner_ref, pool_ref, rows_ref, block_ref, sems,
):
    leaf_rows, fresh_rows = leaf_hbm.shape[0], fresh_hbm.shape[0]
    pairs = [
        (pool_hbm, pool_ref),
        (parent_hbm, parent_ref),
        (pages_hbm, pages_ref),
        (owner_hbm, owner_ref),
        (leaf_hbm, local_ref.at[pl.ds(0, leaf_rows)]),
        (fresh_hbm, local_ref.at[pl.ds(leaf_rows, fresh_rows)]),
    ]
    fetches = [pltpu.make_async_copy(*pair, sems.at[i]) for i, pair in enumerate(pairs)]
    for fetch in fetches:
        fetch.start()
    node_count = pool_ref.shape[0] // (2 * page)
    copies, requests = out_hbm.shape[:2]
    fetches[0].wait()
    rows_ref[...] = pool_ref[...].astype(jnp.float32)
    root = [rows_ref[pl.ds(kind, page, stride=2)] for kind in range(2)]
    fetches[1].wait()

    def one(request, carry):
        mid = parent_ref[node_count + request] * (2 * page)
        for kind in range(2):
            chosen = rows_ref[pl.ds(mid + kind, page, stride=2)]
            block_ref[kind, request] = jnp.concatenate([root[kind], chosen], 0).astype(jnp.bfloat16)
        return carry

    lax.fori_loop(0, requests, one, 0, unroll=requests <= 8)
    sends = [
        pltpu.make_async_copy(block_ref.at[copy % 2], out_hbm.at[copy], sems.at[len(pairs) + copy])
        for copy in range(copies)
    ]
    for send in sends:
        send.start()

    fetches[2].wait()
    fetches[3].wait()
    mid = parent_ref[node_count + lax.axis_index("pool")]
    key = lax.broadcasted_iota(jnp.int32, bias_ref.shape, 1)
    stripe, is_mid = key // (2 * page), (key % (2 * page)) >= page
    offset = stripe - jnp.where(is_mid, owner_ref[mid], owner_ref[0])
    offset = jnp.where(offset < 0, offset + requests, offset)
    used = offset < jnp.where(is_mid, pages_ref[mid], pages_ref[0])
    bias_ref[...] = jnp.where(used, 0.0, MASKED)
    for copy in fetches[4:] + sends:
        copy.wait()


def hand_over_kernel(*refs):
    pass


def hand_over(cost, *arrays):
    anywhere = pl.BlockSpec(memory_space=pl.ANY)
    return pl.pallas_call(
        hand_over_kernel,
        out_shape=[jax.ShapeDtypeStruct(array.shape, array.dtype) for array in arrays],
        in_specs=[anywhere] * len(arrays),
        out_specs=[anywhere] * len(arrays),
        input_output_aliases={i: i for i in range(len(arrays))},
        compiler_params=pltpu.CompilerParams(vmem_limit_bytes=2**20),
        cost_estimate=cost,
    )(*arrays)


def scores_of(rows, keys):
    scores = lax.dot_general(rows, keys, (((1,), (1,)), ((), ())), preferred_element_type=jnp.float32)
    return scores * (LOG2_E * 128 ** (-0.5))


def weigh(weights, values):
    sums = dot(weights.astype(jnp.bfloat16), jnp.concatenate([values, jnp.ones_like(values)], 1))
    return sums[:, : values.shape[1]], sums[:, values.shape[1] :]


def own_kernel(leaf_len_ref, q_ref, *rest, page):
    local_refs = rest[:4]
    result_ref, level_ref, bias_ref, kf_ref, vf_ref = rest[4:]
    tokens, q_heads, dim = q_ref.shape
    group = q_heads // 4
    leaf_slots = bias_ref.shape[0] - 4 * tokens
    rank = lax.axis_index("tp")

    key = lax.broadcasted_iota(jnp.int32, (leaf_slots, dim), 0)
    bias_ref[0:leaf_slots] = jnp.where(key < leaf_len_ref[0] * page, 0.0, MASKED).astype(jnp.bfloat16)
    key = lax.broadcasted_iota(jnp.int32, (tokens, dim), 0)
    row = lax.broadcasted_iota(jnp.int32, (tokens, dim), 1)
    for step in range(4):
        seen = key <= row if step == 0 else jnp.full((tokens, dim), rank ^ step, jnp.int32) < rank
        bias_ref[leaf_slots + step * tokens : leaf_slots + (step + 1) * tokens] = jnp.where(
            seen, 0.0, MASKED
        ).astype(jnp.bfloat16)

    fresh_rows = local_refs[0].shape[0] - 2 * leaf_slots

    def fresh_source(out_row):
        head, kind, token = out_row // (2 * tokens), (out_row // tokens) % 2, out_row % tokens
        return token * 8 + head * 2 + kind

    fresh_pick = pick((fresh_rows, fresh_rows), fresh_source)
    for step in range(4):
        parts = dot(fresh_pick, local_refs[step][2 * leaf_slots :]).astype(jnp.bfloat16)
        for head in range(4):
            base = head * 2 * tokens
            kf_ref[head, step * tokens : (step + 1) * tokens] = parts[base : base + tokens]
            vf_ref[head, step * tokens : (step + 1) * tokens] = parts[base + tokens : base + 2 * tokens]

    chunk = 256
    half = chunk // 2
    leaf_pick = pick((chunk, chunk), lambda out_row: (out_row % half) * 2 + out_row // half)
    bias = bias_ref[...]
    token = lax.broadcasted_iota(jnp.int32, (tokens * group, dim), 0) // group
    column = lax.broadcasted_iota(jnp.int32, (tokens * group, dim), 1)
    own_row = jnp.where(token == column, 1.0, 0.0).astype(jnp.bfloat16)
    for step in range(4):
        head = rank ^ step
        leaf_k, leaf_v = [], []
        for piece in range(leaf_slots // half):
            parts = dot(leaf_pick, local_refs[step][piece * chunk : (piece + 1) * chunk]).astype(jnp.bfloat16)
            leaf_k.append(parts[:half])
            leaf_v.append(parts[half:])
        keys = jnp.concatenate([jnp.concatenate(leaf_k + [kf_ref[head]], 0), bias], 1)
        values = jnp.concatenate(leaf_v + [vf_ref[head]], 0)
        rows = q_ref[:, pl.ds(pl.multiple_of(head * group, group), group), :].reshape(tokens * group, dim)
        scores = scores_of(jnp.concatenate([rows, own_row], 1), keys)
        top = jnp.max(scores, axis=1, keepdims=True)
        sums, totals = weigh(jnp.exp2(scores - top), values)
        result_ref[step] = sums / totals
        level_ref[step] = jnp.log2(totals) + top


def shared_kernel(q_ref, bias_ref, other_ref, level_ref, mine_ref, theirs_ref, out_hbm, stage_ref, sems):
    tokens, q_heads, dim = q_ref.shape
    group = q_heads // 4
    shared_keys = bias_ref.shape[1]
    rank = lax.axis_index("tp")
    has_keys = rank % 2 == 0
    bias = bias_ref[0:1]
    places = [pl.ds(pl.multiple_of((rank ^ step) * group, group), group) for step in range(4)]

    def above_level(step):
        head = rank ^ step
        keys = jnp.where(has_keys, mine_ref[head], theirs_ref[head]).reshape(shared_keys, dim)
        scores = scores_of(q_ref[:, places[step], :].reshape(tokens * group, dim), keys)
        return scores + bias - jnp.concatenate([level_ref[step]] * (shared_keys // dim), 1)

    def weighted(step, weights):
        head = rank ^ step
        values = jnp.where(has_keys, theirs_ref[head], mine_ref[head]).reshape(shared_keys, dim)
        return weigh(weights, values)

    def write(step, result):
        stage_ref[step] = result.astype(jnp.bfloat16).reshape(tokens, group, dim)
        copy = pltpu.make_async_copy(stage_ref.at[step], out_hbm.at[:, places[step]], sems.at[step])
        copy.start()
        return copy

    scores = [above_level(step) for step in range(4)]
    highest = functools.reduce(jnp.maximum, scores)
    writes = []
    for step in range(4):
        sums, totals = weighted(step, jnp.exp2(scores[step]))
        writes.append(write(step, (sums + other_ref[step]) / (totals + 1.0)))
    too_high = jnp.max(highest) > 100.0
    for copy in writes:
        copy.wait()

    @pl.when(too_high)
    def _():
        for step in range(4):
            scores = above_level(step)
            top = jnp.maximum(jnp.max(scores, axis=1, keepdims=True), 0.0)
            sums, totals = weighted(step, jnp.exp2(scores - top))
            other = jnp.exp2(-top)
            write(step, (sums + other_ref[step] * other) / (totals + other)).wait()


def per_device(queries, fresh, pool, leaf, parent, node_pages, node_owner, leaf_len):
    tp = lax.axis_size("tp")
    stripes = lax.axis_size("pool")
    shared_count, _, page, _, _, dim = pool.shape
    tokens, q_heads, _ = queries.shape
    vmem = pl.BlockSpec(memory_space=pltpu.VMEM)
    swap = lambda array, bit: lax.ppermute(array, "tp", [(i, i ^ bit) for i in range(tp)])
    hbm = pl.BlockSpec(memory_space=pltpu.HBM)

    pool_rows = pool.reshape(-1, dim)
    leaf_rows = leaf.reshape(-1, dim)
    fresh_rows = fresh.reshape(-1, dim)
    operands = (parent, node_pages, node_owner, pool_rows, leaf_rows, fresh_rows)
    sent, local_0, bias = pl.pallas_call(
        functools.partial(select_kernel, page),
        out_shape=[
            jax.ShapeDtypeStruct((tp, stripes, 2 * page, dim), jnp.bfloat16),
            jax.ShapeDtypeStruct((leaf_rows.shape[0] + fresh_rows.shape[0], dim), jnp.bfloat16),
            jax.ShapeDtypeStruct((8, stripes * 2 * page), jnp.float32),
        ],
        in_specs=[hbm] * 6,
        out_specs=[hbm, vmem, vmem],
        scratch_shapes=[
            pltpu.SMEM(parent.shape, jnp.int32),
            pltpu.SMEM(node_pages.shape, jnp.int32),
            pltpu.SMEM(node_owner.shape, jnp.int32),
            pltpu.VMEM(pool_rows.shape, jnp.bfloat16),
            pltpu.VMEM(pool_rows.shape, jnp.float32),
            pltpu.VMEM((2, stripes, 2 * page, dim), jnp.bfloat16),
            pltpu.SemaphoreType.DMA((6 + tp,)),
        ],
        compiler_params=pltpu.CompilerParams(vmem_limit_bytes=16 * 2**20),
        cost_estimate=LONG,
    )(*[pltpu.with_memory_space_constraint(operand, pltpu.HBM) for operand in operands])
    local_2 = swap(local_0, 2)
    mine = lax.all_to_all(
        sent.reshape(tp * stripes, 2 * page, dim), ("tp", "pool"), split_axis=0, concat_axis=0, tiled=True
    ).reshape(tp, stripes, 2 * page, dim)
    local_0, local_2 = hand_over(LONG, local_0, local_2)
    local_1, local_3 = swap(local_0, 1), swap(local_2, 1)

    rows = tokens * q_heads // tp
    other, level = pl.pallas_call(
        functools.partial(own_kernel, page=page),
        out_shape=[jax.ShapeDtypeStruct((tp, rows, dim), jnp.float32)] * 2,
        in_specs=[pl.BlockSpec(memory_space=pltpu.SMEM)] + [vmem] * 5,
        out_specs=[vmem] * 2,
        scratch_shapes=[pltpu.VMEM((leaf.shape[1] + tp * tokens, dim), jnp.bfloat16)]
        + [pltpu.VMEM((tp, tp * tokens, dim), jnp.bfloat16)] * 2,
        compiler_params=pltpu.CompilerParams(vmem_limit_bytes=24 * 2**20),
        cost_estimate=SHORT,
    )(leaf_len, queries, local_0, local_1, local_2, local_3)
    mine, level = hand_over(SHORT, mine, level)
    theirs = swap(mine, 1)
    return pl.pallas_call(
        shared_kernel,
        out_shape=jax.ShapeDtypeStruct(queries.shape, jnp.bfloat16),
        in_specs=[vmem] * 6,
        out_specs=hbm,
        scratch_shapes=[
            pltpu.VMEM((tp, tokens, q_heads // tp, dim), jnp.bfloat16),
            pltpu.SemaphoreType.DMA((tp,)),
        ],
        compiler_params=pltpu.CompilerParams(vmem_limit_bytes=(24 if stripes <= 8 else 48) * 2**20),
    )(queries, bias, other, level, mine, theirs)


def solution(mesh):
    return jax.shard_map(
        per_device,
        mesh=mesh,
        in_specs=(
            P(("pool", "tp"), None, None),
            P(("pool", "tp"), None, None, None),
            P(None, "pool", None, "tp", None, None),
            P("pool", None, "tp", None, None),
            P(),
            P(),
            P(),
            P("pool"),
        ),
        out_specs=P(("pool", "tp"), None, None),
        check_vma=False,
    )
```

time: 87 us -> 20.2 us (0.23)
  blocking collectives: 43.1 us -> 0 us
  local copies, waits for them, and re-layouts: 10.4 us -> 0.01 us
  other arithmetic: 7.71 us -> 0 us
  matrix products: 7.58 us -> 0 us
  Pallas kernels: 0 us -> 5.43 us
  between operations: 3.53 us -> 0.7 us
  waiting for transfers between devices: 6.53 us -> 5.23 us
  starting transfers between devices: 7.68 us -> 8.61 us
    all_gather x1 -> x0, blocking collectives: 31.8 us -> none  [per_device(): pieces = lax.all_gather(pooled_page_cache, 'pool', axis=1, tiled=True)]
    all_to_all x1 -> x0, blocking collectives: 11.2 us -> none  [per_device(): return lax.all_to_all(result, 'tp', split_axis=0, concat_axis=1, tiled=True)]
    dot_general x14 -> x0, matrix products: 7.58 us -> none  [the longest x7 5.26 us: attend(): jnp.einsum(value_form, weights.astype(jnp.bfloat16), key_pairs[..., 1, :]...]
    pallas_call x0 -> x5, Pallas kernels: none -> 5.43 us  [the longest x1 2.48 us: per_device(): pl.pallas_call(functools.partial(own_kernel, page=page), out_shape=[jax.S...]
    and x4 -> x0, other arithmetic: 4.91 us -> none  [per_device(): key_mask = relevant[:, None, None] & usable[None, None, :]]
    unnamed x4 -> x2, local copies, waits for them, and re-layouts: 3.72 us -> 0.01 us
    ppermute x0 -> x4, starting transfers between devices: none -> 3.69 us  [per_device(): lax.ppermute(array, 'tp', [(i, i ^ bit) for i in range(tp)])]
    slice x5 -> x0, local copies, waits for them, and re-layouts: 3.3 us -> none  [the longest x1 1.5 us: per_device(): node_pages[node_id]]
  transfers between devices with their start and end apart: 2 -> 5, of which waited for: 1 -> 4; matrix products, arithmetic and copies ran while one was open for 16% -> 0% of each run, Pallas kernels for 0% -> 12%
where the time goes in v1:
time: 20.2 us; the launch traced here: 20 us
  starting transfers between devices  8.61 us (43%)
  Pallas kernels  5.43 us (27%)
  waiting for transfers between devices  5.23 us (26%)
  between operations  0.7 us (3%)
    all_to_all x1, starting transfers between devices, per_device(): lax.all_to_all(sent.reshape(tp * stripes, 2 * page, dim), ('tp', 'pool'),...  4.92 us
    ppermute x4, starting transfers between devices, per_device(): lax.ppermute(array, 'tp', [(i, i ^ bit) for i in range(tp)])  3.69 us
    all_to_all x1, waiting for transfers between devices, per_device(): lax.all_to_all(sent.reshape(tp * stripes, 2 * page, dim), ('tp', 'pool'),...  3.43 us
    pallas_call x1, Pallas kernels, per_device(): pl.pallas_call(functools.partial(own_kernel, page=page), out_shape=[jax.S...  2.48 us
    ppermute x4, waiting for transfers between devices, per_device(): lax.ppermute(array, 'tp', [(i, i ^ bit) for i in range(tp)])  1.8 us
    pallas_call x1, Pallas kernels, per_device(): pl.pallas_call(functools.partial(select_kernel, page), out_shape=[jax.Sha...  1.54 us
    pallas_call x1, Pallas kernels, per_device(): pl.pallas_call(shared_kernel, out_shape=jax.ShapeDtypeStruct(queries.shap...  1.41 us
  transfers between devices with their start and end apart: 5, of which 4 were waited for; matrix products, arithmetic and copies ran while one was open for 0% of the time, Pallas kernels for 12%

profile of v1, /device:TPU:0, one launch (start us, length us, event | category | flops | bytes accessed | tf_op | source)
XLA Modules:
  0.0 20.0 jit_solution(3909224128098317369)
XLA Ops:
  0.0 1.5 %shard_map.82 = (bf16[4,8,16,128]{3,2,1,0:T(8,128)(2,1)}, bf16[768,128]{1,0:T(8,128)(2,1)S(1)}, f32[8,128]{1,0:T(8,128)S(1)}) custom-call(s32[13]{0:T(128)} %parent_hbm.1, s32[5]{0:T(128)} %pages_hbm.1, s32[5]{0:T(128)} %owner_hbm.1, bf16[80,128]{1,0:T(8,128)(2,1)} %bitcast.8, bf16[512,128]{1,0:T(8,128)(2,1)} %bitcast.6, bf16[256,128]{1,0:T(8,128)(2,1)} %bitcast.7), custom_call_target="tpu_custom_call" | custom-call | flops 49999998976 | bytes 1000000 | tf_op jit(solution)/shard_map/pallas_call | solution.py:220
  1.5 3.0 %collective-permute-start = (bf16[768,128]{1,0:T(8,128)(2,1)S(1)}, bf16[768,128]{1,0:T(8,128)(2,1)S(1)}, u32[]{:S(2)}, u32[]{:S(2)}) collective-permute-start(bf16[768,128]{1,0:T(8,128)(2,1)S(1)} %get-tuple-element.15.refs_0_), channel_id=1, source_target_pairs={{0,2},{1,3},{2,0},{3,1},{4,6},{5,7},{6,4},{7,5},{8,10},{9,11},{10,... | collective-permute-start | bytes 589832 | tf_op jit(solution)/shard_map/ppermute | solution.py:213
  4.6 4.9 %all-to-all-start = ((bf16[32,16,128]{2,1,0:T(8,128)(2,1)}), bf16[32,16,128]{2,1,0:T(8,128)(2,1)S(1)}, u32[]{:S(2)}, u32[]{:S(2)}) async-start(bf16[32,16,128]{2,1,0:T(8,128)(2,1)} %bitcast.3), calls=%async_computation | async-start | bytes 262144 | tf_op jit(solution)/shard_map/all_to_all | solution.py:242
  9.5 0.0 copy-start
  9.5 0.0 collective-permute-done.refs_1_
  9.5 0.3 %collective-permute-start.1 = (bf16[768,128]{1,0:T(8,128)(2,1)S(1)}, bf16[768,128]{1,0:T(8,128)(2,1)S(1)}, u32[]{:S(2)}, u32[]{:S(2)}) collective-permute-start(bf16[768,128]{1,0:T(8,128)(2,1)S(1)} %get-tuple-element.16.rest_0_), channel_id=1, source_target_pairs={{0,1},{1,0},{2,3},{3,2},{4,5},{5,4},{6,7},{7,6},{8,9},{9,8},{10,11... | collective-permute-start | bytes 589832 | tf_op jit(solution)/shard_map/ppermute | solution.py:213
  9.8 0.3 %collective-permute-start.2 = (bf16[768,128]{1,0:T(8,128)(2,1)S(1)}, bf16[768,128]{1,0:T(8,128)(2,1)S(1)}, u32[]{:S(2)}, u32[]{:S(2)}) collective-permute-start(bf16[768,128]{1,0:T(8,128)(2,1)S(1)} %get-tuple-element.17.rest_2_), channel_id=1, source_target_pairs={{0,1},{1,0},{2,3},{3,2},{4,5},{5,4},{6,7},{7,6},{8,9},{9,8},{10,11... | collective-permute-start | bytes 589832 | tf_op jit(solution)/shard_map/ppermute | solution.py:213
  10.7 0.3 %collective-permute-done.1.rest_1_ = bf16[768,128]{1,0:T(8,128)(2,1)S(1)} collective-permute-done((bf16[768,128]{1,0:T(8,128)(2,1)S(1)}, bf16[768,128]{1,0:T(8,128)(2,1)S(1)}, u32[]{:S(2)}, u32[]{:S(2)}) %collective-permute-start.1) | collective-permute-done | bytes 196640 | tf_op jit(solution)/shard_map/ppermute | solution.py:213
  11.0 0.3 %collective-permute-done.2.rest_3_ = bf16[768,128]{1,0:T(8,128)(2,1)S(1)} collective-permute-done((bf16[768,128]{1,0:T(8,128)(2,1)S(1)}, bf16[768,128]{1,0:T(8,128)(2,1)S(1)}, u32[]{:S(2)}, u32[]{:S(2)}) %collective-permute-start.2) | collective-permute-done | bytes 196640 | tf_op jit(solution)/shard_map/ppermute | solution.py:213
  11.3 0.0 copy-done
  11.3 2.5 %shard_map.84 = (f32[4,512,128]{2,1,0:T(8,128)S(1)}, f32[4,512,128]{2,1,0:T(8,128)S(1)}) custom-call(s32[1]{0:T(128)S(6)} %copy.17.leaf_len_ref, bf16[32,64,128]{2,1,0:T(8,128)(2,1)S(1)} %copy-done, bf16[768,128]{1,0:T(8,128)(2,1)S(1)} %get-tuple-element.16.rest_0_, bf16[768,128]{1,0:T(8,128)(2,1)S(1)} %collective-permute-done.1.rest_1_, ...), custom_call_target="tpu_custom_call" | custom-call | flops 1000000 | bytes 100000 | tf_op jit(solution)/shard_map/pallas_call | solution.py:249
  13.8 3.4 %all-to-all-done = bf16[32,16,128]{2,1,0:T(8,128)(2,1)S(1)} async-done(((bf16[32,16,128]{2,1,0:T(8,128)(2,1)}), bf16[32,16,128]{2,1,0:T(8,128)(2,1)S(1)}, u32[]{:S(2)}, u32[]{:S(2)}) %all-to-all-start) | async-done | bytes 131104 | tf_op jit(solution)/shard_map/all_to_all | solution.py:242
  17.2 0.1 collective-permute-start.3
  17.3 1.2 %collective-permute-done.3.theirs_ref = bf16[4,8,16,128]{3,2,1,0:T(8,128)(2,1)S(1)} collective-permute-done((bf16[4,8,16,128]{3,2,1,0:T(8,128)(2,1)S(1)}, bf16[4,8,16,128]{3,2,1,0:T(8,128)(2,1)S(1)}, u32[]{:S(2)}, u32[]{:S(2)}) %collective-permute-start.3) | collective-permute-done | bytes 131104 | tf_op jit(solution)/shard_map/ppermute | solution.py:213
  18.6 1.4 %shard_map.86 = bf16[32,64,128]{2,1,0:T(8,128)(2,1)} custom-call(bf16[32,64,128]{2,1,0:T(8,128)(2,1)S(1)} %copy-done, f32[8,128]{1,0:T(8,128)S(1)} %get-tuple-element.14.bias_ref, f32[4,512,128]{2,1,0:T(8,128)S(1)} %get-tuple-element.18.other_ref, f32[4,512,128]{2,1,0:T(8,128)S(1)} %get-tuple-element.21.level_ref, ...), custom_call_target="tpu_custom_call" | custom-call | tf_op jit(solution)/shard_map/pallas_call | solution.py:261
  (2 shorter events, 0.0 us)
Async XLA Ops:
  1.5 7.9 %collective-permute-start = (bf16[768,128]{1,0:T(8,128)(2,1)S(1)}, bf16[768,128]{1,0:T(8,128)(2,1)S(1)}, u32[]{:S(2)}, u32[]{:S(2)}) collective-permute-start(bf16[768,128]{1,0:T(8,128)(2,1)S(1)} %get-tuple-element.15.refs_0_), channel_id=1, source_target_pairs={{0,2},{1,3},{2,0},{3,1},{4,6},{5,7},{6,4},{7,5},{8,10},{9,11},{10,... | collective-permute-start | bytes 589832 | tf_op jit(solution)/shard_map/ppermute | solution.py:213
  4.6 12.7 %all-to-all-start = ((bf16[32,16,128]{2,1,0:T(8,128)(2,1)}), bf16[32,16,128]{2,1,0:T(8,128)(2,1)S(1)}, u32[]{:S(2)}, u32[]{:S(2)}) async-start(bf16[32,16,128]{2,1,0:T(8,128)(2,1)} %bitcast.3), calls=%async_computation | async-start | bytes 262144 | tf_op jit(solution)/shard_map/all_to_all | solution.py:242
  9.5 1.8 %copy-start = (bf16[32,64,128]{2,1,0:T(8,128)(2,1)S(1)}, bf16[32,64,128]{2,1,0:T(8,128)(2,1)}, u32[]{:S(2)}) copy-start(bf16[32,64,128]{2,1,0:T(8,128)(2,1)} %q_ref.3) | copy-start | bytes 1572868
  9.5 1.5 %collective-permute-start.1 = (bf16[768,128]{1,0:T(8,128)(2,1)S(1)}, bf16[768,128]{1,0:T(8,128)(2,1)S(1)}, u32[]{:S(2)}, u32[]{:S(2)}) collective-permute-start(bf16[768,128]{1,0:T(8,128)(2,1)S(1)} %get-tuple-element.16.rest_0_), channel_id=1, source_target_pairs={{0,1},{1,0},{2,3},{3,2},{4,5},{5,4},{6,7},{7,6},{8,9},{9,8},{10,11... | collective-permute-start | bytes 589832 | tf_op jit(solution)/shard_map/ppermute | solution.py:213
  9.8 1.5 %collective-permute-start.2 = (bf16[768,128]{1,0:T(8,128)(2,1)S(1)}, bf16[768,128]{1,0:T(8,128)(2,1)S(1)}, u32[]{:S(2)}, u32[]{:S(2)}) collective-permute-start(bf16[768,128]{1,0:T(8,128)(2,1)S(1)} %get-tuple-element.17.rest_2_), channel_id=1, source_target_pairs={{0,1},{1,0},{2,3},{3,2},{4,5},{5,4},{6,7},{7,6},{8,9},{9,8},{10,11... | collective-permute-start | bytes 589832 | tf_op jit(solution)/shard_map/ppermute | solution.py:213
  17.2 1.3 %collective-permute-start.3 = (bf16[4,8,16,128]{3,2,1,0:T(8,128)(2,1)S(1)}, bf16[4,8,16,128]{3,2,1,0:T(8,128)(2,1)S(1)}, u32[]{:S(2)}, u32[]{:S(2)}) collective-permute-start(bf16[4,8,16,128]{3,2,1,0:T(8,128)(2,1)S(1)} %get-tuple-element.22.mine_ref), channel_id=1, source_target_pairs={{0,1},{1,0},{2,3},{3,2},{4,5},{5,4},{6,7},{7,6},{8,9},{9,8},{10,11... | collective-permute-start | bytes 393224 | tf_op jit(solution)/shard_map/ppermute | solution.py:213

commit v2 on v1

--- a/solution.py
+++ b/solution.py
@@ -25,8 +25,8 @@
 
 def select_kernel(
     page, parent_hbm, pages_hbm, owner_hbm, pool_hbm, leaf_hbm, fresh_hbm,
-    out_hbm, local_ref, bias_ref,
-    parent_ref, pages_ref, owner_ref, pool_ref, rows_ref, block_ref, sems,
+    out_ref, local_ref, bias_ref,
+    parent_ref, pages_ref, owner_ref, pool_ref, rows_ref, sems,
 ):
     leaf_rows, fresh_rows = leaf_hbm.shape[0], fresh_hbm.shape[0]
     pairs = [
@@ -41,7 +41,7 @@
     for fetch in fetches:
         fetch.start()
     node_count = pool_ref.shape[0] // (2 * page)
-    copies, requests = out_hbm.shape[:2]
+    copies, requests = out_ref.shape[:2]
     fetches[0].wait()
     rows_ref[...] = pool_ref[...].astype(jnp.float32)
     root = [rows_ref[pl.ds(kind, page, stride=2)] for kind in range(2)]
@@ -51,17 +51,12 @@
         mid = parent_ref[node_count + request] * (2 * page)
         for kind in range(2):
             chosen = rows_ref[pl.ds(mid + kind, page, stride=2)]
-            block_ref[kind, request] = jnp.concatenate([root[kind], chosen], 0).astype(jnp.bfloat16)
+            block = jnp.concatenate([root[kind], chosen], 0).astype(jnp.bfloat16)
+            for copy in range(kind, copies, 2):
+                out_ref[copy, request] = block
         return carry
 
     lax.fori_loop(0, requests, one, 0, unroll=requests <= 8)
-    sends = [
-        pltpu.make_async_copy(block_ref.at[copy % 2], out_hbm.at[copy], sems.at[len(pairs) + copy])
-        for copy in range(copies)
-    ]
-    for send in sends:
-        send.start()
-
     fetches[2].wait()
     fetches[3].wait()
     mid = parent_ref[node_count + lax.axis_index("pool")]
@@ -71,8 +66,8 @@
     offset = jnp.where(offset < 0, offset + requests, offset)
     used = offset < jnp.where(is_mid, pages_ref[mid], pages_ref[0])
     bias_ref[...] = jnp.where(used, 0.0, MASKED)
-    for copy in fetches[4:] + sends:
-        copy.wait()
+    for fetch in fetches[4:]:
+        fetch.wait()
 
 
 def hand_over_kernel(*refs):
@@ -220,20 +215,19 @@
     sent, local_0, bias = pl.pallas_call(
         functools.partial(select_kernel, page),
         out_shape=[
-            jax.ShapeDtypeStruct((tp, stripes, 2 * page, dim), jnp.bfloat16),
+            pltpu.VMEM((tp, stripes, 2 * page, dim), jnp.bfloat16),
             jax.ShapeDtypeStruct((leaf_rows.shape[0] + fresh_rows.shape[0], dim), jnp.bfloat16),
             jax.ShapeDtypeStruct((8, stripes * 2 * page), jnp.float32),
         ],
         in_specs=[hbm] * 6,
-        out_specs=[hbm, vmem, vmem],
+        out_specs=[vmem] * 3,
         scratch_shapes=[
             pltpu.SMEM(parent.shape, jnp.int32),
             pltpu.SMEM(node_pages.shape, jnp.int32),
             pltpu.SMEM(node_owner.shape, jnp.int32),
             pltpu.VMEM(pool_rows.shape, jnp.bfloat16),
             pltpu.VMEM(pool_rows.shape, jnp.float32),
-            pltpu.VMEM((2, stripes, 2 * page, dim), jnp.bfloat16),
-            pltpu.SemaphoreType.DMA((6 + tp,)),
+            pltpu.SemaphoreType.DMA((6,)),
         ],
         compiler_params=pltpu.CompilerParams(vmem_limit_bytes=16 * 2**20),
         cost_estimate=LONG,

time: 20.2 us -> 20.3 us (level)
  no operation moved by 1% of the time
where the time goes in v2:
time: 20.3 us; the launch traced here: 20.1 us
  starting transfers between devices  8.61 us (42%)
  Pallas kernels  5.53 us (27%)
  waiting for transfers between devices  5.22 us (26%)
  between operations  0.7 us (3%)
    all_to_all x1, starting transfers between devices, per_device(): lax.all_to_all(sent.reshape(tp * stripes, 2 * page, dim), ('tp', 'pool'),...  4.92 us
    ppermute x4, starting transfers between devices, per_device(): lax.ppermute(array, 'tp', [(i, i ^ bit) for i in range(tp)])  3.69 us
    all_to_all x1, waiting for transfers between devices, per_device(): lax.all_to_all(sent.reshape(tp * stripes, 2 * page, dim), ('tp', 'pool'),...  3.42 us
    pallas_call x1, Pallas kernels, per_device(): pl.pallas_call(functools.partial(own_kernel, page=page), out_shape=[jax.S...  2.48 us
    ppermute x4, waiting for transfers between devices, per_device(): lax.ppermute(array, 'tp', [(i, i ^ bit) for i in range(tp)])  1.8 us
    pallas_call x1, Pallas kernels, per_device(): pl.pallas_call(functools.partial(select_kernel, page), out_shape=[pltpu.V...  1.63 us
    pallas_call x1, Pallas kernels, per_device(): pl.pallas_call(shared_kernel, out_shape=jax.ShapeDtypeStruct(queries.shap...  1.42 us
  transfers between devices with their start and end apart: 5, of which 4 were waited for; matrix products, arithmetic and copies ran while one was open for 0% of the time, Pallas kernels for 12%

profile of v2, /device:TPU:0, one launch (start us, length us, event | category | flops | bytes accessed | tf_op | source)
XLA Modules:
  0.0 20.1 jit_solution(6821508587948004933)
XLA Ops:
  0.0 1.6 %shard_map.82 = (bf16[4,8,16,128]{3,2,1,0:T(8,128)(2,1)}, bf16[768,128]{1,0:T(8,128)(2,1)S(1)}, f32[8,128]{1,0:T(8,128)S(1)}) custom-call(s32[13]{0:T(128)} %parent_hbm.1, s32[5]{0:T(128)} %pages_hbm.1, s32[5]{0:T(128)} %owner_hbm.1, bf16[80,128]{1,0:T(8,128)(2,1)} %bitcast.8, bf16[512,128]{1,0:T(8,128)(2,1)} %bitcast.6, bf16[256,128]{1,0:T(8,128)(2,1)} %bitcast.7), custom_call_target="tpu_custom_call" | custom-call | flops 49999998976 | bytes 1000000 | tf_op jit(solution)/shard_map/pallas_call | solution.py:215
  1.6 3.0 %collective-permute-start = (bf16[768,128]{1,0:T(8,128)(2,1)S(1)}, bf16[768,128]{1,0:T(8,128)(2,1)S(1)}, u32[]{:S(2)}, u32[]{:S(2)}) collective-permute-start(bf16[768,128]{1,0:T(8,128)(2,1)S(1)} %get-tuple-element.15.refs_0_), channel_id=1, source_target_pairs={{0,2},{1,3},{2,0},{3,1},{4,6},{5,7},{6,4},{7,5},{8,10},{9,11},{10,... | collective-permute-start | bytes 589832 | tf_op jit(solution)/shard_map/ppermute | solution.py:208
  4.6 4.9 %all-to-all-start = ((bf16[32,16,128]{2,1,0:T(8,128)(2,1)}), bf16[32,16,128]{2,1,0:T(8,128)(2,1)S(1)}, u32[]{:S(2)}, u32[]{:S(2)}) async-start(bf16[32,16,128]{2,1,0:T(8,128)(2,1)} %bitcast.3), calls=%async_computation | async-start | bytes 262144 | tf_op jit(solution)/shard_map/all_to_all | solution.py:236
  9.6 0.0 copy-start
  9.6 0.0 collective-permute-done.refs_1_
  9.6 0.3 %collective-permute-start.1 = (bf16[768,128]{1,0:T(8,128)(2,1)S(1)}, bf16[768,128]{1,0:T(8,128)(2,1)S(1)}, u32[]{:S(2)}, u32[]{:S(2)}) collective-permute-start(bf16[768,128]{1,0:T(8,128)(2,1)S(1)} %get-tuple-element.16.rest_0_), channel_id=1, source_target_pairs={{0,1},{1,0},{2,3},{3,2},{4,5},{5,4},{6,7},{7,6},{8,9},{9,8},{10,11... | collective-permute-start | bytes 589832 | tf_op jit(solution)/shard_map/ppermute | solution.py:208
  9.9 0.3 %collective-permute-start.2 = (bf16[768,128]{1,0:T(8,128)(2,1)S(1)}, bf16[768,128]{1,0:T(8,128)(2,1)S(1)}, u32[]{:S(2)}, u32[]{:S(2)}) collective-permute-start(bf16[768,128]{1,0:T(8,128)(2,1)S(1)} %get-tuple-element.17.rest_2_), channel_id=1, source_target_pairs={{0,1},{1,0},{2,3},{3,2},{4,5},{5,4},{6,7},{7,6},{8,9},{9,8},{10,11... | collective-permute-start | bytes 589832 | tf_op jit(solution)/shard_map/ppermute | solution.py:208
  10.8 0.3 %collective-permute-done.1.rest_1_ = bf16[768,128]{1,0:T(8,128)(2,1)S(1)} collective-permute-done((bf16[768,128]{1,0:T(8,128)(2,1)S(1)}, bf16[768,128]{1,0:T(8,128)(2,1)S(1)}, u32[]{:S(2)}, u32[]{:S(2)}) %collective-permute-start.1) | collective-permute-done | bytes 196640 | tf_op jit(solution)/shard_map/ppermute | solution.py:208
  11.1 0.3 %collective-permute-done.2.rest_3_ = bf16[768,128]{1,0:T(8,128)(2,1)S(1)} collective-permute-done((bf16[768,128]{1,0:T(8,128)(2,1)S(1)}, bf16[768,128]{1,0:T(8,128)(2,1)S(1)}, u32[]{:S(2)}, u32[]{:S(2)}) %collective-permute-start.2) | collective-permute-done | bytes 196640 | tf_op jit(solution)/shard_map/ppermute | solution.py:208
  11.4 0.0 copy-done
  11.4 2.5 %shard_map.84 = (f32[4,512,128]{2,1,0:T(8,128)S(1)}, f32[4,512,128]{2,1,0:T(8,128)S(1)}) custom-call(s32[1]{0:T(128)S(6)} %copy.17.leaf_len_ref, bf16[32,64,128]{2,1,0:T(8,128)(2,1)S(1)} %copy-done, bf16[768,128]{1,0:T(8,128)(2,1)S(1)} %get-tuple-element.16.rest_0_, bf16[768,128]{1,0:T(8,128)(2,1)S(1)} %collective-permute-done.1.rest_1_, ...), custom_call_target="tpu_custom_call" | custom-call | flops 1000000 | bytes 100000 | tf_op jit(solution)/shard_map/pallas_call | solution.py:243
  13.9 3.4 %all-to-all-done = bf16[32,16,128]{2,1,0:T(8,128)(2,1)S(1)} async-done(((bf16[32,16,128]{2,1,0:T(8,128)(2,1)}), bf16[32,16,128]{2,1,0:T(8,128)(2,1)S(1)}, u32[]{:S(2)}, u32[]{:S(2)}) %all-to-all-start) | async-done | bytes 131104 | tf_op jit(solution)/shard_map/all_to_all | solution.py:236
  17.3 0.1 collective-permute-start.3
  17.4 1.2 %collective-permute-done.3.theirs_ref = bf16[4,8,16,128]{3,2,1,0:T(8,128)(2,1)S(1)} collective-permute-done((bf16[4,8,16,128]{3,2,1,0:T(8,128)(2,1)S(1)}, bf16[4,8,16,128]{3,2,1,0:T(8,128)(2,1)S(1)}, u32[]{:S(2)}, u32[]{:S(2)}) %collective-permute-start.3) | collective-permute-done | bytes 131104 | tf_op jit(solution)/shard_map/ppermute | solution.py:208
  18.7 1.4 %shard_map.86 = bf16[32,64,128]{2,1,0:T(8,128)(2,1)} custom-call(bf16[32,64,128]{2,1,0:T(8,128)(2,1)S(1)} %copy-done, f32[8,128]{1,0:T(8,128)S(1)} %get-tuple-element.14.bias_ref, f32[4,512,128]{2,1,0:T(8,128)S(1)} %get-tuple-element.18.other_ref, f32[4,512,128]{2,1,0:T(8,128)S(1)} %get-tuple-element.21.level_ref, ...), custom_call_target="tpu_custom_call" | custom-call | tf_op jit(solution)/shard_map/pallas_call | solution.py:255
  (2 shorter events, 0.0 us)
Async XLA Ops:
  1.6 7.9 %collective-permute-start = (bf16[768,128]{1,0:T(8,128)(2,1)S(1)}, bf16[768,128]{1,0:T(8,128)(2,1)S(1)}, u32[]{:S(2)}, u32[]{:S(2)}) collective-permute-start(bf16[768,128]{1,0:T(8,128)(2,1)S(1)} %get-tuple-element.15.refs_0_), channel_id=1, source_target_pairs={{0,2},{1,3},{2,0},{3,1},{4,6},{5,7},{6,4},{7,5},{8,10},{9,11},{10,... | collective-permute-start | bytes 589832 | tf_op jit(solution)/shard_map/ppermute | solution.py:208
  4.6 12.7 %all-to-all-start = ((bf16[32,16,128]{2,1,0:T(8,128)(2,1)}), bf16[32,16,128]{2,1,0:T(8,128)(2,1)S(1)}, u32[]{:S(2)}, u32[]{:S(2)}) async-start(bf16[32,16,128]{2,1,0:T(8,128)(2,1)} %bitcast.3), calls=%async_computation | async-start | bytes 262144 | tf_op jit(solution)/shard_map/all_to_all | solution.py:236
  9.6 1.8 %copy-start = (bf16[32,64,128]{2,1,0:T(8,128)(2,1)S(1)}, bf16[32,64,128]{2,1,0:T(8,128)(2,1)}, u32[]{:S(2)}) copy-start(bf16[32,64,128]{2,1,0:T(8,128)(2,1)} %q_ref.3) | copy-start | bytes 1572868
  9.6 1.5 %collective-permute-start.1 = (bf16[768,128]{1,0:T(8,128)(2,1)S(1)}, bf16[768,128]{1,0:T(8,128)(2,1)S(1)}, u32[]{:S(2)}, u32[]{:S(2)}) collective-permute-start(bf16[768,128]{1,0:T(8,128)(2,1)S(1)} %get-tuple-element.16.rest_0_), channel_id=1, source_target_pairs={{0,1},{1,0},{2,3},{3,2},{4,5},{5,4},{6,7},{7,6},{8,9},{9,8},{10,11... | collective-permute-start | bytes 589832 | tf_op jit(solution)/shard_map/ppermute | solution.py:208
  9.9 1.5 %collective-permute-start.2 = (bf16[768,128]{1,0:T(8,128)(2,1)S(1)}, bf16[768,128]{1,0:T(8,128)(2,1)S(1)}, u32[]{:S(2)}, u32[]{:S(2)}) collective-permute-start(bf16[768,128]{1,0:T(8,128)(2,1)S(1)} %get-tuple-element.17.rest_2_), channel_id=1, source_target_pairs={{0,1},{1,0},{2,3},{3,2},{4,5},{5,4},{6,7},{7,6},{8,9},{9,8},{10,11... | collective-permute-start | bytes 589832 | tf_op jit(solution)/shard_map/ppermute | solution.py:208
  17.3 1.3 %collective-permute-start.3 = (bf16[4,8,16,128]{3,2,1,0:T(8,128)(2,1)S(1)}, bf16[4,8,16,128]{3,2,1,0:T(8,128)(2,1)S(1)}, u32[]{:S(2)}, u32[]{:S(2)}) collective-permute-start(bf16[4,8,16,128]{3,2,1,0:T(8,128)(2,1)S(1)} %get-tuple-element.22.mine_ref), channel_id=1, source_target_pairs={{0,1},{1,0},{2,3},{3,2},{4,5},{5,4},{6,7},{7,6},{8,9},{9,8},{10,11... | collective-permute-start | bytes 393224 | tf_op jit(solution)/shard_map/ppermute | solution.py:208

commit v3 on v1

--- a/solution.py
+++ b/solution.py
@@ -65,12 +65,22 @@
     fetches[2].wait()
     fetches[3].wait()
     mid = parent_ref[node_count + lax.axis_index("pool")]
-    key = lax.broadcasted_iota(jnp.int32, bias_ref.shape, 1)
+    rank = lax.axis_index("tp")
+    dim = bias_ref.shape[1]
+    shared_keys = requests * 2 * page
+    tokens = (bias_ref.shape[0] - shared_keys) // 4
+    key = lax.broadcasted_iota(jnp.int32, (shared_keys, dim), 0)
     stripe, is_mid = key // (2 * page), (key % (2 * page)) >= page
     offset = stripe - jnp.where(is_mid, owner_ref[mid], owner_ref[0])
     offset = jnp.where(offset < 0, offset + requests, offset)
     used = offset < jnp.where(is_mid, pages_ref[mid], pages_ref[0])
-    bias_ref[...] = jnp.where(used, 0.0, MASKED)
+    bias_ref[0:shared_keys] = jnp.where(used, 0.0, MASKED).astype(jnp.bfloat16)
+    key = lax.broadcasted_iota(jnp.int32, (tokens, dim), 0)
+    row = lax.broadcasted_iota(jnp.int32, (tokens, dim), 1)
+    for step in range(4):
+        seen = key <= row if step == 0 else jnp.full((tokens, dim), rank ^ step, jnp.int32) < rank
+        first = shared_keys + step * tokens
+        bias_ref[first : first + tokens] = jnp.where(seen, 0.0, MASKED).astype(jnp.bfloat16)
     for copy in fetches[4:] + sends:
         copy.wait()
 
@@ -102,81 +112,86 @@
     return sums[:, : values.shape[1]], sums[:, values.shape[1] :]
 
 
-def own_kernel(leaf_len_ref, q_ref, *rest, page):
-    local_refs = rest[:4]
-    result_ref, level_ref, bias_ref, kf_ref, vf_ref = rest[4:]
+def leaf_kernel(steps, fresh, leaf_len_ref, q_ref, *refs, page):
+    count = 4 if fresh else len(steps)
+    local_refs, (result_ref, level_ref, *fresh_refs) = refs[:count], refs[count:]
     tokens, q_heads, dim = q_ref.shape
     group = q_heads // 4
-    leaf_slots = bias_ref.shape[0] - 4 * tokens
+    leaf_rows = local_refs[0].shape[0] - 8 * tokens
+    leaf_slots = leaf_rows // 2
     rank = lax.axis_index("tp")
 
+    chunk = 256
+    half = chunk // 2
+    leaf_pick = pick((chunk, chunk), lambda out_row: (out_row % half) * 2 + out_row // half)
     key = lax.broadcasted_iota(jnp.int32, (leaf_slots, dim), 0)
-    bias_ref[0:leaf_slots] = jnp.where(key < leaf_len_ref[0] * page, 0.0, MASKED).astype(jnp.bfloat16)
-    key = lax.broadcasted_iota(jnp.int32, (tokens, dim), 0)
-    row = lax.broadcasted_iota(jnp.int32, (tokens, dim), 1)
-    for step in range(4):
-        seen = key <= row if step == 0 else jnp.full((tokens, dim), rank ^ step, jnp.int32) < rank
-        bias_ref[leaf_slots + step * tokens : leaf_slots + (step + 1) * tokens] = jnp.where(
-            seen, 0.0, MASKED
-        ).astype(jnp.bfloat16)
-
-    fresh_rows = local_refs[0].shape[0] - 2 * leaf_slots
+    bias = jnp.where(key < leaf_len_ref[0] * page, 0.0, MASKED).astype(jnp.bfloat16)
+    column = lax.broadcasted_iota(jnp.int32, (tokens * group, dim), 1)
+    first = jnp.where(column == 0, 1.0, 0.0).astype(jnp.bfloat16)
+    for place, step in enumerate(steps):
+        local_ref = local_refs[step if fresh else place]
+        heads = pl.ds(pl.multiple_of((rank ^ step) * group, group), group)
+        leaf_k, leaf_v = [], []
+        for piece in range(leaf_slots // half):
+            parts = dot(leaf_pick, local_ref[piece * chunk : (piece + 1) * chunk]).astype(jnp.bfloat16)
+            leaf_k.append(parts[:half])
+            leaf_v.append(parts[half:])
+        keys = jnp.concatenate([jnp.concatenate(leaf_k, 0), bias], 1)
+        rows = jnp.concatenate([q_ref[:, heads, :].reshape(tokens * group, dim), first], 1)
+        scores = scores_of(rows, keys)
+        top = jnp.max(scores, axis=1, keepdims=True)
+        sums, totals = weigh(jnp.exp2(scores - top), jnp.concatenate(leaf_v, 0))
+        result_ref[place] = sums / totals
+        level_ref[place] = jnp.log2(totals) + top
+    if not fresh:
+        return
 
     def fresh_source(out_row):
         head, kind, token = out_row // (2 * tokens), (out_row // tokens) % 2, out_row % tokens
         return token * 8 + head * 2 + kind
 
-    fresh_pick = pick((fresh_rows, fresh_rows), fresh_source)
+    kf_ref, vf_ref = fresh_refs
+    fresh_pick = pick((8 * tokens, 8 * tokens), fresh_source)
     for step in range(4):
-        parts = dot(fresh_pick, local_refs[step][2 * leaf_slots :]).astype(jnp.bfloat16)
+        parts = dot(fresh_pick, local_refs[step][leaf_rows:]).astype(jnp.bfloat16)
         for head in range(4):
             base = head * 2 * tokens
             kf_ref[head, step * tokens : (step + 1) * tokens] = parts[base : base + tokens]
             vf_ref[head, step * tokens : (step + 1) * tokens] = parts[base + tokens : base + 2 * tokens]
 
-    chunk = 256
-    half = chunk // 2
-    leaf_pick = pick((chunk, chunk), lambda out_row: (out_row % half) * 2 + out_row // half)
+
+def shared_kernel(q_ref, bias_ref, *refs):
+    other_refs, level_refs = refs[0:3], refs[3:6]
+    kf_ref, vf_ref, mine_ref, theirs_ref, out_hbm, stage_ref, sems = refs[6:]
+    tokens, q_heads, dim = q_ref.shape
+    group = q_heads // 4
+    shared_keys = bias_ref.shape[0] - 4 * tokens
+    rank = lax.axis_index("tp")
+    has_keys = rank % 2 == 0
     bias = bias_ref[...]
     token = lax.broadcasted_iota(jnp.int32, (tokens * group, dim), 0) // group
     column = lax.broadcasted_iota(jnp.int32, (tokens * group, dim), 1)
     own_row = jnp.where(token == column, 1.0, 0.0).astype(jnp.bfloat16)
-    for step in range(4):
-        head = rank ^ step
-        leaf_k, leaf_v = [], []
-        for piece in range(leaf_slots // half):
-            parts = dot(leaf_pick, local_refs[step][piece * chunk : (piece + 1) * chunk]).astype(jnp.bfloat16)
-            leaf_k.append(parts[:half])
-            leaf_v.append(parts[half:])
-        keys = jnp.concatenate([jnp.concatenate(leaf_k + [kf_ref[head]], 0), bias], 1)
-        values = jnp.concatenate(leaf_v + [vf_ref[head]], 0)
-        rows = q_ref[:, pl.ds(pl.multiple_of(head * group, group), group), :].reshape(tokens * group, dim)
-        scores = scores_of(jnp.concatenate([rows, own_row], 1), keys)
-        top = jnp.max(scores, axis=1, keepdims=True)
-        sums, totals = weigh(jnp.exp2(scores - top), values)
-        result_ref[step] = sums / totals
-        level_ref[step] = jnp.log2(totals) + top
-
-
-def shared_kernel(q_ref, bias_ref, other_ref, level_ref, mine_ref, theirs_ref, out_hbm, stage_ref, sems):
-    tokens, q_heads, dim = q_ref.shape
-    group = q_heads // 4
-    shared_keys = bias_ref.shape[1]
-    rank = lax.axis_index("tp")
-    has_keys = rank % 2 == 0
-    bias = bias_ref[0:1]
     places = [pl.ds(pl.multiple_of((rank ^ step) * group, group), group) for step in range(4)]
+    found = [(0, 0), (0, 1), (1, 0), (2, 0)]
 
     def above_level(step):
         head = rank ^ step
-        keys = jnp.where(has_keys, mine_ref[head], theirs_ref[head]).reshape(shared_keys, dim)
-        scores = scores_of(q_ref[:, places[step], :].reshape(tokens * group, dim), keys)
-        return scores + bias - jnp.concatenate([level_ref[step]] * (shared_keys // dim), 1)
+        shared = jnp.where(has_keys, mine_ref[head], theirs_ref[head]).reshape(shared_keys, dim)
+        keys = jnp.concatenate([jnp.concatenate([shared, kf_ref[head]], 0), bias], 1)
+        rows = jnp.concatenate([q_ref[:, places[step], :].reshape(tokens * group, dim), own_row], 1)
+        which, place = found[step]
+        level = level_refs[which][place]
+        return scores_of(rows, keys) - jnp.concatenate([level] * (keys.shape[0] // dim), 1)
 
     def weighted(step, weights):
         head = rank ^ step
-        values = jnp.where(has_keys, theirs_ref[head], mine_ref[head]).reshape(shared_keys, dim)
-        return weigh(weights, values)
+        shared = jnp.where(has_keys, theirs_ref[head], mine_ref[head]).reshape(shared_keys, dim)
+        return weigh(weights, jnp.concatenate([shared, vf_ref[head]], 0))
+
+    def other(step):
+        which, place = found[step]
+        return other_refs[which][place]
 
     def write(step, result):
         stage_ref[step] = result.astype(jnp.bfloat16).reshape(tokens, group, dim)
@@ -189,7 +204,7 @@
     writes = []
     for step in range(4):
         sums, totals = weighted(step, jnp.exp2(scores[step]))
-        writes.append(write(step, (sums + other_ref[step]) / (totals + 1.0)))
+        writes.append(write(step, (sums + other(step)) / (totals + 1.0)))
     too_high = jnp.max(highest) > 100.0
     for copy in writes:
         copy.wait()
@@ -200,8 +215,8 @@
             scores = above_level(step)
             top = jnp.maximum(jnp.max(scores, axis=1, keepdims=True), 0.0)
             sums, totals = weighted(step, jnp.exp2(scores - top))
-            other = jnp.exp2(-top)
-            write(step, (sums + other_ref[step] * other) / (totals + other)).wait()
+            rest = jnp.exp2(-top)
+            write(step, (sums + other(step) * rest) / (totals + rest)).wait()
 
 
 def per_device(queries, fresh, pool, leaf, parent, node_pages, node_owner, leaf_len):
@@ -222,7 +237,7 @@
         out_shape=[
             jax.ShapeDtypeStruct((tp, stripes, 2 * page, dim), jnp.bfloat16),
             jax.ShapeDtypeStruct((leaf_rows.shape[0] + fresh_rows.shape[0], dim), jnp.bfloat16),
-            jax.ShapeDtypeStruct((8, stripes * 2 * page), jnp.float32),
+            jax.ShapeDtypeStruct((stripes * 2 * page + tp * tokens, dim), jnp.bfloat16),
         ],
         in_specs=[hbm] * 6,
         out_specs=[hbm, vmem, vmem],
@@ -238,37 +253,45 @@
         compiler_params=pltpu.CompilerParams(vmem_limit_bytes=16 * 2**20),
         cost_estimate=LONG,
     )(*[pltpu.with_memory_space_constraint(operand, pltpu.HBM) for operand in operands])
-    local_2 = swap(local_0, 2)
     mine = lax.all_to_all(
         sent.reshape(tp * stripes, 2 * page, dim), ("tp", "pool"), split_axis=0, concat_axis=0, tiled=True
     ).reshape(tp, stripes, 2 * page, dim)
-    local_0, local_2 = hand_over(LONG, local_0, local_2)
-    local_1, local_3 = swap(local_0, 1), swap(local_2, 1)
+    local_1, local_2 = swap(local_0, 1), swap(local_0, 2)
 
     rows = tokens * q_heads // tp
-    other, level = pl.pallas_call(
-        functools.partial(own_kernel, page=page),
-        out_shape=[jax.ShapeDtypeStruct((tp, rows, dim), jnp.float32)] * 2,
-        in_specs=[pl.BlockSpec(memory_space=pltpu.SMEM)] + [vmem] * 5,
-        out_specs=[vmem] * 2,
-        scratch_shapes=[pltpu.VMEM((leaf.shape[1] + tp * tokens, dim), jnp.bfloat16)]
-        + [pltpu.VMEM((tp, tp * tokens, dim), jnp.bfloat16)] * 2,
-        compiler_params=pltpu.CompilerParams(vmem_limit_bytes=24 * 2**20),
-        cost_estimate=SHORT,
-    )(leaf_len, queries, local_0, local_1, local_2, local_3)
-    mine, level = hand_over(SHORT, mine, level)
+
+    def leaf_call(steps, fresh, locals_):
+        fresh_out = [jax.ShapeDtypeStruct((tp, tp * tokens, dim), jnp.bfloat16)] * 2 if fresh else []
+        return pl.pallas_call(
+            functools.partial(leaf_kernel, steps, fresh, page=page),
+            out_shape=[jax.ShapeDtypeStruct((len(steps), rows, dim), jnp.float32)] * 2 + fresh_out,
+            in_specs=[pl.BlockSpec(memory_space=pltpu.SMEM)] + [vmem] * (1 + len(locals_)),
+            out_specs=[vmem] * (2 + len(fresh_out)),
+            compiler_params=pltpu.CompilerParams(vmem_limit_bytes=24 * 2**20),
+            cost_estimate=SHORT,
+        )(leaf_len, queries, *locals_)
+
+    other_a, level_a = leaf_call((0, 1), False, (local_0, local_1))
+    local_2, level_a = hand_over(SHORT, local_2, level_a)
+    local_3 = swap(local_2, 1)
+    other_b, level_b = leaf_call((2,), False, (local_2,))
+    mine, level_b = hand_over(SHORT, mine, level_b)
     theirs = swap(mine, 1)
+    other_c, level_c, fresh_k, fresh_v = leaf_call((3,), True, (local_0, local_1, local_2, local_3))
     return pl.pallas_call(
         shared_kernel,
         out_shape=jax.ShapeDtypeStruct(queries.shape, jnp.bfloat16),
-        in_specs=[vmem] * 6,
+        in_specs=[vmem] * 12,
         out_specs=hbm,
         scratch_shapes=[
             pltpu.VMEM((tp, tokens, q_heads // tp, dim), jnp.bfloat16),
             pltpu.SemaphoreType.DMA((tp,)),
         ],
         compiler_params=pltpu.CompilerParams(vmem_limit_bytes=(24 if stripes <= 8 else 48) * 2**20),
-    )(queries, bias, other, level, mine, theirs)
+    )(
+        queries, bias, other_a, other_b, other_c, level_a, level_b, level_c,
+        fresh_k, fresh_v, mine, theirs,
+    )
 
 
 def solution(mesh):

time: 20.2 us -> 20.5 us (1.015)
  Pallas kernels: 5.43 us -> 5.86 us
    all_to_all x1, waiting for transfers between devices: 3.43 us -> 4.87 us  [per_device(): lax.all_to_all(sent.reshape(tp * stripes, 2 * page, dim), ('tp', 'pool'),...]
    ppermute x4, waiting for transfers between devices: 1.8 us -> 0.41 us  [per_device(): lax.ppermute(array, 'tp', [(i, i ^ bit) for i in range(tp)])]
    pallas_call x1, Pallas kernels: 1.41 us -> 1.64 us  [per_device(): pl.pallas_call(shared_kernel, out_shape=jax.ShapeDtypeStruct(queries.shap...]
    pallas_call x1 -> x3, Pallas kernels: 2.48 us -> 2.67 us  [leaf_call(): pl.pallas_call(functools.partial(leaf_kernel, steps, fresh, page=page), o...]
  transfers between devices with their start and end apart: 5 -> 5, of which waited for: 4 -> 2; matrix products, arithmetic and copies ran while one was open for 0% -> 0% of each run, Pallas kernels for 12% -> 13%
where the time goes in v3:
time: 20.5 us; the launch traced here: 20.3 us
  starting transfers between devices  8.43 us (41%)
  Pallas kernels  5.86 us (29%)
  waiting for transfers between devices  5.28 us (26%)
  between operations  0.72 us (4%)
    all_to_all x1, starting transfers between devices, per_device(): lax.all_to_all(sent.reshape(tp * stripes, 2 * page, dim), ('tp', 'pool'),...  4.92 us
    all_to_all x1, waiting for transfers between devices, per_device(): lax.all_to_all(sent.reshape(tp * stripes, 2 * page, dim), ('tp', 'pool'),...  4.87 us
    ppermute x4, starting transfers between devices, per_device(): lax.ppermute(array, 'tp', [(i, i ^ bit) for i in range(tp)])  3.51 us
    pallas_call x3, Pallas kernels, leaf_call(): pl.pallas_call(functools.partial(leaf_kernel, steps, fresh, page=page), o...  2.67 us
    pallas_call x1, Pallas kernels, per_device(): pl.pallas_call(shared_kernel, out_shape=jax.ShapeDtypeStruct(queries.shap...  1.64 us
    pallas_call x1, Pallas kernels, per_device(): pl.pallas_call(functools.partial(select_kernel, page), out_shape=[jax.Sha...  1.55 us
  transfers between devices with their start and end apart: 5, of which 2 were waited for; matrix products, arithmetic and copies ran while one was open for 0% of the time, Pallas kernels for 13%

profile of v3, /device:TPU:0, one launch (start us, length us, event | category | flops | bytes accessed | tf_op | source)
XLA Modules:
  0.0 20.3 jit_solution(3180100081726212058)
XLA Ops:
  0.0 0.0 copy-start
  0.0 1.5 %shard_map.82 = (bf16[4,8,16,128]{3,2,1,0:T(8,128)(2,1)}, bf16[768,128]{1,0:T(8,128)(2,1)S(1)}, bf16[256,128]{1,0:T(8,128)(2,1)S(1)}) custom-call(s32[13]{0:T(128)} %parent_hbm.1, s32[5]{0:T(128)} %pages_hbm.1, s32[5]{0:T(128)} %owner_hbm.1, bf16[80,128]{1,0:T(8,128)(2,1)} %bitcast.8, bf16[512,128]{1,0:T(8,128)(2,1)} %bitcast.6, bf16[256,128]{1,0:T(8,128)(2,1)} %bitcast.7), custom_call_target="tpu_custom_call" | custom-call | flops 49999998976 | bytes 1000000 | tf_op jit(solution)/shard_map/pallas_call | solution.py:235
  1.6 0.5 %collective-permute-start = (bf16[768,128]{1,0:T(8,128)(2,1)S(1)}, bf16[768,128]{1,0:T(8,128)(2,1)S(1)}, u32[]{:S(2)}, u32[]{:S(2)}) collective-permute-start(bf16[768,128]{1,0:T(8,128)(2,1)S(1)} %get-tuple-element.21.refs_0_), channel_id=1, source_target_pairs={{0,1},{1,0},{2,3},{3,2},{4,5},{5,4},{6,7},{7,6},{8,9},{9,8},{10,11... | collective-permute-start | bytes 589832 | tf_op jit(solution)/shard_map/ppermute | solution.py:228
  2.1 2.6 %collective-permute-start.1 = (bf16[768,128]{1,0:T(8,128)(2,1)S(1)}, bf16[768,128]{1,0:T(8,128)(2,1)S(1)}, u32[]{:S(2)}, u32[]{:S(2)}) collective-permute-start(bf16[768,128]{1,0:T(8,128)(2,1)S(1)} %get-tuple-element.21.refs_0_), channel_id=1, source_target_pairs={{0,2},{1,3},{2,0},{3,1},{4,6},{5,7},{6,4},{7,5},{8,10},{9,11},{10,... | collective-permute-start | bytes 589832 | tf_op jit(solution)/shard_map/ppermute | solution.py:228
  4.6 4.9 %all-to-all-start = ((bf16[32,16,128]{2,1,0:T(8,128)(2,1)}), bf16[32,16,128]{2,1,0:T(8,128)(2,1)S(1)}, u32[]{:S(2)}, u32[]{:S(2)}) async-start(bf16[32,16,128]{2,1,0:T(8,128)(2,1)} %bitcast.3), calls=%async_computation | async-start | bytes 262144 | tf_op jit(solution)/shard_map/all_to_all | solution.py:256
  10.2 0.0 collective-permute-done.refs_1_
  10.2 0.0 copy-done
  10.2 1.2 %shard_map.83 = (f32[2,512,128]{2,1,0:T(8,128)S(1)}, f32[2,512,128]{2,1,0:T(8,128)S(1)}) custom-call(s32[1]{0:T(128)S(6)} %copy.17.leaf_len_ref, bf16[32,64,128]{2,1,0:T(8,128)(2,1)S(1)} %copy-done, bf16[768,128]{1,0:T(8,128)(2,1)S(1)} %get-tuple-element.21.refs_0_, bf16[768,128]{1,0:T(8,128)(2,1)S(1)} %collective-permute-done.refs_1_), custom_call_target="tpu_custom_call" | custom-call | flops 1000000 | bytes 100000 | tf_op jit(solution)/shard_map/pallas_call | solution.py:265
  11.4 0.0 collective-permute-done.1.refs_0_
  11.4 0.3 %collective-permute-start.2 = (bf16[768,128]{1,0:T(8,128)(2,1)S(1)}, bf16[768,128]{1,0:T(8,128)(2,1)S(1)}, u32[]{:S(2)}, u32[]{:S(2)}) collective-permute-start(bf16[768,128]{1,0:T(8,128)(2,1)S(1)} %get-tuple-element.24.refs_0_.refs_2_), channel_id=1, source_target_pairs={{0,1},{1,0},{2,3},{3,2},{4,5},{5,4},{6,7},{7,6},{8,9},{9,8},{10,11... | collective-permute-start | bytes 589832 | tf_op jit(solution)/shard_map/ppermute | solution.py:228
  11.8 0.7 %shard_map.85 = (f32[1,512,128]{2,1,0:T(8,128)S(1)}, f32[1,512,128]{2,1,0:T(8,128)S(1)}) custom-call(s32[1]{0:T(128)S(6)} %copy.17.leaf_len_ref, bf16[32,64,128]{2,1,0:T(8,128)(2,1)S(1)} %copy-done, bf16[768,128]{1,0:T(8,128)(2,1)S(1)} %get-tuple-element.24.refs_0_.refs_2_), custom_call_target="tpu_custom_call" | custom-call | flops 1000000 | bytes 100000 | tf_op jit(solution)/shard_map/pallas_call | solution.py:265
  12.4 4.9 %all-to-all-done = bf16[32,16,128]{2,1,0:T(8,128)(2,1)S(1)} async-done(((bf16[32,16,128]{2,1,0:T(8,128)(2,1)}), bf16[32,16,128]{2,1,0:T(8,128)(2,1)S(1)}, u32[]{:S(2)}, u32[]{:S(2)}) %all-to-all-start) | async-done | bytes 131104 | tf_op jit(solution)/shard_map/all_to_all | solution.py:256
  17.3 0.1 collective-permute-start.3
  17.4 0.0 collective-permute-done.2.refs_3_
  17.4 0.8 %shard_map.86 = (f32[1,512,128]{2,1,0:T(8,128)S(1)}, f32[1,512,128]{2,1,0:T(8,128)S(1)}, bf16[4,128,128]{2,1,0:T(8,128)(2,1)S(1)}, bf16[4,128,128]{2,1,0:T(8,128)(2,1)S(1)}) custom-call(s32[1]{0:T(128)S(6)} %copy.17.leaf_len_ref, bf16[32,64,128]{2,1,0:T(8,128)(2,1)S(1)} %copy-done, bf16[768,128]{1,0:T(8,128)(2,1)S(1)} %get-tuple-element.21.refs_0_, ...), custom_call_target="tpu_custom_call" | custom-call | flops 1000000 | bytes 100000 | tf_op jit(solution)/shard_map/pallas_call | solution.py:265
  18.3 0.4 %collective-permute-done.3.refs_9_ = bf16[4,8,16,128]{3,2,1,0:T(8,128)(2,1)S(1)} collective-permute-done((bf16[4,8,16,128]{3,2,1,0:T(8,128)(2,1)S(1)}, bf16[4,8,16,128]{3,2,1,0:T(8,128)(2,1)S(1)}, u32[]{:S(2)}, u32[]{:S(2)}) %collective-permute-start.3) | collective-permute-done | bytes 131104 | tf_op jit(solution)/shard_map/ppermute | solution.py:228
  18.7 1.6 %shard_map.88 = bf16[32,64,128]{2,1,0:T(8,128)(2,1)} custom-call(bf16[32,64,128]{2,1,0:T(8,128)(2,1)S(1)} %copy-done, bf16[256,128]{1,0:T(8,128)(2,1)S(1)} %get-tuple-element.20.bias_ref, f32[2,512,128]{2,1,0:T(8,128)S(1)} %get-tuple-element.22.refs_0_, f32[1,512,128]{2,1,0:T(8,128)S(1)} %get-tuple-element.25.refs_1_, ...), custom_call_target="tpu_custom_call" | custom-call | tf_op jit(solution)/shard_map/pallas_call | solution.py:281
  (2 shorter events, 0.0 us)
Async XLA Ops:
  0.0 10.2 %copy-start = (bf16[32,64,128]{2,1,0:T(8,128)(2,1)S(1)}, bf16[32,64,128]{2,1,0:T(8,128)(2,1)}, u32[]{:S(2)}) copy-start(bf16[32,64,128]{2,1,0:T(8,128)(2,1)} %q_ref.7) | copy-start | bytes 1572868
  1.6 8.7 %collective-permute-start = (bf16[768,128]{1,0:T(8,128)(2,1)S(1)}, bf16[768,128]{1,0:T(8,128)(2,1)S(1)}, u32[]{:S(2)}, u32[]{:S(2)}) collective-permute-start(bf16[768,128]{1,0:T(8,128)(2,1)S(1)} %get-tuple-element.21.refs_0_), channel_id=1, source_target_pairs={{0,1},{1,0},{2,3},{3,2},{4,5},{5,4},{6,7},{7,6},{8,9},{9,8},{10,11... | collective-permute-start | bytes 589832 | tf_op jit(solution)/shard_map/ppermute | solution.py:228
  2.1 9.3 %collective-permute-start.1 = (bf16[768,128]{1,0:T(8,128)(2,1)S(1)}, bf16[768,128]{1,0:T(8,128)(2,1)S(1)}, u32[]{:S(2)}, u32[]{:S(2)}) collective-permute-start(bf16[768,128]{1,0:T(8,128)(2,1)S(1)} %get-tuple-element.21.refs_0_), channel_id=1, source_target_pairs={{0,2},{1,3},{2,0},{3,1},{4,6},{5,7},{6,4},{7,5},{8,10},{9,11},{10,... | collective-permute-start | bytes 589832 | tf_op jit(solution)/shard_map/ppermute | solution.py:228
  4.6 12.7 %all-to-all-start = ((bf16[32,16,128]{2,1,0:T(8,128)(2,1)}), bf16[32,16,128]{2,1,0:T(8,128)(2,1)S(1)}, u32[]{:S(2)}, u32[]{:S(2)}) async-start(bf16[32,16,128]{2,1,0:T(8,128)(2,1)} %bitcast.3), calls=%async_computation | async-start | bytes 262144 | tf_op jit(solution)/shard_map/all_to_all | solution.py:256
  11.4 6.0 %collective-permute-start.2 = (bf16[768,128]{1,0:T(8,128)(2,1)S(1)}, bf16[768,128]{1,0:T(8,128)(2,1)S(1)}, u32[]{:S(2)}, u32[]{:S(2)}) collective-permute-start(bf16[768,128]{1,0:T(8,128)(2,1)S(1)} %get-tuple-element.24.refs_0_.refs_2_), channel_id=1, source_target_pairs={{0,1},{1,0},{2,3},{3,2},{4,5},{5,4},{6,7},{7,6},{8,9},{9,8},{10,11... | collective-permute-start | bytes 589832 | tf_op jit(solution)/shard_map/ppermute | solution.py:228
  17.3 1.3 %collective-permute-start.3 = (bf16[4,8,16,128]{3,2,1,0:T(8,128)(2,1)S(1)}, bf16[4,8,16,128]{3,2,1,0:T(8,128)(2,1)S(1)}, u32[]{:S(2)}, u32[]{:S(2)}) collective-permute-start(bf16[4,8,16,128]{3,2,1,0:T(8,128)(2,1)S(1)} %get-tuple-element.34.refs_8_), channel_id=1, source_target_pairs={{0,1},{1,0},{2,3},{3,2},{4,5},{5,4},{6,7},{7,6},{8,9},{9,8},{10,11... | collective-permute-start | bytes 393224 | tf_op jit(solution)/shard_map/ppermute | solution.py:228

commit v4 on v1

--- a/solution.py
+++ b/solution.py
@@ -51,12 +51,12 @@
         mid = parent_ref[node_count + request] * (2 * page)
         for kind in range(2):
             chosen = rows_ref[pl.ds(mid + kind, page, stride=2)]
-            block_ref[kind, request] = jnp.concatenate([root[kind], chosen], 0).astype(jnp.bfloat16)
+            block_ref[kind, requests - 1 - request] = jnp.concatenate([root[kind], chosen], 0).astype(jnp.bfloat16)
         return carry
 
     lax.fori_loop(0, requests, one, 0, unroll=requests <= 8)
     sends = [
-        pltpu.make_async_copy(block_ref.at[copy % 2], out_hbm.at[copy], sems.at[len(pairs) + copy])
+        pltpu.make_async_copy(block_ref.at[copy % 2], out_hbm.at[copies - 1 - copy], sems.at[len(pairs) + copy])
         for copy in range(copies)
     ]
     for send in sends:
@@ -66,7 +66,7 @@
     fetches[3].wait()
     mid = parent_ref[node_count + lax.axis_index("pool")]
     key = lax.broadcasted_iota(jnp.int32, bias_ref.shape, 1)
-    stripe, is_mid = key // (2 * page), (key % (2 * page)) >= page
+    stripe, is_mid = requests - 1 - key // (2 * page), (key % (2 * page)) >= page
     offset = stripe - jnp.where(is_mid, owner_ref[mid], owner_ref[0])
     offset = jnp.where(offset < 0, offset + requests, offset)
     used = offset < jnp.where(is_mid, pages_ref[mid], pages_ref[0])
@@ -169,13 +169,13 @@
 
     def above_level(step):
         head = rank ^ step
-        keys = jnp.where(has_keys, mine_ref[head], theirs_ref[head]).reshape(shared_keys, dim)
+        keys = jnp.where(has_keys, mine_ref[3 - head], theirs_ref[3 - head]).reshape(shared_keys, dim)
         scores = scores_of(q_ref[:, places[step], :].reshape(tokens * group, dim), keys)
         return scores + bias - jnp.concatenate([level_ref[step]] * (shared_keys // dim), 1)
 
     def weighted(step, weights):
         head = rank ^ step
-        values = jnp.where(has_keys, theirs_ref[head], mine_ref[head]).reshape(shared_keys, dim)
+        values = jnp.where(has_keys, theirs_ref[3 - head], mine_ref[3 - head]).reshape(shared_keys, dim)
         return weigh(weights, values)
 
     def write(step, result):
@@ -240,7 +240,12 @@
     )(*[pltpu.with_memory_space_constraint(operand, pltpu.HBM) for operand in operands])
     local_2 = swap(local_0, 2)
     mine = lax.all_to_all(
-        sent.reshape(tp * stripes, 2 * page, dim), ("tp", "pool"), split_axis=0, concat_axis=0, tiled=True
+        sent.reshape(tp * stripes, 2 * page, dim),
+        ("tp", "pool"),
+        split_axis=0,
+        concat_axis=0,
+        axis_index_groups=[list(reversed(range(tp * stripes)))],
+        tiled=True,
     ).reshape(tp, stripes, 2 * page, dim)
     local_0, local_2 = hand_over(LONG, local_0, local_2)
     local_1, local_3 = swap(local_0, 1), swap(local_2, 1)

time: 20.2 us -> 20.8 us (1.030)
  waiting for transfers between devices: 5.23 us -> 5.95 us
    all_to_all x1, waiting for transfers between devices: 3.43 us -> 4.05 us  [per_device(): lax.all_to_all(sent.reshape(tp * stripes, 2 * page, dim), ('tp', 'pool'),...]
where the time goes in v4:
time: 20.8 us; the launch traced here: 20.6 us
  starting transfers between devices  8.5 us (41%)
  waiting for transfers between devices  5.95 us (29%)
  Pallas kernels  5.44 us (26%)
  between operations  0.7 us (3%)
    all_to_all x1, starting transfers between devices, per_device(): lax.all_to_all(sent.reshape(tp * stripes, 2 * page, dim), ('tp', 'pool'),...  4.92 us
    all_to_all x1, waiting for transfers between devices, per_device(): lax.all_to_all(sent.reshape(tp * stripes, 2 * page, dim), ('tp', 'pool'),...  4.05 us
    ppermute x4, starting transfers between devices, per_device(): lax.ppermute(array, 'tp', [(i, i ^ bit) for i in range(tp)])  3.58 us
    pallas_call x1, Pallas kernels, per_device(): pl.pallas_call(functools.partial(own_kernel, page=page), out_shape=[jax.S...  2.48 us
    ppermute x4, waiting for transfers between devices, per_device(): lax.ppermute(array, 'tp', [(i, i ^ bit) for i in range(tp)])  1.91 us
    pallas_call x1, Pallas kernels, per_device(): pl.pallas_call(functools.partial(select_kernel, page), out_shape=[jax.Sha...  1.54 us
    pallas_call x1, Pallas kernels, per_device(): pl.pallas_call(shared_kernel, out_shape=jax.ShapeDtypeStruct(queries.shap...  1.42 us
  transfers between devices with their start and end apart: 5, of which 4 were waited for; matrix products, arithmetic and copies ran while one was open for 0% of the time, Pallas kernels for 12%

profile of v4, /device:TPU:0, one launch (start us, length us, event | category | flops | bytes accessed | tf_op | source)
XLA Modules:
  0.0 20.6 jit_solution(14583823130127764079)
XLA Ops:
  0.0 1.5 %shard_map.82 = (bf16[4,8,16,128]{3,2,1,0:T(8,128)(2,1)}, bf16[768,128]{1,0:T(8,128)(2,1)S(1)}, f32[8,128]{1,0:T(8,128)S(1)}) custom-call(s32[13]{0:T(128)} %parent_hbm.1, s32[5]{0:T(128)} %pages_hbm.1, s32[5]{0:T(128)} %owner_hbm.1, bf16[80,128]{1,0:T(8,128)(2,1)} %bitcast.8, bf16[512,128]{1,0:T(8,128)(2,1)} %bitcast.6, bf16[256,128]{1,0:T(8,128)(2,1)} %bitcast.7), custom_call_target="tpu_custom_call" | custom-call | flops 49999998976 | bytes 1000000 | tf_op jit(solution)/shard_map/pallas_call | solution.py:220
  1.5 3.0 %collective-permute-start = (bf16[768,128]{1,0:T(8,128)(2,1)S(1)}, bf16[768,128]{1,0:T(8,128)(2,1)S(1)}, u32[]{:S(2)}, u32[]{:S(2)}) collective-permute-start(bf16[768,128]{1,0:T(8,128)(2,1)S(1)} %get-tuple-element.15.refs_0_), channel_id=1, source_target_pairs={{0,2},{1,3},{2,0},{3,1},{4,6},{5,7},{6,4},{7,5},{8,10},{9,11},{10,... | collective-permute-start | bytes 589832 | tf_op jit(solution)/shard_map/ppermute | solution.py:213
  4.6 4.9 %all-to-all-start = ((bf16[32,16,128]{2,1,0:T(8,128)(2,1)}), bf16[32,16,128]{2,1,0:T(8,128)(2,1)S(1)}, u32[]{:S(2)}, u32[]{:S(2)}) async-start(bf16[32,16,128]{2,1,0:T(8,128)(2,1)} %bitcast.3), calls=%async_computation | async-start | bytes 262144 | tf_op jit(solution)/shard_map/all_to_all | solution.py:242
  9.5 0.0 copy-start
  9.5 0.0 collective-permute-done.refs_1_
  9.5 0.3 %collective-permute-start.1 = (bf16[768,128]{1,0:T(8,128)(2,1)S(1)}, bf16[768,128]{1,0:T(8,128)(2,1)S(1)}, u32[]{:S(2)}, u32[]{:S(2)}) collective-permute-start(bf16[768,128]{1,0:T(8,128)(2,1)S(1)} %get-tuple-element.16.rest_0_), channel_id=1, source_target_pairs={{0,1},{1,0},{2,3},{3,2},{4,5},{5,4},{6,7},{7,6},{8,9},{9,8},{10,11... | collective-permute-start | bytes 589832 | tf_op jit(solution)/shard_map/ppermute | solution.py:213
  9.8 0.3 %collective-permute-start.2 = (bf16[768,128]{1,0:T(8,128)(2,1)S(1)}, bf16[768,128]{1,0:T(8,128)(2,1)S(1)}, u32[]{:S(2)}, u32[]{:S(2)}) collective-permute-start(bf16[768,128]{1,0:T(8,128)(2,1)S(1)} %get-tuple-element.17.rest_2_), channel_id=1, source_target_pairs={{0,1},{1,0},{2,3},{3,2},{4,5},{5,4},{6,7},{7,6},{8,9},{9,8},{10,11... | collective-permute-start | bytes 589832 | tf_op jit(solution)/shard_map/ppermute | solution.py:213
  10.7 0.3 %collective-permute-done.1.rest_1_ = bf16[768,128]{1,0:T(8,128)(2,1)S(1)} collective-permute-done((bf16[768,128]{1,0:T(8,128)(2,1)S(1)}, bf16[768,128]{1,0:T(8,128)(2,1)S(1)}, u32[]{:S(2)}, u32[]{:S(2)}) %collective-permute-start.1) | collective-permute-done | bytes 196640 | tf_op jit(solution)/shard_map/ppermute | solution.py:213
  11.0 0.3 %collective-permute-done.2.rest_3_ = bf16[768,128]{1,0:T(8,128)(2,1)S(1)} collective-permute-done((bf16[768,128]{1,0:T(8,128)(2,1)S(1)}, bf16[768,128]{1,0:T(8,128)(2,1)S(1)}, u32[]{:S(2)}, u32[]{:S(2)}) %collective-permute-start.2) | collective-permute-done | bytes 196640 | tf_op jit(solution)/shard_map/ppermute | solution.py:213
  11.3 0.0 copy-done
  11.3 2.5 %shard_map.84 = (f32[4,512,128]{2,1,0:T(8,128)S(1)}, f32[4,512,128]{2,1,0:T(8,128)S(1)}) custom-call(s32[1]{0:T(128)S(6)} %copy.17.leaf_len_ref, bf16[32,64,128]{2,1,0:T(8,128)(2,1)S(1)} %copy-done, bf16[768,128]{1,0:T(8,128)(2,1)S(1)} %get-tuple-element.16.rest_0_, bf16[768,128]{1,0:T(8,128)(2,1)S(1)} %collective-permute-done.1.rest_1_, ...), custom_call_target="tpu_custom_call" | custom-call | flops 1000000 | bytes 100000 | tf_op jit(solution)/shard_map/pallas_call | solution.py:254
  13.8 4.0 %all-to-all-done = bf16[32,16,128]{2,1,0:T(8,128)(2,1)S(1)} async-done(((bf16[32,16,128]{2,1,0:T(8,128)(2,1)}), bf16[32,16,128]{2,1,0:T(8,128)(2,1)S(1)}, u32[]{:S(2)}, u32[]{:S(2)}) %all-to-all-start) | async-done | bytes 131104 | tf_op jit(solution)/shard_map/all_to_all | solution.py:242
  17.8 0.0 collective-permute-start.3
  17.8 1.3 %collective-permute-done.3.theirs_ref = bf16[4,8,16,128]{3,2,1,0:T(8,128)(2,1)S(1)} collective-permute-done((bf16[4,8,16,128]{3,2,1,0:T(8,128)(2,1)S(1)}, bf16[4,8,16,128]{3,2,1,0:T(8,128)(2,1)S(1)}, u32[]{:S(2)}, u32[]{:S(2)}) %collective-permute-start.3) | collective-permute-done | bytes 131104 | tf_op jit(solution)/shard_map/ppermute | solution.py:213
  19.2 1.4 %shard_map.86 = bf16[32,64,128]{2,1,0:T(8,128)(2,1)} custom-call(bf16[32,64,128]{2,1,0:T(8,128)(2,1)S(1)} %copy-done, f32[8,128]{1,0:T(8,128)S(1)} %get-tuple-element.14.bias_ref, f32[4,512,128]{2,1,0:T(8,128)S(1)} %get-tuple-element.18.other_ref, f32[4,512,128]{2,1,0:T(8,128)S(1)} %get-tuple-element.21.level_ref, ...), custom_call_target="tpu_custom_call" | custom-call | tf_op jit(solution)/shard_map/pallas_call | solution.py:266
  (2 shorter events, 0.0 us)
Async XLA Ops:
  1.5 7.9 %collective-permute-start = (bf16[768,128]{1,0:T(8,128)(2,1)S(1)}, bf16[768,128]{1,0:T(8,128)(2,1)S(1)}, u32[]{:S(2)}, u32[]{:S(2)}) collective-permute-start(bf16[768,128]{1,0:T(8,128)(2,1)S(1)} %get-tuple-element.15.refs_0_), channel_id=1, source_target_pairs={{0,2},{1,3},{2,0},{3,1},{4,6},{5,7},{6,4},{7,5},{8,10},{9,11},{10,... | collective-permute-start | bytes 589832 | tf_op jit(solution)/shard_map/ppermute | solution.py:213
  4.6 13.3 %all-to-all-start = ((bf16[32,16,128]{2,1,0:T(8,128)(2,1)}), bf16[32,16,128]{2,1,0:T(8,128)(2,1)S(1)}, u32[]{:S(2)}, u32[]{:S(2)}) async-start(bf16[32,16,128]{2,1,0:T(8,128)(2,1)} %bitcast.3), calls=%async_computation | async-start | bytes 262144 | tf_op jit(solution)/shard_map/all_to_all | solution.py:242
  9.5 1.8 %copy-start = (bf16[32,64,128]{2,1,0:T(8,128)(2,1)S(1)}, bf16[32,64,128]{2,1,0:T(8,128)(2,1)}, u32[]{:S(2)}) copy-start(bf16[32,64,128]{2,1,0:T(8,128)(2,1)} %q_ref.3) | copy-start | bytes 1572868
  9.5 1.5 %collective-permute-start.1 = (bf16[768,128]{1,0:T(8,128)(2,1)S(1)}, bf16[768,128]{1,0:T(8,128)(2,1)S(1)}, u32[]{:S(2)}, u32[]{:S(2)}) collective-permute-start(bf16[768,128]{1,0:T(8,128)(2,1)S(1)} %get-tuple-element.16.rest_0_), channel_id=1, source_target_pairs={{0,1},{1,0},{2,3},{3,2},{4,5},{5,4},{6,7},{7,6},{8,9},{9,8},{10,11... | collective-permute-start | bytes 589832 | tf_op jit(solution)/shard_map/ppermute | solution.py:213
  9.8 1.5 %collective-permute-start.2 = (bf16[768,128]{1,0:T(8,128)(2,1)S(1)}, bf16[768,128]{1,0:T(8,128)(2,1)S(1)}, u32[]{:S(2)}, u32[]{:S(2)}) collective-permute-start(bf16[768,128]{1,0:T(8,128)(2,1)S(1)} %get-tuple-element.17.rest_2_), channel_id=1, source_target_pairs={{0,1},{1,0},{2,3},{3,2},{4,5},{5,4},{6,7},{7,6},{8,9},{9,8},{10,11... | collective-permute-start | bytes 589832 | tf_op jit(solution)/shard_map/ppermute | solution.py:213
  17.8 1.3 %collective-permute-start.3 = (bf16[4,8,16,128]{3,2,1,0:T(8,128)(2,1)S(1)}, bf16[4,8,16,128]{3,2,1,0:T(8,128)(2,1)S(1)}, u32[]{:S(2)}, u32[]{:S(2)}) collective-permute-start(bf16[4,8,16,128]{3,2,1,0:T(8,128)(2,1)S(1)} %get-tuple-element.22.mine_ref), channel_id=1, source_target_pairs={{0,1},{1,0},{2,3},{3,2},{4,5},{5,4},{6,7},{7,6},{8,9},{9,8},{10,11... | collective-permute-start | bytes 393224 | tf_op jit(solution)/shard_map/ppermute | solution.py:213

commit v5 on v1

--- a/solution.py
+++ b/solution.py
@@ -9,6 +9,7 @@
 
 LOG2_E = 1.4426950408889634
 MASKED = -1e30
+HEAD_SIZE = 128
 LONG = pl.CostEstimate(flops=5 * 10**10, bytes_accessed=10**6, transcendentals=0)
 SHORT = pl.CostEstimate(flops=10**6, bytes_accessed=10**5, transcendentals=0)
 
@@ -94,7 +95,7 @@
 
 def scores_of(rows, keys):
     scores = lax.dot_general(rows, keys, (((1,), (1,)), ((), ())), preferred_element_type=jnp.float32)
-    return scores * (LOG2_E * 128 ** (-0.5))
+    return scores * (LOG2_E * HEAD_SIZE ** (-0.5))
 
 
 def weigh(weights, values):
@@ -158,6 +159,11 @@
         level_ref[step] = jnp.log2(totals) + top
 
 
+def blocks(a, b):
+    zero = jnp.zeros_like(a)
+    return jnp.concatenate([jnp.concatenate([a, zero], 1), jnp.concatenate([zero, b], 1)], 0)
+
+
 def shared_kernel(q_ref, bias_ref, other_ref, level_ref, mine_ref, theirs_ref, out_hbm, stage_ref, sems):
     tokens, q_heads, dim = q_ref.shape
     group = q_heads // 4
@@ -166,42 +172,63 @@
     has_keys = rank % 2 == 0
     bias = bias_ref[0:1]
     places = [pl.ds(pl.multiple_of((rank ^ step) * group, group), group) for step in range(4)]
-
-    def above_level(step):
-        head = rank ^ step
-        keys = jnp.where(has_keys, mine_ref[head], theirs_ref[head]).reshape(shared_keys, dim)
-        scores = scores_of(q_ref[:, places[step], :].reshape(tokens * group, dim), keys)
-        return scores + bias - jnp.concatenate([level_ref[step]] * (shared_keys // dim), 1)
-
-    def weighted(step, weights):
-        head = rank ^ step
-        values = jnp.where(has_keys, theirs_ref[head], mine_ref[head]).reshape(shared_keys, dim)
-        return weigh(weights, values)
-
-    def write(step, result):
-        stage_ref[step] = result.astype(jnp.bfloat16).reshape(tokens, group, dim)
-        copy = pltpu.make_async_copy(stage_ref.at[step], out_hbm.at[:, places[step]], sems.at[step])
-        copy.start()
-        return copy
-
-    scores = [above_level(step) for step in range(4)]
-    highest = functools.reduce(jnp.maximum, scores)
+    pairs = ((0, 1), (2, 3))
+    ones = jnp.ones((shared_keys, dim), jnp.bfloat16)
+    ones = blocks(ones, ones)
+
+    def above_level(pair):
+        keys, rows, levels = [], [], []
+        for step in pair:
+            head = rank ^ step
+            keys.append(jnp.where(has_keys, mine_ref[head], theirs_ref[head]).reshape(shared_keys, dim))
+            rows.append(q_ref[:, places[step], :].reshape(tokens * group, dim))
+            levels += [bias - level_ref[step]] if shared_keys == dim else [
+                bias - jnp.concatenate([level_ref[step]] * (shared_keys // dim), 1)
+            ]
+        return scores_of(jnp.concatenate(rows, 1), blocks(*keys)) + jnp.concatenate(levels, 1)
+
+    def weighted(pair, weights):
+        values = []
+        for step in pair:
+            head = rank ^ step
+            values.append(jnp.where(has_keys, theirs_ref[head], mine_ref[head]).reshape(shared_keys, dim))
+        weights = weights.astype(jnp.bfloat16)
+        return dot(weights, blocks(*values)), dot(weights, ones)
+
+    def write(pair, result):
+        copies = []
+        for place, step in enumerate(pair):
+            part = result[:, place * dim : (place + 1) * dim]
+            stage_ref[step] = part.astype(jnp.bfloat16).reshape(tokens, group, dim)
+            copies.append(pltpu.make_async_copy(stage_ref.at[step], out_hbm.at[:, places[step]], sems.at[step]))
+            copies[-1].start()
+        return copies
+
+    def other(pair):
+        return jnp.concatenate([other_ref[step] for step in pair], 1)
+
+    scores = [above_level(pair) for pair in pairs]
     writes = []
-    for step in range(4):
-        sums, totals = weighted(step, jnp.exp2(scores[step]))
-        writes.append(write(step, (sums + other_ref[step]) / (totals + 1.0)))
-    too_high = jnp.max(highest) > 100.0
+    for pair, score in zip(pairs, scores):
+        sums, totals = weighted(pair, jnp.exp2(score))
+        writes += write(pair, (sums + other(pair)) / (totals + 1.0))
+    too_high = jnp.max(functools.reduce(jnp.maximum, scores)) > 100.0
     for copy in writes:
         copy.wait()
 
     @pl.when(too_high)
     def _():
-        for step in range(4):
-            scores = above_level(step)
-            top = jnp.maximum(jnp.max(scores, axis=1, keepdims=True), 0.0)
-            sums, totals = weighted(step, jnp.exp2(scores - top))
-            other = jnp.exp2(-top)
-            write(step, (sums + other_ref[step] * other) / (totals + other)).wait()
+        for pair in pairs:
+            score = above_level(pair)
+            tops = [
+                jnp.maximum(jnp.max(score[:, i * shared_keys : (i + 1) * shared_keys], axis=1, keepdims=True), 0.0)
+                for i in range(2)
+            ]
+            wide = [jnp.broadcast_to(top, (tokens * group, shared_keys)) for top in tops]
+            sums, totals = weighted(pair, jnp.exp2(score - jnp.concatenate(wide, 1)))
+            rest = jnp.concatenate([jnp.broadcast_to(jnp.exp2(-top), (tokens * group, dim)) for top in tops], 1)
+            for copy in write(pair, (sums + other(pair) * rest) / (totals + rest)):
+                copy.wait()
 
 
 def per_device(queries, fresh, pool, leaf, parent, node_pages, node_owner, leaf_len):

time: 20.2 us -> 20.2 us (level)
  no operation moved by 1% of the time
where the time goes in v5:
time: 20.2 us; the launch traced here: 20 us
  starting transfers between devices  8.61 us (43%)
  Pallas kernels  5.45 us (27%)
  waiting for transfers between devices  5.23 us (26%)
  between operations  0.7 us (3%)
    all_to_all x1, starting transfers between devices, per_device(): lax.all_to_all(sent.reshape(tp * stripes, 2 * page, dim), ('tp', 'pool'),...  4.92 us
    ppermute x4, starting transfers between devices, per_device(): lax.ppermute(array, 'tp', [(i, i ^ bit) for i in range(tp)])  3.69 us
    all_to_all x1, waiting for transfers between devices, per_device(): lax.all_to_all(sent.reshape(tp * stripes, 2 * page, dim), ('tp', 'pool'),...  3.43 us
    pallas_call x1, Pallas kernels, per_device(): pl.pallas_call(functools.partial(own_kernel, page=page), out_shape=[jax.S...  2.48 us
    ppermute x4, waiting for transfers between devices, per_device(): lax.ppermute(array, 'tp', [(i, i ^ bit) for i in range(tp)])  1.8 us
    pallas_call x1, Pallas kernels, per_device(): pl.pallas_call(functools.partial(select_kernel, page), out_shape=[jax.Sha...  1.54 us
    pallas_call x1, Pallas kernels, per_device(): pl.pallas_call(shared_kernel, out_shape=jax.ShapeDtypeStruct(queries.shap...  1.43 us
  transfers between devices with their start and end apart: 5, of which 4 were waited for; matrix products, arithmetic and copies ran while one was open for 0% of the time, Pallas kernels for 12%

profile of v5, /device:TPU:0, one launch (start us, length us, event | category | flops | bytes accessed | tf_op | source)
XLA Modules:
  0.0 20.0 jit_solution(7420425078498024494)
XLA Ops:
  0.0 1.5 %shard_map.82 = (bf16[4,8,16,128]{3,2,1,0:T(8,128)(2,1)}, bf16[768,128]{1,0:T(8,128)(2,1)S(1)}, f32[8,128]{1,0:T(8,128)S(1)}) custom-call(s32[13]{0:T(128)} %parent_hbm.1, s32[5]{0:T(128)} %pages_hbm.1, s32[5]{0:T(128)} %owner_hbm.1, bf16[80,128]{1,0:T(8,128)(2,1)} %bitcast.8, bf16[512,128]{1,0:T(8,128)(2,1)} %bitcast.6, bf16[256,128]{1,0:T(8,128)(2,1)} %bitcast.7), custom_call_target="tpu_custom_call" | custom-call | flops 49999998976 | bytes 1000000 | tf_op jit(solution)/shard_map/pallas_call | solution.py:247
  1.5 3.0 %collective-permute-start = (bf16[768,128]{1,0:T(8,128)(2,1)S(1)}, bf16[768,128]{1,0:T(8,128)(2,1)S(1)}, u32[]{:S(2)}, u32[]{:S(2)}) collective-permute-start(bf16[768,128]{1,0:T(8,128)(2,1)S(1)} %get-tuple-element.15.refs_0_), channel_id=1, source_target_pairs={{0,2},{1,3},{2,0},{3,1},{4,6},{5,7},{6,4},{7,5},{8,10},{9,11},{10,... | collective-permute-start | bytes 589832 | tf_op jit(solution)/shard_map/ppermute | solution.py:240
  4.6 4.9 %all-to-all-start = ((bf16[32,16,128]{2,1,0:T(8,128)(2,1)}), bf16[32,16,128]{2,1,0:T(8,128)(2,1)S(1)}, u32[]{:S(2)}, u32[]{:S(2)}) async-start(bf16[32,16,128]{2,1,0:T(8,128)(2,1)} %bitcast.3), calls=%async_computation | async-start | bytes 262144 | tf_op jit(solution)/shard_map/all_to_all | solution.py:269
  9.5 0.0 copy-start
  9.5 0.0 collective-permute-done.refs_1_
  9.5 0.3 %collective-permute-start.1 = (bf16[768,128]{1,0:T(8,128)(2,1)S(1)}, bf16[768,128]{1,0:T(8,128)(2,1)S(1)}, u32[]{:S(2)}, u32[]{:S(2)}) collective-permute-start(bf16[768,128]{1,0:T(8,128)(2,1)S(1)} %get-tuple-element.16.rest_0_), channel_id=1, source_target_pairs={{0,1},{1,0},{2,3},{3,2},{4,5},{5,4},{6,7},{7,6},{8,9},{9,8},{10,11... | collective-permute-start | bytes 589832 | tf_op jit(solution)/shard_map/ppermute | solution.py:240
  9.8 0.3 %collective-permute-start.2 = (bf16[768,128]{1,0:T(8,128)(2,1)S(1)}, bf16[768,128]{1,0:T(8,128)(2,1)S(1)}, u32[]{:S(2)}, u32[]{:S(2)}) collective-permute-start(bf16[768,128]{1,0:T(8,128)(2,1)S(1)} %get-tuple-element.17.rest_2_), channel_id=1, source_target_pairs={{0,1},{1,0},{2,3},{3,2},{4,5},{5,4},{6,7},{7,6},{8,9},{9,8},{10,11... | collective-permute-start | bytes 589832 | tf_op jit(solution)/shard_map/ppermute | solution.py:240
  10.7 0.3 %collective-permute-done.1.rest_1_ = bf16[768,128]{1,0:T(8,128)(2,1)S(1)} collective-permute-done((bf16[768,128]{1,0:T(8,128)(2,1)S(1)}, bf16[768,128]{1,0:T(8,128)(2,1)S(1)}, u32[]{:S(2)}, u32[]{:S(2)}) %collective-permute-start.1) | collective-permute-done | bytes 196640 | tf_op jit(solution)/shard_map/ppermute | solution.py:240
  11.0 0.3 %collective-permute-done.2.rest_3_ = bf16[768,128]{1,0:T(8,128)(2,1)S(1)} collective-permute-done((bf16[768,128]{1,0:T(8,128)(2,1)S(1)}, bf16[768,128]{1,0:T(8,128)(2,1)S(1)}, u32[]{:S(2)}, u32[]{:S(2)}) %collective-permute-start.2) | collective-permute-done | bytes 196640 | tf_op jit(solution)/shard_map/ppermute | solution.py:240
  11.3 0.0 copy-done
  11.3 2.5 %shard_map.84 = (f32[4,512,128]{2,1,0:T(8,128)S(1)}, f32[4,512,128]{2,1,0:T(8,128)S(1)}) custom-call(s32[1]{0:T(128)S(6)} %copy.17.leaf_len_ref, bf16[32,64,128]{2,1,0:T(8,128)(2,1)S(1)} %copy-done, bf16[768,128]{1,0:T(8,128)(2,1)S(1)} %get-tuple-element.16.rest_0_, bf16[768,128]{1,0:T(8,128)(2,1)S(1)} %collective-permute-done.1.rest_1_, ...), custom_call_target="tpu_custom_call" | custom-call | flops 1000000 | bytes 100000 | tf_op jit(solution)/shard_map/pallas_call | solution.py:276
  13.8 3.4 %all-to-all-done = bf16[32,16,128]{2,1,0:T(8,128)(2,1)S(1)} async-done(((bf16[32,16,128]{2,1,0:T(8,128)(2,1)}), bf16[32,16,128]{2,1,0:T(8,128)(2,1)S(1)}, u32[]{:S(2)}, u32[]{:S(2)}) %all-to-all-start) | async-done | bytes 131104 | tf_op jit(solution)/shard_map/all_to_all | solution.py:269
  17.2 0.1 collective-permute-start.3
  17.3 1.2 %collective-permute-done.3.theirs_ref = bf16[4,8,16,128]{3,2,1,0:T(8,128)(2,1)S(1)} collective-permute-done((bf16[4,8,16,128]{3,2,1,0:T(8,128)(2,1)S(1)}, bf16[4,8,16,128]{3,2,1,0:T(8,128)(2,1)S(1)}, u32[]{:S(2)}, u32[]{:S(2)}) %collective-permute-start.3) | collective-permute-done | bytes 131104 | tf_op jit(solution)/shard_map/ppermute | solution.py:240
  18.6 1.4 %shard_map.86 = bf16[32,64,128]{2,1,0:T(8,128)(2,1)} custom-call(bf16[32,64,128]{2,1,0:T(8,128)(2,1)S(1)} %copy-done, f32[8,128]{1,0:T(8,128)S(1)} %get-tuple-element.14.bias_ref, f32[4,512,128]{2,1,0:T(8,128)S(1)} %get-tuple-element.18.other_ref, f32[4,512,128]{2,1,0:T(8,128)S(1)} %get-tuple-element.21.level_ref, ...), custom_call_target="tpu_custom_call" | custom-call | tf_op jit(solution)/shard_map/pallas_call | solution.py:288
  (2 shorter events, 0.0 us)
Async XLA Ops:
  1.5 7.9 %collective-permute-start = (bf16[768,128]{1,0:T(8,128)(2,1)S(1)}, bf16[768,128]{1,0:T(8,128)(2,1)S(1)}, u32[]{:S(2)}, u32[]{:S(2)}) collective-permute-start(bf16[768,128]{1,0:T(8,128)(2,1)S(1)} %get-tuple-element.15.refs_0_), channel_id=1, source_target_pairs={{0,2},{1,3},{2,0},{3,1},{4,6},{5,7},{6,4},{7,5},{8,10},{9,11},{10,... | collective-permute-start | bytes 589832 | tf_op jit(solution)/shard_map/ppermute | solution.py:240
  4.6 12.7 %all-to-all-start = ((bf16[32,16,128]{2,1,0:T(8,128)(2,1)}), bf16[32,16,128]{2,1,0:T(8,128)(2,1)S(1)}, u32[]{:S(2)}, u32[]{:S(2)}) async-start(bf16[32,16,128]{2,1,0:T(8,128)(2,1)} %bitcast.3), calls=%async_computation | async-start | bytes 262144 | tf_op jit(solution)/shard_map/all_to_all | solution.py:269
  9.5 1.8 %copy-start = (bf16[32,64,128]{2,1,0:T(8,128)(2,1)S(1)}, bf16[32,64,128]{2,1,0:T(8,128)(2,1)}, u32[]{:S(2)}) copy-start(bf16[32,64,128]{2,1,0:T(8,128)(2,1)} %q_ref.3) | copy-start | bytes 1572868
  9.5 1.5 %collective-permute-start.1 = (bf16[768,128]{1,0:T(8,128)(2,1)S(1)}, bf16[768,128]{1,0:T(8,128)(2,1)S(1)}, u32[]{:S(2)}, u32[]{:S(2)}) collective-permute-start(bf16[768,128]{1,0:T(8,128)(2,1)S(1)} %get-tuple-element.16.rest_0_), channel_id=1, source_target_pairs={{0,1},{1,0},{2,3},{3,2},{4,5},{5,4},{6,7},{7,6},{8,9},{9,8},{10,11... | collective-permute-start | bytes 589832 | tf_op jit(solution)/shard_map/ppermute | solution.py:240
  9.8 1.5 %collective-permute-start.2 = (bf16[768,128]{1,0:T(8,128)(2,1)S(1)}, bf16[768,128]{1,0:T(8,128)(2,1)S(1)}, u32[]{:S(2)}, u32[]{:S(2)}) collective-permute-start(bf16[768,128]{1,0:T(8,128)(2,1)S(1)} %get-tuple-element.17.rest_2_), channel_id=1, source_target_pairs={{0,1},{1,0},{2,3},{3,2},{4,5},{5,4},{6,7},{7,6},{8,9},{9,8},{10,11... | collective-permute-start | bytes 589832 | tf_op jit(solution)/shard_map/ppermute | solution.py:240
  17.2 1.3 %collective-permute-start.3 = (bf16[4,8,16,128]{3,2,1,0:T(8,128)(2,1)S(1)}, bf16[4,8,16,128]{3,2,1,0:T(8,128)(2,1)S(1)}, u32[]{:S(2)}, u32[]{:S(2)}) collective-permute-start(bf16[4,8,16,128]{3,2,1,0:T(8,128)(2,1)S(1)} %get-tuple-element.22.mine_ref), channel_id=1, source_target_pairs={{0,1},{1,0},{2,3},{3,2},{4,5},{5,4},{6,7},{7,6},{8,9},{9,8},{10,11... | collective-permute-start | bytes 393224 | tf_op jit(solution)/shard_map/ppermute | solution.py:240

commit v6 on v1

--- a/solution.py
+++ b/solution.py
@@ -166,42 +166,53 @@
     has_keys = rank % 2 == 0
     bias = bias_ref[0:1]
     places = [pl.ds(pl.multiple_of((rank ^ step) * group, group), group) for step in range(4)]
-
-    def above_level(step):
+    part = tokens // 2
+    parts = [(step, half) for step in range(4) for half in range(2)]
+
+    def rows_of(ref, step, half):
+        return ref[step, half * part * group : (half + 1) * part * group]
+
+    def above_level(step, half):
         head = rank ^ step
         keys = jnp.where(has_keys, mine_ref[head], theirs_ref[head]).reshape(shared_keys, dim)
-        scores = scores_of(q_ref[:, places[step], :].reshape(tokens * group, dim), keys)
-        return scores + bias - jnp.concatenate([level_ref[step]] * (shared_keys // dim), 1)
+        rows = q_ref[half * part : (half + 1) * part, places[step], :].reshape(part * group, dim)
+        level = rows_of(level_ref, step, half)
+        return scores_of(rows, keys) + bias - jnp.concatenate([level] * (shared_keys // dim), 1)
 
     def weighted(step, weights):
         head = rank ^ step
         values = jnp.where(has_keys, theirs_ref[head], mine_ref[head]).reshape(shared_keys, dim)
         return weigh(weights, values)
 
-    def write(step, result):
-        stage_ref[step] = result.astype(jnp.bfloat16).reshape(tokens, group, dim)
-        copy = pltpu.make_async_copy(stage_ref.at[step], out_hbm.at[:, places[step]], sems.at[step])
+    def write(step, half, result):
+        tile = slice(half * part, (half + 1) * part)
+        stage_ref[step, tile] = result.astype(jnp.bfloat16).reshape(part, group, dim)
+        copy = pltpu.make_async_copy(stage_ref.at[step, tile], out_hbm.at[tile, places[step]], sems.at[2 * step + half])
         copy.start()
         return copy
 
-    scores = [above_level(step) for step in range(4)]
+    ahead = 2
+    scores = [above_level(*parts[i]) for i in range(ahead)]
     highest = functools.reduce(jnp.maximum, scores)
     writes = []
-    for step in range(4):
-        sums, totals = weighted(step, jnp.exp2(scores[step]))
-        writes.append(write(step, (sums + other_ref[step]) / (totals + 1.0)))
+    for i, (step, half) in enumerate(parts):
+        if i + ahead < len(parts):
+            scores.append(above_level(*parts[i + ahead]))
+            highest = jnp.maximum(highest, scores[-1])
+        sums, totals = weighted(step, jnp.exp2(scores[i]))
+        writes.append(write(step, half, (sums + rows_of(other_ref, step, half)) / (totals + 1.0)))
     too_high = jnp.max(highest) > 100.0
     for copy in writes:
         copy.wait()
 
     @pl.when(too_high)
     def _():
-        for step in range(4):
-            scores = above_level(step)
+        for step, half in parts:
+            scores = above_level(step, half)
             top = jnp.maximum(jnp.max(scores, axis=1, keepdims=True), 0.0)
             sums, totals = weighted(step, jnp.exp2(scores - top))
             other = jnp.exp2(-top)
-            write(step, (sums + other_ref[step] * other) / (totals + other)).wait()
+            write(step, half, (sums + rows_of(other_ref, step, half) * other) / (totals + other)).wait()
 
 
 def per_device(queries, fresh, pool, leaf, parent, node_pages, node_owner, leaf_len):
@@ -265,7 +276,7 @@
         out_specs=hbm,
         scratch_shapes=[
             pltpu.VMEM((tp, tokens, q_heads // tp, dim), jnp.bfloat16),
-            pltpu.SemaphoreType.DMA((tp,)),
+            pltpu.SemaphoreType.DMA((2 * tp,)),
         ],
         compiler_params=pltpu.CompilerParams(vmem_limit_bytes=(24 if stripes <= 8 else 48) * 2**20),
     )(queries, bias, other, level, mine, theirs)

time: 20.2 us -> 20.2 us (level)
  no operation moved by 1% of the time
where the time goes in v6:
time: 20.2 us; the launch traced here: 20 us
  starting transfers between devices  8.61 us (43%)
  Pallas kernels  5.46 us (27%)
  waiting for transfers between devices  5.23 us (26%)
  between operations  0.7 us (3%)
    all_to_all x1, starting transfers between devices, per_device(): lax.all_to_all(sent.reshape(tp * stripes, 2 * page, dim), ('tp', 'pool'),...  4.92 us
    ppermute x4, starting transfers between devices, per_device(): lax.ppermute(array, 'tp', [(i, i ^ bit) for i in range(tp)])  3.69 us
    all_to_all x1, waiting for transfers between devices, per_device(): lax.all_to_all(sent.reshape(tp * stripes, 2 * page, dim), ('tp', 'pool'),...  3.43 us
    pallas_call x1, Pallas kernels, per_device(): pl.pallas_call(functools.partial(own_kernel, page=page), out_shape=[jax.S...  2.48 us
    ppermute x4, waiting for transfers between devices, per_device(): lax.ppermute(array, 'tp', [(i, i ^ bit) for i in range(tp)])  1.8 us
    pallas_call x1, Pallas kernels, per_device(): pl.pallas_call(functools.partial(select_kernel, page), out_shape=[jax.Sha...  1.54 us
    pallas_call x1, Pallas kernels, per_device(): pl.pallas_call(shared_kernel, out_shape=jax.ShapeDtypeStruct(queries.shap...  1.44 us
  transfers between devices with their start and end apart: 5, of which 4 were waited for; matrix products, arithmetic and copies ran while one was open for 0% of the time, Pallas kernels for 12%

profile of v6, /device:TPU:0, one launch (start us, length us, event | category | flops | bytes accessed | tf_op | source)
XLA Modules:
  0.0 20.0 jit_solution(16358066186083892125)
XLA Ops:
  0.0 1.5 %shard_map.82 = (bf16[4,8,16,128]{3,2,1,0:T(8,128)(2,1)}, bf16[768,128]{1,0:T(8,128)(2,1)S(1)}, f32[8,128]{1,0:T(8,128)S(1)}) custom-call(s32[13]{0:T(128)} %parent_hbm.1, s32[5]{0:T(128)} %pages_hbm.1, s32[5]{0:T(128)} %owner_hbm.1, bf16[80,128]{1,0:T(8,128)(2,1)} %bitcast.8, bf16[512,128]{1,0:T(8,128)(2,1)} %bitcast.6, bf16[256,128]{1,0:T(8,128)(2,1)} %bitcast.7), custom_call_target="tpu_custom_call" | custom-call | flops 49999998976 | bytes 1000000 | tf_op jit(solution)/shard_map/pallas_call | solution.py:231
  1.5 3.0 %collective-permute-start = (bf16[768,128]{1,0:T(8,128)(2,1)S(1)}, bf16[768,128]{1,0:T(8,128)(2,1)S(1)}, u32[]{:S(2)}, u32[]{:S(2)}) collective-permute-start(bf16[768,128]{1,0:T(8,128)(2,1)S(1)} %get-tuple-element.15.refs_0_), channel_id=1, source_target_pairs={{0,2},{1,3},{2,0},{3,1},{4,6},{5,7},{6,4},{7,5},{8,10},{9,11},{10,... | collective-permute-start | bytes 589832 | tf_op jit(solution)/shard_map/ppermute | solution.py:224
  4.6 4.9 %all-to-all-start = ((bf16[32,16,128]{2,1,0:T(8,128)(2,1)}), bf16[32,16,128]{2,1,0:T(8,128)(2,1)S(1)}, u32[]{:S(2)}, u32[]{:S(2)}) async-start(bf16[32,16,128]{2,1,0:T(8,128)(2,1)} %bitcast.3), calls=%async_computation | async-start | bytes 262144 | tf_op jit(solution)/shard_map/all_to_all | solution.py:253
  9.5 0.0 copy-start
  9.5 0.0 collective-permute-done.refs_1_
  9.5 0.3 %collective-permute-start.1 = (bf16[768,128]{1,0:T(8,128)(2,1)S(1)}, bf16[768,128]{1,0:T(8,128)(2,1)S(1)}, u32[]{:S(2)}, u32[]{:S(2)}) collective-permute-start(bf16[768,128]{1,0:T(8,128)(2,1)S(1)} %get-tuple-element.16.rest_0_), channel_id=1, source_target_pairs={{0,1},{1,0},{2,3},{3,2},{4,5},{5,4},{6,7},{7,6},{8,9},{9,8},{10,11... | collective-permute-start | bytes 589832 | tf_op jit(solution)/shard_map/ppermute | solution.py:224
  9.8 0.3 %collective-permute-start.2 = (bf16[768,128]{1,0:T(8,128)(2,1)S(1)}, bf16[768,128]{1,0:T(8,128)(2,1)S(1)}, u32[]{:S(2)}, u32[]{:S(2)}) collective-permute-start(bf16[768,128]{1,0:T(8,128)(2,1)S(1)} %get-tuple-element.17.rest_2_), channel_id=1, source_target_pairs={{0,1},{1,0},{2,3},{3,2},{4,5},{5,4},{6,7},{7,6},{8,9},{9,8},{10,11... | collective-permute-start | bytes 589832 | tf_op jit(solution)/shard_map/ppermute | solution.py:224
  10.7 0.3 %collective-permute-done.1.rest_1_ = bf16[768,128]{1,0:T(8,128)(2,1)S(1)} collective-permute-done((bf16[768,128]{1,0:T(8,128)(2,1)S(1)}, bf16[768,128]{1,0:T(8,128)(2,1)S(1)}, u32[]{:S(2)}, u32[]{:S(2)}) %collective-permute-start.1) | collective-permute-done | bytes 196640 | tf_op jit(solution)/shard_map/ppermute | solution.py:224
  11.0 0.3 %collective-permute-done.2.rest_3_ = bf16[768,128]{1,0:T(8,128)(2,1)S(1)} collective-permute-done((bf16[768,128]{1,0:T(8,128)(2,1)S(1)}, bf16[768,128]{1,0:T(8,128)(2,1)S(1)}, u32[]{:S(2)}, u32[]{:S(2)}) %collective-permute-start.2) | collective-permute-done | bytes 196640 | tf_op jit(solution)/shard_map/ppermute | solution.py:224
  11.3 0.0 copy-done
  11.3 2.5 %shard_map.84 = (f32[4,512,128]{2,1,0:T(8,128)S(1)}, f32[4,512,128]{2,1,0:T(8,128)S(1)}) custom-call(s32[1]{0:T(128)S(6)} %copy.17.leaf_len_ref, bf16[32,64,128]{2,1,0:T(8,128)(2,1)S(1)} %copy-done, bf16[768,128]{1,0:T(8,128)(2,1)S(1)} %get-tuple-element.16.rest_0_, bf16[768,128]{1,0:T(8,128)(2,1)S(1)} %collective-permute-done.1.rest_1_, ...), custom_call_target="tpu_custom_call" | custom-call | flops 1000000 | bytes 100000 | tf_op jit(solution)/shard_map/pallas_call | solution.py:260
  13.8 3.4 %all-to-all-done = bf16[32,16,128]{2,1,0:T(8,128)(2,1)S(1)} async-done(((bf16[32,16,128]{2,1,0:T(8,128)(2,1)}), bf16[32,16,128]{2,1,0:T(8,128)(2,1)S(1)}, u32[]{:S(2)}, u32[]{:S(2)}) %all-to-all-start) | async-done | bytes 131104 | tf_op jit(solution)/shard_map/all_to_all | solution.py:253
  17.2 0.1 collective-permute-start.3
  17.3 1.2 %collective-permute-done.3.theirs_ref = bf16[4,8,16,128]{3,2,1,0:T(8,128)(2,1)S(1)} collective-permute-done((bf16[4,8,16,128]{3,2,1,0:T(8,128)(2,1)S(1)}, bf16[4,8,16,128]{3,2,1,0:T(8,128)(2,1)S(1)}, u32[]{:S(2)}, u32[]{:S(2)}) %collective-permute-start.3) | collective-permute-done | bytes 131104 | tf_op jit(solution)/shard_map/ppermute | solution.py:224
  18.6 1.4 %shard_map.86 = bf16[32,64,128]{2,1,0:T(8,128)(2,1)} custom-call(bf16[32,64,128]{2,1,0:T(8,128)(2,1)S(1)} %copy-done, f32[8,128]{1,0:T(8,128)S(1)} %get-tuple-element.14.bias_ref, f32[4,512,128]{2,1,0:T(8,128)S(1)} %get-tuple-element.18.other_ref, f32[4,512,128]{2,1,0:T(8,128)S(1)} %get-tuple-element.21.level_ref, ...), custom_call_target="tpu_custom_call" | custom-call | tf_op jit(solution)/shard_map/pallas_call | solution.py:272
  (2 shorter events, 0.0 us)
Async XLA Ops:
  1.5 7.9 %collective-permute-start = (bf16[768,128]{1,0:T(8,128)(2,1)S(1)}, bf16[768,128]{1,0:T(8,128)(2,1)S(1)}, u32[]{:S(2)}, u32[]{:S(2)}) collective-permute-start(bf16[768,128]{1,0:T(8,128)(2,1)S(1)} %get-tuple-element.15.refs_0_), channel_id=1, source_target_pairs={{0,2},{1,3},{2,0},{3,1},{4,6},{5,7},{6,4},{7,5},{8,10},{9,11},{10,... | collective-permute-start | bytes 589832 | tf_op jit(solution)/shard_map/ppermute | solution.py:224
  4.6 12.7 %all-to-all-start = ((bf16[32,16,128]{2,1,0:T(8,128)(2,1)}), bf16[32,16,128]{2,1,0:T(8,128)(2,1)S(1)}, u32[]{:S(2)}, u32[]{:S(2)}) async-start(bf16[32,16,128]{2,1,0:T(8,128)(2,1)} %bitcast.3), calls=%async_computation | async-start | bytes 262144 | tf_op jit(solution)/shard_map/all_to_all | solution.py:253
  9.5 1.8 %copy-start = (bf16[32,64,128]{2,1,0:T(8,128)(2,1)S(1)}, bf16[32,64,128]{2,1,0:T(8,128)(2,1)}, u32[]{:S(2)}) copy-start(bf16[32,64,128]{2,1,0:T(8,128)(2,1)} %q_ref.3) | copy-start | bytes 1572868
  9.5 1.5 %collective-permute-start.1 = (bf16[768,128]{1,0:T(8,128)(2,1)S(1)}, bf16[768,128]{1,0:T(8,128)(2,1)S(1)}, u32[]{:S(2)}, u32[]{:S(2)}) collective-permute-start(bf16[768,128]{1,0:T(8,128)(2,1)S(1)} %get-tuple-element.16.rest_0_), channel_id=1, source_target_pairs={{0,1},{1,0},{2,3},{3,2},{4,5},{5,4},{6,7},{7,6},{8,9},{9,8},{10,11... | collective-permute-start | bytes 589832 | tf_op jit(solution)/shard_map/ppermute | solution.py:224
  9.8 1.5 %collective-permute-start.2 = (bf16[768,128]{1,0:T(8,128)(2,1)S(1)}, bf16[768,128]{1,0:T(8,128)(2,1)S(1)}, u32[]{:S(2)}, u32[]{:S(2)}) collective-permute-start(bf16[768,128]{1,0:T(8,128)(2,1)S(1)} %get-tuple-element.17.rest_2_), channel_id=1, source_target_pairs={{0,1},{1,0},{2,3},{3,2},{4,5},{5,4},{6,7},{7,6},{8,9},{9,8},{10,11... | collective-permute-start | bytes 589832 | tf_op jit(solution)/shard_map/ppermute | solution.py:224
  17.2 1.3 %collective-permute-start.3 = (bf16[4,8,16,128]{3,2,1,0:T(8,128)(2,1)S(1)}, bf16[4,8,16,128]{3,2,1,0:T(8,128)(2,1)S(1)}, u32[]{:S(2)}, u32[]{:S(2)}) collective-permute-start(bf16[4,8,16,128]{3,2,1,0:T(8,128)(2,1)S(1)} %get-tuple-element.22.mine_ref), channel_id=1, source_target_pairs={{0,1},{1,0},{2,3},{3,2},{4,5},{5,4},{6,7},{7,6},{8,9},{9,8},{10,11... | collective-permute-start | bytes 393224 | tf_op jit(solution)/shard_map/ppermute | solution.py:224

commit v7 on v1

--- a/solution.py
+++ b/solution.py
@@ -97,6 +97,11 @@
     return scores * (LOG2_E * 128 ** (-0.5))
 
 
+def over(sums, totals):
+    inverse = pl.reciprocal(totals, approx=True)
+    return sums * (inverse * (2.0 - totals * inverse))
+
+
 def weigh(weights, values):
     sums = dot(weights.astype(jnp.bfloat16), jnp.concatenate([values, jnp.ones_like(values)], 1))
     return sums[:, : values.shape[1]], sums[:, values.shape[1] :]
@@ -185,12 +190,12 @@
         return copy
 
     scores = [above_level(step) for step in range(4)]
-    highest = functools.reduce(jnp.maximum, scores)
-    writes = []
-    for step in range(4):
-        sums, totals = weighted(step, jnp.exp2(scores[step]))
-        writes.append(write(step, (sums + other_ref[step]) / (totals + 1.0)))
-    too_high = jnp.max(highest) > 100.0
+    writes, weights = [], []
+    for step in range(4):
+        weights.append(jnp.exp2(scores[step]).astype(jnp.bfloat16))
+        sums, totals = weighted(step, weights[-1])
+        writes.append(write(step, over(sums + other_ref[step], totals + 1.0)))
+    too_high = jnp.max(functools.reduce(jnp.maximum, weights).astype(jnp.float32)) > 2.0**100
     for copy in writes:
         copy.wait()
 
@@ -201,7 +206,7 @@
             top = jnp.maximum(jnp.max(scores, axis=1, keepdims=True), 0.0)
             sums, totals = weighted(step, jnp.exp2(scores - top))
             other = jnp.exp2(-top)
-            write(step, (sums + other_ref[step] * other) / (totals + other)).wait()
+            write(step, over(sums + other_ref[step] * other, totals + other)).wait()
 
 
 def per_device(queries, fresh, pool, leaf, parent, node_pages, node_owner, leaf_len):

time: 20.2 us -> 20.2 us (level)
  no operation moved by 1% of the time
where the time goes in v7:
time: 20.2 us; the launch traced here: 20 us
  starting transfers between devices  8.61 us (43%)
  Pallas kernels  5.45 us (27%)
  waiting for transfers between devices  5.23 us (26%)
  between operations  0.7 us (3%)
    all_to_all x1, starting transfers between devices, per_device(): lax.all_to_all(sent.reshape(tp * stripes, 2 * page, dim), ('tp', 'pool'),...  4.92 us
    ppermute x4, starting transfers between devices, per_device(): lax.ppermute(array, 'tp', [(i, i ^ bit) for i in range(tp)])  3.69 us
    all_to_all x1, waiting for transfers between devices, per_device(): lax.all_to_all(sent.reshape(tp * stripes, 2 * page, dim), ('tp', 'pool'),...  3.43 us
    pallas_call x1, Pallas kernels, per_device(): pl.pallas_call(functools.partial(own_kernel, page=page), out_shape=[jax.S...  2.48 us
    ppermute x4, waiting for transfers between devices, per_device(): lax.ppermute(array, 'tp', [(i, i ^ bit) for i in range(tp)])  1.8 us
    pallas_call x1, Pallas kernels, per_device(): pl.pallas_call(functools.partial(select_kernel, page), out_shape=[jax.Sha...  1.54 us
    pallas_call x1, Pallas kernels, per_device(): pl.pallas_call(shared_kernel, out_shape=jax.ShapeDtypeStruct(queries.shap...  1.43 us
  transfers between devices with their start and end apart: 5, of which 4 were waited for; matrix products, arithmetic and copies ran while one was open for 0% of the time, Pallas kernels for 12%

profile of v7, /device:TPU:0, one launch (start us, length us, event | category | flops | bytes accessed | tf_op | source)
XLA Modules:
  0.0 20.0 jit_solution(15760564731632091132)
XLA Ops:
  0.0 1.5 %shard_map.82 = (bf16[4,8,16,128]{3,2,1,0:T(8,128)(2,1)}, bf16[768,128]{1,0:T(8,128)(2,1)S(1)}, f32[8,128]{1,0:T(8,128)S(1)}) custom-call(s32[13]{0:T(128)} %parent_hbm.1, s32[5]{0:T(128)} %pages_hbm.1, s32[5]{0:T(128)} %owner_hbm.1, bf16[80,128]{1,0:T(8,128)(2,1)} %bitcast.8, bf16[512,128]{1,0:T(8,128)(2,1)} %bitcast.6, bf16[256,128]{1,0:T(8,128)(2,1)} %bitcast.7), custom_call_target="tpu_custom_call" | custom-call | flops 49999998976 | bytes 1000000 | tf_op jit(solution)/shard_map/pallas_call | solution.py:225
  1.5 3.0 %collective-permute-start = (bf16[768,128]{1,0:T(8,128)(2,1)S(1)}, bf16[768,128]{1,0:T(8,128)(2,1)S(1)}, u32[]{:S(2)}, u32[]{:S(2)}) collective-permute-start(bf16[768,128]{1,0:T(8,128)(2,1)S(1)} %get-tuple-element.15.refs_0_), channel_id=1, source_target_pairs={{0,2},{1,3},{2,0},{3,1},{4,6},{5,7},{6,4},{7,5},{8,10},{9,11},{10,... | collective-permute-start | bytes 589832 | tf_op jit(solution)/shard_map/ppermute | solution.py:218
  4.6 4.9 %all-to-all-start = ((bf16[32,16,128]{2,1,0:T(8,128)(2,1)}), bf16[32,16,128]{2,1,0:T(8,128)(2,1)S(1)}, u32[]{:S(2)}, u32[]{:S(2)}) async-start(bf16[32,16,128]{2,1,0:T(8,128)(2,1)} %bitcast.3), calls=%async_computation | async-start | bytes 262144 | tf_op jit(solution)/shard_map/all_to_all | solution.py:247
  9.5 0.0 copy-start
  9.5 0.0 collective-permute-done.refs_1_
  9.5 0.3 %collective-permute-start.1 = (bf16[768,128]{1,0:T(8,128)(2,1)S(1)}, bf16[768,128]{1,0:T(8,128)(2,1)S(1)}, u32[]{:S(2)}, u32[]{:S(2)}) collective-permute-start(bf16[768,128]{1,0:T(8,128)(2,1)S(1)} %get-tuple-element.16.rest_0_), channel_id=1, source_target_pairs={{0,1},{1,0},{2,3},{3,2},{4,5},{5,4},{6,7},{7,6},{8,9},{9,8},{10,11... | collective-permute-start | bytes 589832 | tf_op jit(solution)/shard_map/ppermute | solution.py:218
  9.8 0.3 %collective-permute-start.2 = (bf16[768,128]{1,0:T(8,128)(2,1)S(1)}, bf16[768,128]{1,0:T(8,128)(2,1)S(1)}, u32[]{:S(2)}, u32[]{:S(2)}) collective-permute-start(bf16[768,128]{1,0:T(8,128)(2,1)S(1)} %get-tuple-element.17.rest_2_), channel_id=1, source_target_pairs={{0,1},{1,0},{2,3},{3,2},{4,5},{5,4},{6,7},{7,6},{8,9},{9,8},{10,11... | collective-permute-start | bytes 589832 | tf_op jit(solution)/shard_map/ppermute | solution.py:218
  10.7 0.3 %collective-permute-done.1.rest_1_ = bf16[768,128]{1,0:T(8,128)(2,1)S(1)} collective-permute-done((bf16[768,128]{1,0:T(8,128)(2,1)S(1)}, bf16[768,128]{1,0:T(8,128)(2,1)S(1)}, u32[]{:S(2)}, u32[]{:S(2)}) %collective-permute-start.1) | collective-permute-done | bytes 196640 | tf_op jit(solution)/shard_map/ppermute | solution.py:218
  11.0 0.3 %collective-permute-done.2.rest_3_ = bf16[768,128]{1,0:T(8,128)(2,1)S(1)} collective-permute-done((bf16[768,128]{1,0:T(8,128)(2,1)S(1)}, bf16[768,128]{1,0:T(8,128)(2,1)S(1)}, u32[]{:S(2)}, u32[]{:S(2)}) %collective-permute-start.2) | collective-permute-done | bytes 196640 | tf_op jit(solution)/shard_map/ppermute | solution.py:218
  11.3 0.0 copy-done
  11.3 2.5 %shard_map.84 = (f32[4,512,128]{2,1,0:T(8,128)S(1)}, f32[4,512,128]{2,1,0:T(8,128)S(1)}) custom-call(s32[1]{0:T(128)S(6)} %copy.17.leaf_len_ref, bf16[32,64,128]{2,1,0:T(8,128)(2,1)S(1)} %copy-done, bf16[768,128]{1,0:T(8,128)(2,1)S(1)} %get-tuple-element.16.rest_0_, bf16[768,128]{1,0:T(8,128)(2,1)S(1)} %collective-permute-done.1.rest_1_, ...), custom_call_target="tpu_custom_call" | custom-call | flops 1000000 | bytes 100000 | tf_op jit(solution)/shard_map/pallas_call | solution.py:254
  13.8 3.4 %all-to-all-done = bf16[32,16,128]{2,1,0:T(8,128)(2,1)S(1)} async-done(((bf16[32,16,128]{2,1,0:T(8,128)(2,1)}), bf16[32,16,128]{2,1,0:T(8,128)(2,1)S(1)}, u32[]{:S(2)}, u32[]{:S(2)}) %all-to-all-start) | async-done | bytes 131104 | tf_op jit(solution)/shard_map/all_to_all | solution.py:247
  17.2 0.1 collective-permute-start.3
  17.3 1.2 %collective-permute-done.3.theirs_ref = bf16[4,8,16,128]{3,2,1,0:T(8,128)(2,1)S(1)} collective-permute-done((bf16[4,8,16,128]{3,2,1,0:T(8,128)(2,1)S(1)}, bf16[4,8,16,128]{3,2,1,0:T(8,128)(2,1)S(1)}, u32[]{:S(2)}, u32[]{:S(2)}) %collective-permute-start.3) | collective-permute-done | bytes 131104 | tf_op jit(solution)/shard_map/ppermute | solution.py:218
  18.6 1.4 %shard_map.86 = bf16[32,64,128]{2,1,0:T(8,128)(2,1)} custom-call(bf16[32,64,128]{2,1,0:T(8,128)(2,1)S(1)} %copy-done, f32[8,128]{1,0:T(8,128)S(1)} %get-tuple-element.14.bias_ref, f32[4,512,128]{2,1,0:T(8,128)S(1)} %get-tuple-element.18.other_ref, f32[4,512,128]{2,1,0:T(8,128)S(1)} %get-tuple-element.21.level_ref, ...), custom_call_target="tpu_custom_call" | custom-call | tf_op jit(solution)/shard_map/pallas_call | solution.py:266
  (2 shorter events, 0.0 us)
Async XLA Ops:
  1.5 7.9 %collective-permute-start = (bf16[768,128]{1,0:T(8,128)(2,1)S(1)}, bf16[768,128]{1,0:T(8,128)(2,1)S(1)}, u32[]{:S(2)}, u32[]{:S(2)}) collective-permute-start(bf16[768,128]{1,0:T(8,128)(2,1)S(1)} %get-tuple-element.15.refs_0_), channel_id=1, source_target_pairs={{0,2},{1,3},{2,0},{3,1},{4,6},{5,7},{6,4},{7,5},{8,10},{9,11},{10,... | collective-permute-start | bytes 589832 | tf_op jit(solution)/shard_map/ppermute | solution.py:218
  4.6 12.7 %all-to-all-start = ((bf16[32,16,128]{2,1,0:T(8,128)(2,1)}), bf16[32,16,128]{2,1,0:T(8,128)(2,1)S(1)}, u32[]{:S(2)}, u32[]{:S(2)}) async-start(bf16[32,16,128]{2,1,0:T(8,128)(2,1)} %bitcast.3), calls=%async_computation | async-start | bytes 262144 | tf_op jit(solution)/shard_map/all_to_all | solution.py:247
  9.5 1.8 %copy-start = (bf16[32,64,128]{2,1,0:T(8,128)(2,1)S(1)}, bf16[32,64,128]{2,1,0:T(8,128)(2,1)}, u32[]{:S(2)}) copy-start(bf16[32,64,128]{2,1,0:T(8,128)(2,1)} %q_ref.3) | copy-start | bytes 1572868
  9.5 1.5 %collective-permute-start.1 = (bf16[768,128]{1,0:T(8,128)(2,1)S(1)}, bf16[768,128]{1,0:T(8,128)(2,1)S(1)}, u32[]{:S(2)}, u32[]{:S(2)}) collective-permute-start(bf16[768,128]{1,0:T(8,128)(2,1)S(1)} %get-tuple-element.16.rest_0_), channel_id=1, source_target_pairs={{0,1},{1,0},{2,3},{3,2},{4,5},{5,4},{6,7},{7,6},{8,9},{9,8},{10,11... | collective-permute-start | bytes 589832 | tf_op jit(solution)/shard_map/ppermute | solution.py:218
  9.8 1.5 %collective-permute-start.2 = (bf16[768,128]{1,0:T(8,128)(2,1)S(1)}, bf16[768,128]{1,0:T(8,128)(2,1)S(1)}, u32[]{:S(2)}, u32[]{:S(2)}) collective-permute-start(bf16[768,128]{1,0:T(8,128)(2,1)S(1)} %get-tuple-element.17.rest_2_), channel_id=1, source_target_pairs={{0,1},{1,0},{2,3},{3,2},{4,5},{5,4},{6,7},{7,6},{8,9},{9,8},{10,11... | collective-permute-start | bytes 589832 | tf_op jit(solution)/shard_map/ppermute | solution.py:218
  17.2 1.3 %collective-permute-start.3 = (bf16[4,8,16,128]{3,2,1,0:T(8,128)(2,1)S(1)}, bf16[4,8,16,128]{3,2,1,0:T(8,128)(2,1)S(1)}, u32[]{:S(2)}, u32[]{:S(2)}) collective-permute-start(bf16[4,8,16,128]{3,2,1,0:T(8,128)(2,1)S(1)} %get-tuple-element.22.mine_ref), channel_id=1, source_target_pairs={{0,1},{1,0},{2,3},{3,2},{4,5},{5,4},{6,7},{7,6},{8,9},{9,8},{10,11... | collective-permute-start | bytes 393224 | tf_op jit(solution)/shard_map/ppermute | solution.py:218

commit v8 on v7

--- a/solution.py
+++ b/solution.py
@@ -171,42 +171,59 @@
     has_keys = rank % 2 == 0
     bias = bias_ref[0:1]
     places = [pl.ds(pl.multiple_of((rank ^ step) * group, group), group) for step in range(4)]
-
-    def above_level(step):
+    part = tokens // 2
+    parts = [(half, step) for half in range(2) for step in range(4)]
+
+    def rows_of(ref, half, step):
+        return ref[step, half * part * group : (half + 1) * part * group]
+
+    def above_level(half, step):
         head = rank ^ step
         keys = jnp.where(has_keys, mine_ref[head], theirs_ref[head]).reshape(shared_keys, dim)
-        scores = scores_of(q_ref[:, places[step], :].reshape(tokens * group, dim), keys)
-        return scores + bias - jnp.concatenate([level_ref[step]] * (shared_keys // dim), 1)
+        rows = q_ref[half * part : (half + 1) * part, places[step], :].reshape(part * group, dim)
+        level = rows_of(level_ref, half, step)
+        return scores_of(rows, keys) + bias - jnp.concatenate([level] * (shared_keys // dim), 1)
 
     def weighted(step, weights):
         head = rank ^ step
         values = jnp.where(has_keys, theirs_ref[head], mine_ref[head]).reshape(shared_keys, dim)
         return weigh(weights, values)
 
-    def write(step, result):
-        stage_ref[step] = result.astype(jnp.bfloat16).reshape(tokens, group, dim)
-        copy = pltpu.make_async_copy(stage_ref.at[step], out_hbm.at[:, places[step]], sems.at[step])
+    def store(half, step, result):
+        tile = slice(half * part, (half + 1) * part)
+        stage_ref[tile, places[step], :] = result.astype(jnp.bfloat16).reshape(part, group, dim)
+
+    def write(half):
+        tile = pl.ds(half * part, part)
+        copy = pltpu.make_async_copy(stage_ref.at[tile], out_hbm.at[tile], sems.at[half])
         copy.start()
         return copy
 
-    scores = [above_level(step) for step in range(4)]
+    ahead = 2
+    scores = [above_level(*parts[i]) for i in range(ahead)]
     writes, weights = [], []
-    for step in range(4):
-        weights.append(jnp.exp2(scores[step]).astype(jnp.bfloat16))
+    for i, (half, step) in enumerate(parts):
+        if i + ahead < len(parts):
+            scores.append(above_level(*parts[i + ahead]))
+        weights.append(jnp.exp2(scores[i]).astype(jnp.bfloat16))
         sums, totals = weighted(step, weights[-1])
-        writes.append(write(step, over(sums + other_ref[step], totals + 1.0)))
+        store(half, step, over(sums + rows_of(other_ref, half, step), totals + 1.0))
+        if step == 3:
+            writes.append(write(half))
     too_high = jnp.max(functools.reduce(jnp.maximum, weights).astype(jnp.float32)) > 2.0**100
     for copy in writes:
         copy.wait()
 
     @pl.when(too_high)
     def _():
-        for step in range(4):
-            scores = above_level(step)
-            top = jnp.maximum(jnp.max(scores, axis=1, keepdims=True), 0.0)
-            sums, totals = weighted(step, jnp.exp2(scores - top))
+        for half, step in parts:
+            score = above_level(half, step)
+            top = jnp.maximum(jnp.max(score, axis=1, keepdims=True), 0.0)
+            sums, totals = weighted(step, jnp.exp2(score - top))
             other = jnp.exp2(-top)
-            write(step, over(sums + other_ref[step] * other, totals + other)).wait()
+            store(half, step, over(sums + rows_of(other_ref, half, step) * other, totals + other))
+        for half in range(2):
+            write(half).wait()
 
 
 def per_device(queries, fresh, pool, leaf, parent, node_pages, node_owner, leaf_len):
@@ -269,8 +286,8 @@
         in_specs=[vmem] * 6,
         out_specs=hbm,
         scratch_shapes=[
-            pltpu.VMEM((tp, tokens, q_heads // tp, dim), jnp.bfloat16),
-            pltpu.SemaphoreType.DMA((tp,)),
+            pltpu.VMEM(queries.shape, jnp.bfloat16),
+            pltpu.SemaphoreType.DMA((2,)),
         ],
         compiler_params=pltpu.CompilerParams(vmem_limit_bytes=(24 if stripes <= 8 else 48) * 2**20),
     )(queries, bias, other, level, mine, theirs)

time: 20.2 us -> 20.3 us (level)
  no operation moved by 1% of the time
where the time goes in v8:
time: 20.3 us; the launch traced here: 20.1 us
  starting transfers between devices  8.61 us (42%)
  Pallas kernels  5.52 us (27%)
  waiting for transfers between devices  5.23 us (26%)
  between operations  0.7 us (3%)
    all_to_all x1, starting transfers between devices, per_device(): lax.all_to_all(sent.reshape(tp * stripes, 2 * page, dim), ('tp', 'pool'),...  4.92 us
    ppermute x4, starting transfers between devices, per_device(): lax.ppermute(array, 'tp', [(i, i ^ bit) for i in range(tp)])  3.69 us
    all_to_all x1, waiting for transfers between devices, per_device(): lax.all_to_all(sent.reshape(tp * stripes, 2 * page, dim), ('tp', 'pool'),...  3.43 us
    pallas_call x1, Pallas kernels, per_device(): pl.pallas_call(functools.partial(own_kernel, page=page), out_shape=[jax.S...  2.48 us
    ppermute x4, waiting for transfers between devices, per_device(): lax.ppermute(array, 'tp', [(i, i ^ bit) for i in range(tp)])  1.8 us
    pallas_call x1, Pallas kernels, per_device(): pl.pallas_call(functools.partial(select_kernel, page), out_shape=[jax.Sha...  1.54 us
    pallas_call x1, Pallas kernels, per_device(): pl.pallas_call(shared_kernel, out_shape=jax.ShapeDtypeStruct(queries.shap...  1.49 us
  transfers between devices with their start and end apart: 5, of which 4 were waited for; matrix products, arithmetic and copies ran while one was open for 0% of the time, Pallas kernels for 12%

profile of v8, /device:TPU:0, one launch (start us, length us, event | category | flops | bytes accessed | tf_op | source)
XLA Modules:
  0.0 20.1 jit_solution(3344950824967806215)
XLA Ops:
  0.0 1.5 %shard_map.82 = (bf16[4,8,16,128]{3,2,1,0:T(8,128)(2,1)}, bf16[768,128]{1,0:T(8,128)(2,1)S(1)}, f32[8,128]{1,0:T(8,128)S(1)}) custom-call(s32[13]{0:T(128)} %parent_hbm.1, s32[5]{0:T(128)} %pages_hbm.1, s32[5]{0:T(128)} %owner_hbm.1, bf16[80,128]{1,0:T(8,128)(2,1)} %bitcast.8, bf16[512,128]{1,0:T(8,128)(2,1)} %bitcast.6, bf16[256,128]{1,0:T(8,128)(2,1)} %bitcast.7), custom_call_target="tpu_custom_call" | custom-call | flops 49999998976 | bytes 1000000 | tf_op jit(solution)/shard_map/pallas_call | solution.py:242
  1.5 3.0 %collective-permute-start = (bf16[768,128]{1,0:T(8,128)(2,1)S(1)}, bf16[768,128]{1,0:T(8,128)(2,1)S(1)}, u32[]{:S(2)}, u32[]{:S(2)}) collective-permute-start(bf16[768,128]{1,0:T(8,128)(2,1)S(1)} %get-tuple-element.15.refs_0_), channel_id=1, source_target_pairs={{0,2},{1,3},{2,0},{3,1},{4,6},{5,7},{6,4},{7,5},{8,10},{9,11},{10,... | collective-permute-start | bytes 589832 | tf_op jit(solution)/shard_map/ppermute | solution.py:235
  4.6 4.9 %all-to-all-start = ((bf16[32,16,128]{2,1,0:T(8,128)(2,1)}), bf16[32,16,128]{2,1,0:T(8,128)(2,1)S(1)}, u32[]{:S(2)}, u32[]{:S(2)}) async-start(bf16[32,16,128]{2,1,0:T(8,128)(2,1)} %bitcast.3), calls=%async_computation | async-start | bytes 262144 | tf_op jit(solution)/shard_map/all_to_all | solution.py:264
  9.5 0.0 copy-start
  9.5 0.0 collective-permute-done.refs_1_
  9.5 0.3 %collective-permute-start.1 = (bf16[768,128]{1,0:T(8,128)(2,1)S(1)}, bf16[768,128]{1,0:T(8,128)(2,1)S(1)}, u32[]{:S(2)}, u32[]{:S(2)}) collective-permute-start(bf16[768,128]{1,0:T(8,128)(2,1)S(1)} %get-tuple-element.16.rest_0_), channel_id=1, source_target_pairs={{0,1},{1,0},{2,3},{3,2},{4,5},{5,4},{6,7},{7,6},{8,9},{9,8},{10,11... | collective-permute-start | bytes 589832 | tf_op jit(solution)/shard_map/ppermute | solution.py:235
  9.8 0.3 %collective-permute-start.2 = (bf16[768,128]{1,0:T(8,128)(2,1)S(1)}, bf16[768,128]{1,0:T(8,128)(2,1)S(1)}, u32[]{:S(2)}, u32[]{:S(2)}) collective-permute-start(bf16[768,128]{1,0:T(8,128)(2,1)S(1)} %get-tuple-element.17.rest_2_), channel_id=1, source_target_pairs={{0,1},{1,0},{2,3},{3,2},{4,5},{5,4},{6,7},{7,6},{8,9},{9,8},{10,11... | collective-permute-start | bytes 589832 | tf_op jit(solution)/shard_map/ppermute | solution.py:235
  10.7 0.3 %collective-permute-done.1.rest_1_ = bf16[768,128]{1,0:T(8,128)(2,1)S(1)} collective-permute-done((bf16[768,128]{1,0:T(8,128)(2,1)S(1)}, bf16[768,128]{1,0:T(8,128)(2,1)S(1)}, u32[]{:S(2)}, u32[]{:S(2)}) %collective-permute-start.1) | collective-permute-done | bytes 196640 | tf_op jit(solution)/shard_map/ppermute | solution.py:235
  11.0 0.3 %collective-permute-done.2.rest_3_ = bf16[768,128]{1,0:T(8,128)(2,1)S(1)} collective-permute-done((bf16[768,128]{1,0:T(8,128)(2,1)S(1)}, bf16[768,128]{1,0:T(8,128)(2,1)S(1)}, u32[]{:S(2)}, u32[]{:S(2)}) %collective-permute-start.2) | collective-permute-done | bytes 196640 | tf_op jit(solution)/shard_map/ppermute | solution.py:235
  11.3 0.0 copy-done
  11.3 2.5 %shard_map.84 = (f32[4,512,128]{2,1,0:T(8,128)S(1)}, f32[4,512,128]{2,1,0:T(8,128)S(1)}) custom-call(s32[1]{0:T(128)S(6)} %copy.17.leaf_len_ref, bf16[32,64,128]{2,1,0:T(8,128)(2,1)S(1)} %copy-done, bf16[768,128]{1,0:T(8,128)(2,1)S(1)} %get-tuple-element.16.rest_0_, bf16[768,128]{1,0:T(8,128)(2,1)S(1)} %collective-permute-done.1.rest_1_, ...), custom_call_target="tpu_custom_call" | custom-call | flops 1000000 | bytes 100000 | tf_op jit(solution)/shard_map/pallas_call | solution.py:271
  13.8 3.4 %all-to-all-done = bf16[32,16,128]{2,1,0:T(8,128)(2,1)S(1)} async-done(((bf16[32,16,128]{2,1,0:T(8,128)(2,1)}), bf16[32,16,128]{2,1,0:T(8,128)(2,1)S(1)}, u32[]{:S(2)}, u32[]{:S(2)}) %all-to-all-start) | async-done | bytes 131104 | tf_op jit(solution)/shard_map/all_to_all | solution.py:264
  17.2 0.1 collective-permute-start.3
  17.3 1.2 %collective-permute-done.3.theirs_ref = bf16[4,8,16,128]{3,2,1,0:T(8,128)(2,1)S(1)} collective-permute-done((bf16[4,8,16,128]{3,2,1,0:T(8,128)(2,1)S(1)}, bf16[4,8,16,128]{3,2,1,0:T(8,128)(2,1)S(1)}, u32[]{:S(2)}, u32[]{:S(2)}) %collective-permute-start.3) | collective-permute-done | bytes 131104 | tf_op jit(solution)/shard_map/ppermute | solution.py:235
  18.6 1.5 %shard_map.86 = bf16[32,64,128]{2,1,0:T(8,128)(2,1)} custom-call(bf16[32,64,128]{2,1,0:T(8,128)(2,1)S(1)} %copy-done, f32[8,128]{1,0:T(8,128)S(1)} %get-tuple-element.14.bias_ref, f32[4,512,128]{2,1,0:T(8,128)S(1)} %get-tuple-element.18.other_ref, f32[4,512,128]{2,1,0:T(8,128)S(1)} %get-tuple-element.21.level_ref, ...), custom_call_target="tpu_custom_call" | custom-call | tf_op jit(solution)/shard_map/pallas_call | solution.py:283
  (2 shorter events, 0.0 us)
Async XLA Ops:
  1.5 7.9 %collective-permute-start = (bf16[768,128]{1,0:T(8,128)(2,1)S(1)}, bf16[768,128]{1,0:T(8,128)(2,1)S(1)}, u32[]{:S(2)}, u32[]{:S(2)}) collective-permute-start(bf16[768,128]{1,0:T(8,128)(2,1)S(1)} %get-tuple-element.15.refs_0_), channel_id=1, source_target_pairs={{0,2},{1,3},{2,0},{3,1},{4,6},{5,7},{6,4},{7,5},{8,10},{9,11},{10,... | collective-permute-start | bytes 589832 | tf_op jit(solution)/shard_map/ppermute | solution.py:235
  4.6 12.7 %all-to-all-start = ((bf16[32,16,128]{2,1,0:T(8,128)(2,1)}), bf16[32,16,128]{2,1,0:T(8,128)(2,1)S(1)}, u32[]{:S(2)}, u32[]{:S(2)}) async-start(bf16[32,16,128]{2,1,0:T(8,128)(2,1)} %bitcast.3), calls=%async_computation | async-start | bytes 262144 | tf_op jit(solution)/shard_map/all_to_all | solution.py:264
  9.5 1.8 %copy-start = (bf16[32,64,128]{2,1,0:T(8,128)(2,1)S(1)}, bf16[32,64,128]{2,1,0:T(8,128)(2,1)}, u32[]{:S(2)}) copy-start(bf16[32,64,128]{2,1,0:T(8,128)(2,1)} %q_ref.3) | copy-start | bytes 1572868
  9.5 1.5 %collective-permute-start.1 = (bf16[768,128]{1,0:T(8,128)(2,1)S(1)}, bf16[768,128]{1,0:T(8,128)(2,1)S(1)}, u32[]{:S(2)}, u32[]{:S(2)}) collective-permute-start(bf16[768,128]{1,0:T(8,128)(2,1)S(1)} %get-tuple-element.16.rest_0_), channel_id=1, source_target_pairs={{0,1},{1,0},{2,3},{3,2},{4,5},{5,4},{6,7},{7,6},{8,9},{9,8},{10,11... | collective-permute-start | bytes 589832 | tf_op jit(solution)/shard_map/ppermute | solution.py:235
  9.8 1.5 %collective-permute-start.2 = (bf16[768,128]{1,0:T(8,128)(2,1)S(1)}, bf16[768,128]{1,0:T(8,128)(2,1)S(1)}, u32[]{:S(2)}, u32[]{:S(2)}) collective-permute-start(bf16[768,128]{1,0:T(8,128)(2,1)S(1)} %get-tuple-element.17.rest_2_), channel_id=1, source_target_pairs={{0,1},{1,0},{2,3},{3,2},{4,5},{5,4},{6,7},{7,6},{8,9},{9,8},{10,11... | collective-permute-start | bytes 589832 | tf_op jit(solution)/shard_map/ppermute | solution.py:235
  17.2 1.3 %collective-permute-start.3 = (bf16[4,8,16,128]{3,2,1,0:T(8,128)(2,1)S(1)}, bf16[4,8,16,128]{3,2,1,0:T(8,128)(2,1)S(1)}, u32[]{:S(2)}, u32[]{:S(2)}) collective-permute-start(bf16[4,8,16,128]{3,2,1,0:T(8,128)(2,1)S(1)} %get-tuple-element.22.mine_ref), channel_id=1, source_target_pairs={{0,1},{1,0},{2,3},{3,2},{4,5},{5,4},{6,7},{7,6},{8,9},{9,8},{10,11... | collective-permute-start | bytes 393224 | tf_op jit(solution)/shard_map/ppermute | solution.py:235

commit v9 on v7

--- a/solution.py
+++ b/solution.py
@@ -170,12 +170,12 @@
     rank = lax.axis_index("tp")
     has_keys = rank % 2 == 0
     bias = bias_ref[0:1]
-    places = [pl.ds(pl.multiple_of((rank ^ step) * group, group), group) for step in range(4)]
+    place = lambda step: pl.ds(pl.multiple_of((rank ^ step) * group, group), group)
 
     def above_level(step):
         head = rank ^ step
         keys = jnp.where(has_keys, mine_ref[head], theirs_ref[head]).reshape(shared_keys, dim)
-        scores = scores_of(q_ref[:, places[step], :].reshape(tokens * group, dim), keys)
+        scores = scores_of(q_ref[:, place(step), :].reshape(tokens * group, dim), keys)
         return scores + bias - jnp.concatenate([level_ref[step]] * (shared_keys // dim), 1)
 
     def weighted(step, weights):
@@ -185,7 +185,7 @@
 
     def write(step, result):
         stage_ref[step] = result.astype(jnp.bfloat16).reshape(tokens, group, dim)
-        copy = pltpu.make_async_copy(stage_ref.at[step], out_hbm.at[:, places[step]], sems.at[step])
+        copy = pltpu.make_async_copy(stage_ref.at[step], out_hbm.at[:, place(step)], sems.at[step])
         copy.start()
         return copy
 
@@ -201,7 +201,8 @@
 
     @pl.when(too_high)
     def _():
-        for step in range(4):
+        @pl.loop(0, 4)
+        def _(step):
             scores = above_level(step)
             top = jnp.maximum(jnp.max(scores, axis=1, keepdims=True), 0.0)
             sums, totals = weighted(step, jnp.exp2(scores - top))

time: 20.2 us -> 20.2 us (level)
  no operation moved by 1% of the time
where the time goes in v9:
time: 20.2 us; the launch traced here: 20 us
  starting transfers between devices  8.61 us (43%)
  Pallas kernels  5.45 us (27%)
  waiting for transfers between devices  5.23 us (26%)
  between operations  0.7 us (3%)
    all_to_all x1, starting transfers between devices, per_device(): lax.all_to_all(sent.reshape(tp * stripes, 2 * page, dim), ('tp', 'pool'),...  4.92 us
    ppermute x4, starting transfers between devices, per_device(): lax.ppermute(array, 'tp', [(i, i ^ bit) for i in range(tp)])  3.69 us
    all_to_all x1, waiting for transfers between devices, per_device(): lax.all_to_all(sent.reshape(tp * stripes, 2 * page, dim), ('tp', 'pool'),...  3.43 us
    pallas_call x1, Pallas kernels, per_device(): pl.pallas_call(functools.partial(own_kernel, page=page), out_shape=[jax.S...  2.48 us
    ppermute x4, waiting for transfers between devices, per_device(): lax.ppermute(array, 'tp', [(i, i ^ bit) for i in range(tp)])  1.8 us
    pallas_call x1, Pallas kernels, per_device(): pl.pallas_call(functools.partial(select_kernel, page), out_shape=[jax.Sha...  1.54 us
    pallas_call x1, Pallas kernels, per_device(): pl.pallas_call(shared_kernel, out_shape=jax.ShapeDtypeStruct(queries.shap...  1.43 us
  transfers between devices with their start and end apart: 5, of which 4 were waited for; matrix products, arithmetic and copies ran while one was open for 0% of the time, Pallas kernels for 12%

profile of v9, /device:TPU:0, one launch (start us, length us, event | category | flops | bytes accessed | tf_op | source)
XLA Modules:
  0.0 20.0 jit_solution(5583228141977022612)
XLA Ops:
  0.0 1.5 %shard_map.82 = (bf16[4,8,16,128]{3,2,1,0:T(8,128)(2,1)}, bf16[768,128]{1,0:T(8,128)(2,1)S(1)}, f32[8,128]{1,0:T(8,128)S(1)}) custom-call(s32[13]{0:T(128)} %parent_hbm.1, s32[5]{0:T(128)} %pages_hbm.1, s32[5]{0:T(128)} %owner_hbm.1, bf16[80,128]{1,0:T(8,128)(2,1)} %bitcast.8, bf16[512,128]{1,0:T(8,128)(2,1)} %bitcast.6, bf16[256,128]{1,0:T(8,128)(2,1)} %bitcast.7), custom_call_target="tpu_custom_call" | custom-call | flops 49999998976 | bytes 1000000 | tf_op jit(solution)/shard_map/pallas_call | solution.py:226
  1.5 3.0 %collective-permute-start = (bf16[768,128]{1,0:T(8,128)(2,1)S(1)}, bf16[768,128]{1,0:T(8,128)(2,1)S(1)}, u32[]{:S(2)}, u32[]{:S(2)}) collective-permute-start(bf16[768,128]{1,0:T(8,128)(2,1)S(1)} %get-tuple-element.15.refs_0_), channel_id=1, source_target_pairs={{0,2},{1,3},{2,0},{3,1},{4,6},{5,7},{6,4},{7,5},{8,10},{9,11},{10,... | collective-permute-start | bytes 589832 | tf_op jit(solution)/shard_map/ppermute | solution.py:219
  4.6 4.9 %all-to-all-start = ((bf16[32,16,128]{2,1,0:T(8,128)(2,1)}), bf16[32,16,128]{2,1,0:T(8,128)(2,1)S(1)}, u32[]{:S(2)}, u32[]{:S(2)}) async-start(bf16[32,16,128]{2,1,0:T(8,128)(2,1)} %bitcast.3), calls=%async_computation | async-start | bytes 262144 | tf_op jit(solution)/shard_map/all_to_all | solution.py:248
  9.5 0.0 copy-start
  9.5 0.0 collective-permute-done.refs_1_
  9.5 0.3 %collective-permute-start.1 = (bf16[768,128]{1,0:T(8,128)(2,1)S(1)}, bf16[768,128]{1,0:T(8,128)(2,1)S(1)}, u32[]{:S(2)}, u32[]{:S(2)}) collective-permute-start(bf16[768,128]{1,0:T(8,128)(2,1)S(1)} %get-tuple-element.16.rest_0_), channel_id=1, source_target_pairs={{0,1},{1,0},{2,3},{3,2},{4,5},{5,4},{6,7},{7,6},{8,9},{9,8},{10,11... | collective-permute-start | bytes 589832 | tf_op jit(solution)/shard_map/ppermute | solution.py:219
  9.8 0.3 %collective-permute-start.2 = (bf16[768,128]{1,0:T(8,128)(2,1)S(1)}, bf16[768,128]{1,0:T(8,128)(2,1)S(1)}, u32[]{:S(2)}, u32[]{:S(2)}) collective-permute-start(bf16[768,128]{1,0:T(8,128)(2,1)S(1)} %get-tuple-element.17.rest_2_), channel_id=1, source_target_pairs={{0,1},{1,0},{2,3},{3,2},{4,5},{5,4},{6,7},{7,6},{8,9},{9,8},{10,11... | collective-permute-start | bytes 589832 | tf_op jit(solution)/shard_map/ppermute | solution.py:219
  10.7 0.3 %collective-permute-done.1.rest_1_ = bf16[768,128]{1,0:T(8,128)(2,1)S(1)} collective-permute-done((bf16[768,128]{1,0:T(8,128)(2,1)S(1)}, bf16[768,128]{1,0:T(8,128)(2,1)S(1)}, u32[]{:S(2)}, u32[]{:S(2)}) %collective-permute-start.1) | collective-permute-done | bytes 196640 | tf_op jit(solution)/shard_map/ppermute | solution.py:219
  11.0 0.3 %collective-permute-done.2.rest_3_ = bf16[768,128]{1,0:T(8,128)(2,1)S(1)} collective-permute-done((bf16[768,128]{1,0:T(8,128)(2,1)S(1)}, bf16[768,128]{1,0:T(8,128)(2,1)S(1)}, u32[]{:S(2)}, u32[]{:S(2)}) %collective-permute-start.2) | collective-permute-done | bytes 196640 | tf_op jit(solution)/shard_map/ppermute | solution.py:219
  11.3 0.0 copy-done
  11.3 2.5 %shard_map.84 = (f32[4,512,128]{2,1,0:T(8,128)S(1)}, f32[4,512,128]{2,1,0:T(8,128)S(1)}) custom-call(s32[1]{0:T(128)S(6)} %copy.17.leaf_len_ref, bf16[32,64,128]{2,1,0:T(8,128)(2,1)S(1)} %copy-done, bf16[768,128]{1,0:T(8,128)(2,1)S(1)} %get-tuple-element.16.rest_0_, bf16[768,128]{1,0:T(8,128)(2,1)S(1)} %collective-permute-done.1.rest_1_, ...), custom_call_target="tpu_custom_call" | custom-call | flops 1000000 | bytes 100000 | tf_op jit(solution)/shard_map/pallas_call | solution.py:255
  13.8 3.4 %all-to-all-done = bf16[32,16,128]{2,1,0:T(8,128)(2,1)S(1)} async-done(((bf16[32,16,128]{2,1,0:T(8,128)(2,1)}), bf16[32,16,128]{2,1,0:T(8,128)(2,1)S(1)}, u32[]{:S(2)}, u32[]{:S(2)}) %all-to-all-start) | async-done | bytes 131104 | tf_op jit(solution)/shard_map/all_to_all | solution.py:248
  17.2 0.1 collective-permute-start.3
  17.3 1.2 %collective-permute-done.3.theirs_ref = bf16[4,8,16,128]{3,2,1,0:T(8,128)(2,1)S(1)} collective-permute-done((bf16[4,8,16,128]{3,2,1,0:T(8,128)(2,1)S(1)}, bf16[4,8,16,128]{3,2,1,0:T(8,128)(2,1)S(1)}, u32[]{:S(2)}, u32[]{:S(2)}) %collective-permute-start.3) | collective-permute-done | bytes 131104 | tf_op jit(solution)/shard_map/ppermute | solution.py:219
  18.6 1.4 %shard_map.86 = bf16[32,64,128]{2,1,0:T(8,128)(2,1)} custom-call(bf16[32,64,128]{2,1,0:T(8,128)(2,1)S(1)} %copy-done, f32[8,128]{1,0:T(8,128)S(1)} %get-tuple-element.14.bias_ref, f32[4,512,128]{2,1,0:T(8,128)S(1)} %get-tuple-element.18.other_ref, f32[4,512,128]{2,1,0:T(8,128)S(1)} %get-tuple-element.21.level_ref, ...), custom_call_target="tpu_custom_call" | custom-call | tf_op jit(solution)/shard_map/pallas_call | solution.py:267
  (2 shorter events, 0.0 us)
Async XLA Ops:
  1.5 7.9 %collective-permute-start = (bf16[768,128]{1,0:T(8,128)(2,1)S(1)}, bf16[768,128]{1,0:T(8,128)(2,1)S(1)}, u32[]{:S(2)}, u32[]{:S(2)}) collective-permute-start(bf16[768,128]{1,0:T(8,128)(2,1)S(1)} %get-tuple-element.15.refs_0_), channel_id=1, source_target_pairs={{0,2},{1,3},{2,0},{3,1},{4,6},{5,7},{6,4},{7,5},{8,10},{9,11},{10,... | collective-permute-start | bytes 589832 | tf_op jit(solution)/shard_map/ppermute | solution.py:219
  4.6 12.7 %all-to-all-start = ((bf16[32,16,128]{2,1,0:T(8,128)(2,1)}), bf16[32,16,128]{2,1,0:T(8,128)(2,1)S(1)}, u32[]{:S(2)}, u32[]{:S(2)}) async-start(bf16[32,16,128]{2,1,0:T(8,128)(2,1)} %bitcast.3), calls=%async_computation | async-start | bytes 262144 | tf_op jit(solution)/shard_map/all_to_all | solution.py:248
  9.5 1.8 %copy-start = (bf16[32,64,128]{2,1,0:T(8,128)(2,1)S(1)}, bf16[32,64,128]{2,1,0:T(8,128)(2,1)}, u32[]{:S(2)}) copy-start(bf16[32,64,128]{2,1,0:T(8,128)(2,1)} %q_ref.3) | copy-start | bytes 1572868
  9.5 1.5 %collective-permute-start.1 = (bf16[768,128]{1,0:T(8,128)(2,1)S(1)}, bf16[768,128]{1,0:T(8,128)(2,1)S(1)}, u32[]{:S(2)}, u32[]{:S(2)}) collective-permute-start(bf16[768,128]{1,0:T(8,128)(2,1)S(1)} %get-tuple-element.16.rest_0_), channel_id=1, source_target_pairs={{0,1},{1,0},{2,3},{3,2},{4,5},{5,4},{6,7},{7,6},{8,9},{9,8},{10,11... | collective-permute-start | bytes 589832 | tf_op jit(solution)/shard_map/ppermute | solution.py:219
  9.8 1.5 %collective-permute-start.2 = (bf16[768,128]{1,0:T(8,128)(2,1)S(1)}, bf16[768,128]{1,0:T(8,128)(2,1)S(1)}, u32[]{:S(2)}, u32[]{:S(2)}) collective-permute-start(bf16[768,128]{1,0:T(8,128)(2,1)S(1)} %get-tuple-element.17.rest_2_), channel_id=1, source_target_pairs={{0,1},{1,0},{2,3},{3,2},{4,5},{5,4},{6,7},{7,6},{8,9},{9,8},{10,11... | collective-permute-start | bytes 589832 | tf_op jit(solution)/shard_map/ppermute | solution.py:219
  17.2 1.3 %collective-permute-start.3 = (bf16[4,8,16,128]{3,2,1,0:T(8,128)(2,1)S(1)}, bf16[4,8,16,128]{3,2,1,0:T(8,128)(2,1)S(1)}, u32[]{:S(2)}, u32[]{:S(2)}) collective-permute-start(bf16[4,8,16,128]{3,2,1,0:T(8,128)(2,1)S(1)} %get-tuple-element.22.mine_ref), channel_id=1, source_target_pairs={{0,1},{1,0},{2,3},{3,2},{4,5},{5,4},{6,7},{7,6},{8,9},{9,8},{10,11... | collective-permute-start | bytes 393224 | tf_op jit(solution)/shard_map/ppermute | solution.py:219

commit v10 on v9

--- a/solution.py
+++ b/solution.py
@@ -51,16 +51,14 @@
         mid = parent_ref[node_count + request] * (2 * page)
         for kind in range(2):
             chosen = rows_ref[pl.ds(mid + kind, page, stride=2)]
-            block_ref[kind, request] = jnp.concatenate([root[kind], chosen], 0).astype(jnp.bfloat16)
+            block = jnp.concatenate([root[kind], chosen], 0).astype(jnp.bfloat16)
+            for copy in range(kind, copies, 2):
+                block_ref[copy, request] = block
         return carry
 
     lax.fori_loop(0, requests, one, 0, unroll=requests <= 8)
-    sends = [
-        pltpu.make_async_copy(block_ref.at[copy % 2], out_hbm.at[copy], sems.at[len(pairs) + copy])
-        for copy in range(copies)
-    ]
-    for send in sends:
-        send.start()
+    send = pltpu.make_async_copy(block_ref, out_hbm, sems.at[len(pairs)])
+    send.start()
 
     fetches[2].wait()
     fetches[3].wait()
@@ -71,7 +69,7 @@
     offset = jnp.where(offset < 0, offset + requests, offset)
     used = offset < jnp.where(is_mid, pages_ref[mid], pages_ref[0])
     bias_ref[...] = jnp.where(used, 0.0, MASKED)
-    for copy in fetches[4:] + sends:
+    for copy in fetches[4:] + [send]:
         copy.wait()
 
 
@@ -238,8 +236,8 @@
             pltpu.SMEM(node_owner.shape, jnp.int32),
             pltpu.VMEM(pool_rows.shape, jnp.bfloat16),
             pltpu.VMEM(pool_rows.shape, jnp.float32),
-            pltpu.VMEM((2, stripes, 2 * page, dim), jnp.bfloat16),
-            pltpu.SemaphoreType.DMA((6 + tp,)),
+            pltpu.VMEM((tp, stripes, 2 * page, dim), jnp.bfloat16),
+            pltpu.SemaphoreType.DMA((7,)),
         ],
         compiler_params=pltpu.CompilerParams(vmem_limit_bytes=16 * 2**20),
         cost_estimate=LONG,

time: 20.2 us -> 20.2 us (level)
  no operation moved by 1% of the time
where the time goes in v10:
time: 20.2 us; the launch traced here: 20 us
  starting transfers between devices  8.61 us (43%)
  Pallas kernels  5.43 us (27%)
  waiting for transfers between devices  5.23 us (26%)
  between operations  0.7 us (3%)
    all_to_all x1, starting transfers between devices, per_device(): lax.all_to_all(sent.reshape(tp * stripes, 2 * page, dim), ('tp', 'pool'),...  4.92 us
    ppermute x4, starting transfers between devices, per_device(): lax.ppermute(array, 'tp', [(i, i ^ bit) for i in range(tp)])  3.69 us
    all_to_all x1, waiting for transfers between devices, per_device(): lax.all_to_all(sent.reshape(tp * stripes, 2 * page, dim), ('tp', 'pool'),...  3.43 us
    pallas_call x1, Pallas kernels, per_device(): pl.pallas_call(functools.partial(own_kernel, page=page), out_shape=[jax.S...  2.48 us
    ppermute x4, waiting for transfers between devices, per_device(): lax.ppermute(array, 'tp', [(i, i ^ bit) for i in range(tp)])  1.8 us
    pallas_call x1, Pallas kernels, per_device(): pl.pallas_call(functools.partial(select_kernel, page), out_shape=[jax.Sha...  1.52 us
    pallas_call x1, Pallas kernels, per_device(): pl.pallas_call(shared_kernel, out_shape=jax.ShapeDtypeStruct(queries.shap...  1.43 us
  transfers between devices with their start and end apart: 5, of which 4 were waited for; matrix products, arithmetic and copies ran while one was open for 0% of the time, Pallas kernels for 12%

profile of v10, /device:TPU:0, one launch (start us, length us, event | category | flops | bytes accessed | tf_op | source)
XLA Modules:
  0.0 20.0 jit_solution(9212044203532045788)
XLA Ops:
  0.0 1.5 %shard_map.82 = (bf16[4,8,16,128]{3,2,1,0:T(8,128)(2,1)}, bf16[768,128]{1,0:T(8,128)(2,1)S(1)}, f32[8,128]{1,0:T(8,128)S(1)}) custom-call(s32[13]{0:T(128)} %parent_hbm.1, s32[5]{0:T(128)} %pages_hbm.1, s32[5]{0:T(128)} %owner_hbm.1, bf16[80,128]{1,0:T(8,128)(2,1)} %bitcast.8, bf16[512,128]{1,0:T(8,128)(2,1)} %bitcast.6, bf16[256,128]{1,0:T(8,128)(2,1)} %bitcast.7), custom_call_target="tpu_custom_call" | custom-call | flops 49999998976 | bytes 1000000 | tf_op jit(solution)/shard_map/pallas_call | solution.py:224
  1.5 3.0 %collective-permute-start = (bf16[768,128]{1,0:T(8,128)(2,1)S(1)}, bf16[768,128]{1,0:T(8,128)(2,1)S(1)}, u32[]{:S(2)}, u32[]{:S(2)}) collective-permute-start(bf16[768,128]{1,0:T(8,128)(2,1)S(1)} %get-tuple-element.15.refs_0_), channel_id=1, source_target_pairs={{0,2},{1,3},{2,0},{3,1},{4,6},{5,7},{6,4},{7,5},{8,10},{9,11},{10,... | collective-permute-start | bytes 589832 | tf_op jit(solution)/shard_map/ppermute | solution.py:217
  4.5 4.9 %all-to-all-start = ((bf16[32,16,128]{2,1,0:T(8,128)(2,1)}), bf16[32,16,128]{2,1,0:T(8,128)(2,1)S(1)}, u32[]{:S(2)}, u32[]{:S(2)}) async-start(bf16[32,16,128]{2,1,0:T(8,128)(2,1)} %bitcast.3), calls=%async_computation | async-start | bytes 262144 | tf_op jit(solution)/shard_map/all_to_all | solution.py:246
  9.5 0.0 copy-start
  9.5 0.0 collective-permute-done.refs_1_
  9.5 0.3 %collective-permute-start.1 = (bf16[768,128]{1,0:T(8,128)(2,1)S(1)}, bf16[768,128]{1,0:T(8,128)(2,1)S(1)}, u32[]{:S(2)}, u32[]{:S(2)}) collective-permute-start(bf16[768,128]{1,0:T(8,128)(2,1)S(1)} %get-tuple-element.16.rest_0_), channel_id=1, source_target_pairs={{0,1},{1,0},{2,3},{3,2},{4,5},{5,4},{6,7},{7,6},{8,9},{9,8},{10,11... | collective-permute-start | bytes 589832 | tf_op jit(solution)/shard_map/ppermute | solution.py:217
  9.8 0.3 %collective-permute-start.2 = (bf16[768,128]{1,0:T(8,128)(2,1)S(1)}, bf16[768,128]{1,0:T(8,128)(2,1)S(1)}, u32[]{:S(2)}, u32[]{:S(2)}) collective-permute-start(bf16[768,128]{1,0:T(8,128)(2,1)S(1)} %get-tuple-element.17.rest_2_), channel_id=1, source_target_pairs={{0,1},{1,0},{2,3},{3,2},{4,5},{5,4},{6,7},{7,6},{8,9},{9,8},{10,11... | collective-permute-start | bytes 589832 | tf_op jit(solution)/shard_map/ppermute | solution.py:217
  10.7 0.3 %collective-permute-done.1.rest_1_ = bf16[768,128]{1,0:T(8,128)(2,1)S(1)} collective-permute-done((bf16[768,128]{1,0:T(8,128)(2,1)S(1)}, bf16[768,128]{1,0:T(8,128)(2,1)S(1)}, u32[]{:S(2)}, u32[]{:S(2)}) %collective-permute-start.1) | collective-permute-done | bytes 196640 | tf_op jit(solution)/shard_map/ppermute | solution.py:217
  11.0 0.3 %collective-permute-done.2.rest_3_ = bf16[768,128]{1,0:T(8,128)(2,1)S(1)} collective-permute-done((bf16[768,128]{1,0:T(8,128)(2,1)S(1)}, bf16[768,128]{1,0:T(8,128)(2,1)S(1)}, u32[]{:S(2)}, u32[]{:S(2)}) %collective-permute-start.2) | collective-permute-done | bytes 196640 | tf_op jit(solution)/shard_map/ppermute | solution.py:217
  11.3 0.0 copy-done
  11.3 2.5 %shard_map.84 = (f32[4,512,128]{2,1,0:T(8,128)S(1)}, f32[4,512,128]{2,1,0:T(8,128)S(1)}) custom-call(s32[1]{0:T(128)S(6)} %copy.17.leaf_len_ref, bf16[32,64,128]{2,1,0:T(8,128)(2,1)S(1)} %copy-done, bf16[768,128]{1,0:T(8,128)(2,1)S(1)} %get-tuple-element.16.rest_0_, bf16[768,128]{1,0:T(8,128)(2,1)S(1)} %collective-permute-done.1.rest_1_, ...), custom_call_target="tpu_custom_call" | custom-call | flops 1000000 | bytes 100000 | tf_op jit(solution)/shard_map/pallas_call | solution.py:253
  13.8 3.4 %all-to-all-done = bf16[32,16,128]{2,1,0:T(8,128)(2,1)S(1)} async-done(((bf16[32,16,128]{2,1,0:T(8,128)(2,1)}), bf16[32,16,128]{2,1,0:T(8,128)(2,1)S(1)}, u32[]{:S(2)}, u32[]{:S(2)}) %all-to-all-start) | async-done | bytes 131104 | tf_op jit(solution)/shard_map/all_to_all | solution.py:246
  17.2 0.1 collective-permute-start.3
  17.3 1.2 %collective-permute-done.3.theirs_ref = bf16[4,8,16,128]{3,2,1,0:T(8,128)(2,1)S(1)} collective-permute-done((bf16[4,8,16,128]{3,2,1,0:T(8,128)(2,1)S(1)}, bf16[4,8,16,128]{3,2,1,0:T(8,128)(2,1)S(1)}, u32[]{:S(2)}, u32[]{:S(2)}) %collective-permute-start.3) | collective-permute-done | bytes 131104 | tf_op jit(solution)/shard_map/ppermute | solution.py:217
  18.6 1.4 %shard_map.86 = bf16[32,64,128]{2,1,0:T(8,128)(2,1)} custom-call(bf16[32,64,128]{2,1,0:T(8,128)(2,1)S(1)} %copy-done, f32[8,128]{1,0:T(8,128)S(1)} %get-tuple-element.14.bias_ref, f32[4,512,128]{2,1,0:T(8,128)S(1)} %get-tuple-element.18.other_ref, f32[4,512,128]{2,1,0:T(8,128)S(1)} %get-tuple-element.21.level_ref, ...), custom_call_target="tpu_custom_call" | custom-call | tf_op jit(solution)/shard_map/pallas_call | solution.py:265
  (2 shorter events, 0.0 us)
Async XLA Ops:
  1.5 7.9 %collective-permute-start = (bf16[768,128]{1,0:T(8,128)(2,1)S(1)}, bf16[768,128]{1,0:T(8,128)(2,1)S(1)}, u32[]{:S(2)}, u32[]{:S(2)}) collective-permute-start(bf16[768,128]{1,0:T(8,128)(2,1)S(1)} %get-tuple-element.15.refs_0_), channel_id=1, source_target_pairs={{0,2},{1,3},{2,0},{3,1},{4,6},{5,7},{6,4},{7,5},{8,10},{9,11},{10,... | collective-permute-start | bytes 589832 | tf_op jit(solution)/shard_map/ppermute | solution.py:217
  4.5 12.7 %all-to-all-start = ((bf16[32,16,128]{2,1,0:T(8,128)(2,1)}), bf16[32,16,128]{2,1,0:T(8,128)(2,1)S(1)}, u32[]{:S(2)}, u32[]{:S(2)}) async-start(bf16[32,16,128]{2,1,0:T(8,128)(2,1)} %bitcast.3), calls=%async_computation | async-start | bytes 262144 | tf_op jit(solution)/shard_map/all_to_all | solution.py:246
  9.5 1.8 %copy-start = (bf16[32,64,128]{2,1,0:T(8,128)(2,1)S(1)}, bf16[32,64,128]{2,1,0:T(8,128)(2,1)}, u32[]{:S(2)}) copy-start(bf16[32,64,128]{2,1,0:T(8,128)(2,1)} %q_ref.3) | copy-start | bytes 1572868
  9.5 1.5 %collective-permute-start.1 = (bf16[768,128]{1,0:T(8,128)(2,1)S(1)}, bf16[768,128]{1,0:T(8,128)(2,1)S(1)}, u32[]{:S(2)}, u32[]{:S(2)}) collective-permute-start(bf16[768,128]{1,0:T(8,128)(2,1)S(1)} %get-tuple-element.16.rest_0_), channel_id=1, source_target_pairs={{0,1},{1,0},{2,3},{3,2},{4,5},{5,4},{6,7},{7,6},{8,9},{9,8},{10,11... | collective-permute-start | bytes 589832 | tf_op jit(solution)/shard_map/ppermute | solution.py:217
  9.8 1.5 %collective-permute-start.2 = (bf16[768,128]{1,0:T(8,128)(2,1)S(1)}, bf16[768,128]{1,0:T(8,128)(2,1)S(1)}, u32[]{:S(2)}, u32[]{:S(2)}) collective-permute-start(bf16[768,128]{1,0:T(8,128)(2,1)S(1)} %get-tuple-element.17.rest_2_), channel_id=1, source_target_pairs={{0,1},{1,0},{2,3},{3,2},{4,5},{5,4},{6,7},{7,6},{8,9},{9,8},{10,11... | collective-permute-start | bytes 589832 | tf_op jit(solution)/shard_map/ppermute | solution.py:217
  17.2 1.3 %collective-permute-start.3 = (bf16[4,8,16,128]{3,2,1,0:T(8,128)(2,1)S(1)}, bf16[4,8,16,128]{3,2,1,0:T(8,128)(2,1)S(1)}, u32[]{:S(2)}, u32[]{:S(2)}) collective-permute-start(bf16[4,8,16,128]{3,2,1,0:T(8,128)(2,1)S(1)} %get-tuple-element.22.mine_ref), channel_id=1, source_target_pairs={{0,1},{1,0},{2,3},{3,2},{4,5},{5,4},{6,7},{7,6},{8,9},{9,8},{10,11... | collective-permute-start | bytes 393224 | tf_op jit(solution)/shard_map/ppermute | solution.py:217

commit v11 on v10

--- a/solution.py
+++ b/solution.py
@@ -49,11 +49,10 @@
 
     def one(request, carry):
         mid = parent_ref[node_count + request] * (2 * page)
-        for kind in range(2):
-            chosen = rows_ref[pl.ds(mid + kind, page, stride=2)]
-            block = jnp.concatenate([root[kind], chosen], 0).astype(jnp.bfloat16)
-            for copy in range(kind, copies, 2):
-                block_ref[copy, request] = block
+        chosen = [rows_ref[pl.ds(mid + kind, page, stride=2)] for kind in range(2)]
+        for copy in range(copies):
+            block = jnp.concatenate(root if copy % 2 == 0 else chosen, 0)
+            block_ref[copy, request] = block.astype(jnp.bfloat16)
         return carry
 
     lax.fori_loop(0, requests, one, 0, unroll=requests <= 8)
@@ -63,9 +62,10 @@
     fetches[2].wait()
     fetches[3].wait()
     mid = parent_ref[node_count + lax.axis_index("pool")]
-    key = lax.broadcasted_iota(jnp.int32, bias_ref.shape, 1)
-    stripe, is_mid = key // (2 * page), (key % (2 * page)) >= page
-    offset = stripe - jnp.where(is_mid, owner_ref[mid], owner_ref[0])
+    half = lax.broadcasted_iota(jnp.int32, bias_ref.shape, 0) // 8
+    is_mid = (lax.axis_index("tp") + half) % 2 == 1
+    key = lax.broadcasted_iota(jnp.int32, bias_ref.shape, 1) % (requests * page)
+    offset = key // page - jnp.where(is_mid, owner_ref[mid], owner_ref[0])
     offset = jnp.where(offset < 0, offset + requests, offset)
     used = offset < jnp.where(is_mid, pages_ref[mid], pages_ref[0])
     bias_ref[...] = jnp.where(used, 0.0, MASKED)
@@ -161,51 +161,110 @@
         level_ref[step] = jnp.log2(totals) + top
 
 
-def shared_kernel(q_ref, bias_ref, other_ref, level_ref, mine_ref, theirs_ref, out_hbm, stage_ref, sems):
+PAIRS = ((0, 1), (2, 3))
+
+
+def blocks(a, b):
+    zero = jnp.zeros_like(a)
+    return jnp.concatenate([jnp.concatenate([a, zero], 1), jnp.concatenate([zero, b], 1)], 0)
+
+
+def spread(a, b, width):
+    lanes = a.shape[1]
+    if width == lanes:
+        return jnp.where(lax.broadcasted_iota(jnp.int32, a.shape, 1) < width // 2, a, b)
+    return jnp.concatenate([a] * (width // 2 // lanes) + [b] * (width // 2 // lanes), 1)
+
+
+def place_of(step, group):
+    return pl.ds(pl.multiple_of((lax.axis_index("tp") ^ step) * group, group), group)
+
+
+def kinds_of(pool_ref, step):
+    rows = pool_ref[lax.axis_index("tp") ^ step].astype(jnp.float32)
+    page, dim = rows.shape[1] // 2, rows.shape[2]
+    return [rows[:, i * page : (i + 1) * page].reshape(-1, dim).astype(jnp.bfloat16) for i in range(2)]
+
+
+def above_level(pair, q_ref, bias, level_ref, pool_ref):
     tokens, q_heads, dim = q_ref.shape
     group = q_heads // 4
-    shared_keys = bias_ref.shape[1]
-    rank = lax.axis_index("tp")
-    has_keys = rank % 2 == 0
-    bias = bias_ref[0:1]
-    place = lambda step: pl.ds(pl.multiple_of((rank ^ step) * group, group), group)
-
-    def above_level(step):
-        head = rank ^ step
-        keys = jnp.where(has_keys, mine_ref[head], theirs_ref[head]).reshape(shared_keys, dim)
-        scores = scores_of(q_ref[:, place(step), :].reshape(tokens * group, dim), keys)
-        return scores + bias - jnp.concatenate([level_ref[step]] * (shared_keys // dim), 1)
-
-    def weighted(step, weights):
-        head = rank ^ step
-        values = jnp.where(has_keys, theirs_ref[head], mine_ref[head]).reshape(shared_keys, dim)
-        return weigh(weights, values)
-
-    def write(step, result):
-        stage_ref[step] = result.astype(jnp.bfloat16).reshape(tokens, group, dim)
-        copy = pltpu.make_async_copy(stage_ref.at[step], out_hbm.at[:, place(step)], sems.at[step])
-        copy.start()
-        return copy
-
-    scores = [above_level(step) for step in range(4)]
+    rows = [q_ref[:, place_of(step, group), :].reshape(tokens * group, dim) for step in pair]
+    keys = blocks(*[kinds_of(pool_ref, step)[0] for step in pair])
+    scores = scores_of(jnp.concatenate(rows, 1), keys)
+    return scores + bias - spread(level_ref[pair[0]], level_ref[pair[1]], scores.shape[1])
+
+
+def weigh_pair(pair, weights, pool_ref):
+    values = [kinds_of(pool_ref, step)[1] for step in pair]
+    ones = jnp.ones_like(values[0])
+    return dot(weights, blocks(*values)), dot(weights, blocks(ones, ones))
+
+
+def side_by_side(ref, pair):
+    return jnp.concatenate([ref[step] for step in pair], 1)
+
+
+def first_half_kernel(q_ref, bias_ref, other_ref, level_ref, pool_ref, sums_ref, totals_ref, peak_ref):
+    peak = None
+    scores = [above_level(pair, q_ref, bias_ref[0:1], level_ref, pool_ref) for pair in PAIRS]
+    for i, pair in enumerate(PAIRS):
+        weights = jnp.exp2(scores[i]).astype(jnp.bfloat16)
+        peak = weights if peak is None else jnp.maximum(peak, weights)
+        sums, totals = weigh_pair(pair, weights, pool_ref)
+        sums_ref[i] = sums + side_by_side(other_ref, pair)
+        totals_ref[i] = totals + 1.0
+    peak = jnp.max(peak.astype(jnp.float32), axis=0, keepdims=True)
+    peak_ref[...] = jnp.broadcast_to(peak, peak_ref.shape)
+
+
+def second_half_kernel(
+    q_ref, bias_ref, other_ref, level_ref, mine_ref, sums_ref, totals_ref, peak_ref, theirs_ref,
+    out_hbm, stage_ref, sems,
+):
+    tokens, q_heads, dim = q_ref.shape
+    group = q_heads // 4
+
+    def write(pair, result):
+        copies = []
+        for i, step in enumerate(pair):
+            part = result[:, i * dim : (i + 1) * dim]
+            stage_ref[step] = part.astype(jnp.bfloat16).reshape(tokens, group, dim)
+            target = out_hbm.at[:, place_of(step, group)]
+            copies.append(pltpu.make_async_copy(stage_ref.at[step], target, sems.at[step]))
+            copies[-1].start()
+        return copies
+
+    scores = [above_level(pair, q_ref, bias_ref[8:9], level_ref, theirs_ref) for pair in PAIRS]
     writes, weights = [], []
-    for step in range(4):
-        weights.append(jnp.exp2(scores[step]).astype(jnp.bfloat16))
-        sums, totals = weighted(step, weights[-1])
-        writes.append(write(step, over(sums + other_ref[step], totals + 1.0)))
-    too_high = jnp.max(functools.reduce(jnp.maximum, weights).astype(jnp.float32)) > 2.0**100
+    for i, pair in enumerate(PAIRS):
+        weights.append(jnp.exp2(scores[i]).astype(jnp.bfloat16))
+        sums, totals = weigh_pair(pair, weights[-1], theirs_ref)
+        writes += write(pair, over(sums + sums_ref[i], totals + totals_ref[i]))
+    peak = jnp.maximum(jnp.max(functools.reduce(jnp.maximum, weights).astype(jnp.float32)), jnp.max(peak_ref[...]))
     for copy in writes:
         copy.wait()
 
-    @pl.when(too_high)
+    @pl.when(peak > 2.0**100)
     def _():
-        @pl.loop(0, 4)
-        def _(step):
-            scores = above_level(step)
-            top = jnp.maximum(jnp.max(scores, axis=1, keepdims=True), 0.0)
-            sums, totals = weighted(step, jnp.exp2(scores - top))
-            other = jnp.exp2(-top)
-            write(step, over(sums + other_ref[step] * other, totals + other)).wait()
+        for pair in PAIRS:
+            mine = above_level(pair, q_ref, bias_ref[0:1], level_ref, mine_ref)
+            theirs = above_level(pair, q_ref, bias_ref[8:9], level_ref, theirs_ref)
+            both = jnp.maximum(mine, theirs)
+            half = both.shape[1] // 2
+            first = lax.broadcasted_iota(jnp.int32, both.shape, 1) < half
+            tops = [
+                jnp.maximum(jnp.max(jnp.where(first == (i == 0), both, 0.0), axis=1, keepdims=True), 0.0)
+                for i in range(2)
+            ]
+            tops = [jnp.broadcast_to(top, (tokens * group, dim)) for top in tops]
+            top = spread(*tops, both.shape[1])
+            rest = jnp.exp2(-jnp.concatenate(tops, 1))
+            sums, totals = weigh_pair(pair, jnp.exp2(mine - top).astype(jnp.bfloat16), mine_ref)
+            more, added = weigh_pair(pair, jnp.exp2(theirs - top).astype(jnp.bfloat16), theirs_ref)
+            sums = sums + more + side_by_side(other_ref, pair) * rest
+            for copy in write(pair, over(sums, totals + added + rest)):
+                copy.wait()
 
 
 def per_device(queries, fresh, pool, leaf, parent, node_pages, node_owner, leaf_len):
@@ -226,7 +285,7 @@
         out_shape=[
             jax.ShapeDtypeStruct((tp, stripes, 2 * page, dim), jnp.bfloat16),
             jax.ShapeDtypeStruct((leaf_rows.shape[0] + fresh_rows.shape[0], dim), jnp.bfloat16),
-            jax.ShapeDtypeStruct((8, stripes * 2 * page), jnp.float32),
+            jax.ShapeDtypeStruct((16, stripes * 2 * page), jnp.float32),
         ],
         in_specs=[hbm] * 6,
         out_specs=[hbm, vmem, vmem],
@@ -262,17 +321,27 @@
     )(leaf_len, queries, local_0, local_1, local_2, local_3)
     mine, level = hand_over(SHORT, mine, level)
     theirs = swap(mine, 1)
+    limit = pltpu.CompilerParams(vmem_limit_bytes=(24 if stripes <= 8 else 48) * 2**20)
+    sums, totals, peak = pl.pallas_call(
+        first_half_kernel,
+        out_shape=[jax.ShapeDtypeStruct((len(PAIRS), rows, 2 * dim), jnp.float32)] * 2
+        + [jax.ShapeDtypeStruct((8, bias.shape[1]), jnp.float32)],
+        in_specs=[vmem] * 5,
+        out_specs=[vmem] * 3,
+        compiler_params=limit,
+        cost_estimate=SHORT,
+    )(queries, bias, other, level, mine)
     return pl.pallas_call(
-        shared_kernel,
+        second_half_kernel,
         out_shape=jax.ShapeDtypeStruct(queries.shape, jnp.bfloat16),
-        in_specs=[vmem] * 6,
+        in_specs=[vmem] * 9,
         out_specs=hbm,
         scratch_shapes=[
             pltpu.VMEM((tp, tokens, q_heads // tp, dim), jnp.bfloat16),
             pltpu.SemaphoreType.DMA((tp,)),
         ],
-        compiler_params=pltpu.CompilerParams(vmem_limit_bytes=(24 if stripes <= 8 else 48) * 2**20),
-    )(queries, bias, other, level, mine, theirs)
+        compiler_params=limit,
+    )(queries, bias, other, level, mine, sums, totals, peak, theirs)
 
 
 def solution(mesh):

time: 20.2 us -> 20.1 us (level)
  waiting for transfers between devices: 5.23 us -> 4.65 us
  Pallas kernels: 5.43 us -> 5.91 us
    ppermute x4, waiting for transfers between devices: 1.8 us -> 1.22 us  [per_device(): lax.ppermute(array, 'tp', [(i, i ^ bit) for i in range(tp)])]
    pallas_call x1 -> x2, Pallas kernels: 1.43 us -> 1.9 us  [the longest x1 1.34 us: per_device(): pl.pallas_call(second_half_kernel, out_shape=jax.ShapeDtypeStruct(queries...]
  transfers between devices with their start and end apart: 5 -> 5, of which waited for: 4 -> 4; matrix products, arithmetic and copies ran while one was open for 0% -> 0% of each run, Pallas kernels for 12% -> 15%
where the time goes in v11:
time: 20.1 us; the launch traced here: 19.9 us
  starting transfers between devices  8.61 us (43%)
  Pallas kernels  5.91 us (29%)
  waiting for transfers between devices  4.65 us (23%)
  between operations  0.71 us (4%)
    all_to_all x1, starting transfers between devices, per_device(): lax.all_to_all(sent.reshape(tp * stripes, 2 * page, dim), ('tp', 'pool'),...  4.92 us
    ppermute x4, starting transfers between devices, per_device(): lax.ppermute(array, 'tp', [(i, i ^ bit) for i in range(tp)])  3.69 us
    all_to_all x1, waiting for transfers between devices, per_device(): lax.all_to_all(sent.reshape(tp * stripes, 2 * page, dim), ('tp', 'pool'),...  3.43 us
    pallas_call x1, Pallas kernels, per_device(): pl.pallas_call(functools.partial(own_kernel, page=page), out_shape=[jax.S...  2.48 us
    pallas_call x1, Pallas kernels, per_device(): pl.pallas_call(functools.partial(select_kernel, page), out_shape=[jax.Sha...  1.52 us
    pallas_call x1, Pallas kernels, per_device(): pl.pallas_call(second_half_kernel, out_shape=jax.ShapeDtypeStruct(queries...  1.34 us
    ppermute x4, waiting for transfers between devices, per_device(): lax.ppermute(array, 'tp', [(i, i ^ bit) for i in range(tp)])  1.22 us
    pallas_call x1, Pallas kernels, per_device(): pl.pallas_call(first_half_kernel, out_shape=[jax.ShapeDtypeStruct((len(PA...  0.57 us
  transfers between devices with their start and end apart: 5, of which 4 were waited for; matrix products, arithmetic and copies ran while one was open for 0% of the time, Pallas kernels for 15%

profile of v11, /device:TPU:0, one launch (start us, length us, event | category | flops | bytes accessed | tf_op | source)
XLA Modules:
  0.0 19.9 jit_solution(9065362107499404102)
XLA Ops:
  0.0 1.5 %shard_map.82 = (bf16[4,8,16,128]{3,2,1,0:T(8,128)(2,1)}, bf16[768,128]{1,0:T(8,128)(2,1)S(1)}, f32[16,128]{1,0:T(8,128)S(1)}) custom-call(s32[13]{0:T(128)} %parent_hbm.1, s32[5]{0:T(128)} %pages_hbm.1, s32[5]{0:T(128)} %owner_hbm.1, bf16[80,128]{1,0:T(8,128)(2,1)} %bitcast.8, bf16[512,128]{1,0:T(8,128)(2,1)} %bitcast.6, bf16[256,128]{1,0:T(8,128)(2,1)} %bitcast.7), custom_call_target="tpu_custom_call" | custom-call | flops 49999998976 | bytes 1000000 | tf_op jit(solution)/shard_map/pallas_call | solution.py:283
  1.5 3.0 %collective-permute-start = (bf16[768,128]{1,0:T(8,128)(2,1)S(1)}, bf16[768,128]{1,0:T(8,128)(2,1)S(1)}, u32[]{:S(2)}, u32[]{:S(2)}) collective-permute-start(bf16[768,128]{1,0:T(8,128)(2,1)S(1)} %get-tuple-element.18.refs_0_), channel_id=1, source_target_pairs={{0,2},{1,3},{2,0},{3,1},{4,6},{5,7},{6,4},{7,5},{8,10},{9,11},{10,... | collective-permute-start | bytes 589832 | tf_op jit(solution)/shard_map/ppermute | solution.py:276
  4.5 4.9 %all-to-all-start = ((bf16[32,16,128]{2,1,0:T(8,128)(2,1)}), bf16[32,16,128]{2,1,0:T(8,128)(2,1)S(1)}, u32[]{:S(2)}, u32[]{:S(2)}) async-start(bf16[32,16,128]{2,1,0:T(8,128)(2,1)} %bitcast.3), calls=%async_computation | async-start | bytes 262144 | tf_op jit(solution)/shard_map/all_to_all | solution.py:305
  9.5 0.0 copy-start
  9.5 0.0 collective-permute-done.refs_1_
  9.5 0.3 %collective-permute-start.1 = (bf16[768,128]{1,0:T(8,128)(2,1)S(1)}, bf16[768,128]{1,0:T(8,128)(2,1)S(1)}, u32[]{:S(2)}, u32[]{:S(2)}) collective-permute-start(bf16[768,128]{1,0:T(8,128)(2,1)S(1)} %get-tuple-element.19.rest_0_), channel_id=1, source_target_pairs={{0,1},{1,0},{2,3},{3,2},{4,5},{5,4},{6,7},{7,6},{8,9},{9,8},{10,11... | collective-permute-start | bytes 589832 | tf_op jit(solution)/shard_map/ppermute | solution.py:276
  9.8 0.3 %collective-permute-start.2 = (bf16[768,128]{1,0:T(8,128)(2,1)S(1)}, bf16[768,128]{1,0:T(8,128)(2,1)S(1)}, u32[]{:S(2)}, u32[]{:S(2)}) collective-permute-start(bf16[768,128]{1,0:T(8,128)(2,1)S(1)} %get-tuple-element.20.rest_2_), channel_id=1, source_target_pairs={{0,1},{1,0},{2,3},{3,2},{4,5},{5,4},{6,7},{7,6},{8,9},{9,8},{10,11... | collective-permute-start | bytes 589832 | tf_op jit(solution)/shard_map/ppermute | solution.py:276
  10.7 0.3 %collective-permute-done.1.rest_1_ = bf16[768,128]{1,0:T(8,128)(2,1)S(1)} collective-permute-done((bf16[768,128]{1,0:T(8,128)(2,1)S(1)}, bf16[768,128]{1,0:T(8,128)(2,1)S(1)}, u32[]{:S(2)}, u32[]{:S(2)}) %collective-permute-start.1) | collective-permute-done | bytes 196640 | tf_op jit(solution)/shard_map/ppermute | solution.py:276
  11.0 0.3 %collective-permute-done.2.rest_3_ = bf16[768,128]{1,0:T(8,128)(2,1)S(1)} collective-permute-done((bf16[768,128]{1,0:T(8,128)(2,1)S(1)}, bf16[768,128]{1,0:T(8,128)(2,1)S(1)}, u32[]{:S(2)}, u32[]{:S(2)}) %collective-permute-start.2) | collective-permute-done | bytes 196640 | tf_op jit(solution)/shard_map/ppermute | solution.py:276
  11.3 0.0 copy-done
  11.3 2.5 %shard_map.84 = (f32[4,512,128]{2,1,0:T(8,128)S(1)}, f32[4,512,128]{2,1,0:T(8,128)S(1)}) custom-call(s32[1]{0:T(128)S(6)} %copy.17.leaf_len_ref, bf16[32,64,128]{2,1,0:T(8,128)(2,1)S(1)} %copy-done, bf16[768,128]{1,0:T(8,128)(2,1)S(1)} %get-tuple-element.19.rest_0_, bf16[768,128]{1,0:T(8,128)(2,1)S(1)} %collective-permute-done.1.rest_1_, ...), custom_call_target="tpu_custom_call" | custom-call | flops 1000000 | bytes 100000 | tf_op jit(solution)/shard_map/pallas_call | solution.py:312
  13.8 3.4 %all-to-all-done = bf16[32,16,128]{2,1,0:T(8,128)(2,1)S(1)} async-done(((bf16[32,16,128]{2,1,0:T(8,128)(2,1)}), bf16[32,16,128]{2,1,0:T(8,128)(2,1)S(1)}, u32[]{:S(2)}, u32[]{:S(2)}) %all-to-all-start) | async-done | bytes 131104 | tf_op jit(solution)/shard_map/all_to_all | solution.py:305
  17.2 0.1 collective-permute-start.3
  17.3 0.6 %shard_map.86 = (f32[2,512,256]{2,1,0:T(8,128)S(1)}, f32[2,512,256]{2,1,0:T(8,128)S(1)}, f32[8,128]{1,0:T(8,128)S(1)}) custom-call(bf16[32,64,128]{2,1,0:T(8,128)(2,1)S(1)} %copy-done, f32[16,128]{1,0:T(8,128)S(1)} %get-tuple-element.17.bias_ref, f32[4,512,128]{2,1,0:T(8,128)S(1)} %get-tuple-element.21.other_ref, ...), custom_call_target="tpu_custom_call" | custom-call | flops 1000000 | bytes 100000 | tf_op jit(solution)/shard_map/pallas_call | solution.py:325
  17.9 0.7 %collective-permute-done.3.theirs_ref = bf16[4,8,16,128]{3,2,1,0:T(8,128)(2,1)S(1)} collective-permute-done((bf16[4,8,16,128]{3,2,1,0:T(8,128)(2,1)S(1)}, bf16[4,8,16,128]{3,2,1,0:T(8,128)(2,1)S(1)}, u32[]{:S(2)}, u32[]{:S(2)}) %collective-permute-start.3) | collective-permute-done | bytes 131104 | tf_op jit(solution)/shard_map/ppermute | solution.py:276
  18.6 1.3 %shard_map.87 = bf16[32,64,128]{2,1,0:T(8,128)(2,1)} custom-call(bf16[32,64,128]{2,1,0:T(8,128)(2,1)S(1)} %copy-done, f32[16,128]{1,0:T(8,128)S(1)} %get-tuple-element.17.bias_ref, f32[4,512,128]{2,1,0:T(8,128)S(1)} %get-tuple-element.21.other_ref, f32[4,512,128]{2,1,0:T(8,128)S(1)} %get-tuple-element.24.level_ref, ...), custom_call_target="tpu_custom_call" | custom-call | tf_op jit(solution)/shard_map/pallas_call | solution.py:334
  (2 shorter events, 0.0 us)
Async XLA Ops:
  1.5 7.9 %collective-permute-start = (bf16[768,128]{1,0:T(8,128)(2,1)S(1)}, bf16[768,128]{1,0:T(8,128)(2,1)S(1)}, u32[]{:S(2)}, u32[]{:S(2)}) collective-permute-start(bf16[768,128]{1,0:T(8,128)(2,1)S(1)} %get-tuple-element.18.refs_0_), channel_id=1, source_target_pairs={{0,2},{1,3},{2,0},{3,1},{4,6},{5,7},{6,4},{7,5},{8,10},{9,11},{10,... | collective-permute-start | bytes 589832 | tf_op jit(solution)/shard_map/ppermute | solution.py:276
  4.5 12.7 %all-to-all-start = ((bf16[32,16,128]{2,1,0:T(8,128)(2,1)}), bf16[32,16,128]{2,1,0:T(8,128)(2,1)S(1)}, u32[]{:S(2)}, u32[]{:S(2)}) async-start(bf16[32,16,128]{2,1,0:T(8,128)(2,1)} %bitcast.3), calls=%async_computation | async-start | bytes 262144 | tf_op jit(solution)/shard_map/all_to_all | solution.py:305
  9.5 1.8 %copy-start = (bf16[32,64,128]{2,1,0:T(8,128)(2,1)S(1)}, bf16[32,64,128]{2,1,0:T(8,128)(2,1)}, u32[]{:S(2)}) copy-start(bf16[32,64,128]{2,1,0:T(8,128)(2,1)} %q_ref.5) | copy-start | bytes 1572868
  9.5 1.5 %collective-permute-start.1 = (bf16[768,128]{1,0:T(8,128)(2,1)S(1)}, bf16[768,128]{1,0:T(8,128)(2,1)S(1)}, u32[]{:S(2)}, u32[]{:S(2)}) collective-permute-start(bf16[768,128]{1,0:T(8,128)(2,1)S(1)} %get-tuple-element.19.rest_0_), channel_id=1, source_target_pairs={{0,1},{1,0},{2,3},{3,2},{4,5},{5,4},{6,7},{7,6},{8,9},{9,8},{10,11... | collective-permute-start | bytes 589832 | tf_op jit(solution)/shard_map/ppermute | solution.py:276
  9.8 1.5 %collective-permute-start.2 = (bf16[768,128]{1,0:T(8,128)(2,1)S(1)}, bf16[768,128]{1,0:T(8,128)(2,1)S(1)}, u32[]{:S(2)}, u32[]{:S(2)}) collective-permute-start(bf16[768,128]{1,0:T(8,128)(2,1)S(1)} %get-tuple-element.20.rest_2_), channel_id=1, source_target_pairs={{0,1},{1,0},{2,3},{3,2},{4,5},{5,4},{6,7},{7,6},{8,9},{9,8},{10,11... | collective-permute-start | bytes 589832 | tf_op jit(solution)/shard_map/ppermute | solution.py:276
  17.2 1.3 %collective-permute-start.3 = (bf16[4,8,16,128]{3,2,1,0:T(8,128)(2,1)S(1)}, bf16[4,8,16,128]{3,2,1,0:T(8,128)(2,1)S(1)}, u32[]{:S(2)}, u32[]{:S(2)}) collective-permute-start(bf16[4,8,16,128]{3,2,1,0:T(8,128)(2,1)S(1)} %get-tuple-element.25.pool_ref.mine_ref), channel_id=1, source_target_pairs={{0,1},{1,0},{2,3},{3,2},{4,5},{5,4},{6,7},{7,6},{8,9},{9,8},{10,11... | collective-permute-start | bytes 393224 | tf_op jit(solution)/shard_map/ppermute | solution.py:276

commit v12 on v11

--- a/solution.py
+++ b/solution.py
@@ -186,13 +186,16 @@
     return [rows[:, i * page : (i + 1) * page].reshape(-1, dim).astype(jnp.bfloat16) for i in range(2)]
 
 
-def above_level(pair, q_ref, bias, level_ref, pool_ref):
+def shift_of(pair, bias, level_ref):
+    return bias - spread(level_ref[pair[0]], level_ref[pair[1]], bias.shape[1])
+
+
+def above_level(pair, q_ref, shift, pool_ref):
     tokens, q_heads, dim = q_ref.shape
     group = q_heads // 4
     rows = [q_ref[:, place_of(step, group), :].reshape(tokens * group, dim) for step in pair]
     keys = blocks(*[kinds_of(pool_ref, step)[0] for step in pair])
-    scores = scores_of(jnp.concatenate(rows, 1), keys)
-    return scores + bias - spread(level_ref[pair[0]], level_ref[pair[1]], scores.shape[1])
+    return scores_of(jnp.concatenate(rows, 1), keys) + shift
 
 
 def weigh_pair(pair, weights, pool_ref):
@@ -205,21 +208,22 @@
     return jnp.concatenate([ref[step] for step in pair], 1)
 
 
-def first_half_kernel(q_ref, bias_ref, other_ref, level_ref, pool_ref, sums_ref, totals_ref, peak_ref):
+def first_half_kernel(q_ref, bias_ref, other_ref, level_ref, pool_ref, sums_ref, totals_ref, peak_ref, shift_ref):
     peak = None
-    scores = [above_level(pair, q_ref, bias_ref[0:1], level_ref, pool_ref) for pair in PAIRS]
+    scores = [above_level(pair, q_ref, shift_of(pair, bias_ref[0:1], level_ref), pool_ref) for pair in PAIRS]
     for i, pair in enumerate(PAIRS):
         weights = jnp.exp2(scores[i]).astype(jnp.bfloat16)
         peak = weights if peak is None else jnp.maximum(peak, weights)
         sums, totals = weigh_pair(pair, weights, pool_ref)
         sums_ref[i] = sums + side_by_side(other_ref, pair)
         totals_ref[i] = totals + 1.0
+        shift_ref[i] = shift_of(pair, bias_ref[8:9], level_ref)
     peak = jnp.max(peak.astype(jnp.float32), axis=0, keepdims=True)
     peak_ref[...] = jnp.broadcast_to(peak, peak_ref.shape)
 
 
 def second_half_kernel(
-    q_ref, bias_ref, other_ref, level_ref, mine_ref, sums_ref, totals_ref, peak_ref, theirs_ref,
+    q_ref, bias_ref, other_ref, level_ref, mine_ref, sums_ref, totals_ref, peak_ref, shift_ref, theirs_ref,
     out_hbm, stage_ref, sems,
 ):
     tokens, q_heads, dim = q_ref.shape
@@ -235,7 +239,7 @@
             copies[-1].start()
         return copies
 
-    scores = [above_level(pair, q_ref, bias_ref[8:9], level_ref, theirs_ref) for pair in PAIRS]
+    scores = [above_level(pair, q_ref, shift_ref[i], theirs_ref) for i, pair in enumerate(PAIRS)]
     writes, weights = [], []
     for i, pair in enumerate(PAIRS):
         weights.append(jnp.exp2(scores[i]).astype(jnp.bfloat16))
@@ -247,9 +251,9 @@
 
     @pl.when(peak > 2.0**100)
     def _():
-        for pair in PAIRS:
-            mine = above_level(pair, q_ref, bias_ref[0:1], level_ref, mine_ref)
-            theirs = above_level(pair, q_ref, bias_ref[8:9], level_ref, theirs_ref)
+        for i, pair in enumerate(PAIRS):
+            mine = above_level(pair, q_ref, shift_of(pair, bias_ref[0:1], level_ref), mine_ref)
+            theirs = above_level(pair, q_ref, shift_ref[i], theirs_ref)
             both = jnp.maximum(mine, theirs)
             half = both.shape[1] // 2
             first = lax.broadcasted_iota(jnp.int32, both.shape, 1) < half
@@ -322,26 +326,27 @@
     mine, level = hand_over(SHORT, mine, level)
     theirs = swap(mine, 1)
     limit = pltpu.CompilerParams(vmem_limit_bytes=(24 if stripes <= 8 else 48) * 2**20)
-    sums, totals, peak = pl.pallas_call(
+    sums, totals, peak, shift = pl.pallas_call(
         first_half_kernel,
         out_shape=[jax.ShapeDtypeStruct((len(PAIRS), rows, 2 * dim), jnp.float32)] * 2
-        + [jax.ShapeDtypeStruct((8, bias.shape[1]), jnp.float32)],
+        + [jax.ShapeDtypeStruct((8, bias.shape[1]), jnp.float32)]
+        + [jax.ShapeDtypeStruct((len(PAIRS), rows, bias.shape[1]), jnp.float32)],
         in_specs=[vmem] * 5,
-        out_specs=[vmem] * 3,
+        out_specs=[vmem] * 4,
         compiler_params=limit,
         cost_estimate=SHORT,
     )(queries, bias, other, level, mine)
     return pl.pallas_call(
         second_half_kernel,
         out_shape=jax.ShapeDtypeStruct(queries.shape, jnp.bfloat16),
-        in_specs=[vmem] * 9,
+        in_specs=[vmem] * 10,
         out_specs=hbm,
         scratch_shapes=[
             pltpu.VMEM((tp, tokens, q_heads // tp, dim), jnp.bfloat16),
             pltpu.SemaphoreType.DMA((tp,)),
         ],
         compiler_params=limit,
-    )(queries, bias, other, level, mine, sums, totals, peak, theirs)
+    )(queries, bias, other, level, mine, sums, totals, peak, shift, theirs)
 
 
 def solution(mesh):

time: 20.1 us -> 20.1 us (level)
  no operation moved by 1% of the time
where the time goes in v12:
time: 20.1 us; the launch traced here: 19.9 us
  starting transfers between devices  8.61 us (43%)
  Pallas kernels  5.94 us (30%)
  waiting for transfers between devices  4.62 us (23%)
  between operations  0.71 us (4%)
    all_to_all x1, starting transfers between devices, per_device(): lax.all_to_all(sent.reshape(tp * stripes, 2 * page, dim), ('tp', 'pool'),...  4.92 us
    ppermute x4, starting transfers between devices, per_device(): lax.ppermute(array, 'tp', [(i, i ^ bit) for i in range(tp)])  3.69 us
    all_to_all x1, waiting for transfers between devices, per_device(): lax.all_to_all(sent.reshape(tp * stripes, 2 * page, dim), ('tp', 'pool'),...  3.43 us
    pallas_call x1, Pallas kernels, per_device(): pl.pallas_call(functools.partial(own_kernel, page=page), out_shape=[jax.S...  2.48 us
    pallas_call x1, Pallas kernels, per_device(): pl.pallas_call(functools.partial(select_kernel, page), out_shape=[jax.Sha...  1.52 us
    pallas_call x1, Pallas kernels, per_device(): pl.pallas_call(second_half_kernel, out_shape=jax.ShapeDtypeStruct(queries...  1.34 us
    ppermute x4, waiting for transfers between devices, per_device(): lax.ppermute(array, 'tp', [(i, i ^ bit) for i in range(tp)])  1.2 us
    pallas_call x1, Pallas kernels, per_device(): pl.pallas_call(first_half_kernel, out_shape=[jax.ShapeDtypeStruct((len(PA...  0.59 us
  transfers between devices with their start and end apart: 5, of which 4 were waited for; matrix products, arithmetic and copies ran while one was open for 0% of the time, Pallas kernels for 15%

profile of v12, /device:TPU:0, one launch (start us, length us, event | category | flops | bytes accessed | tf_op | source)
XLA Modules:
  0.0 19.9 jit_solution(17132552086335200919)
XLA Ops:
  0.0 1.5 %shard_map.82 = (bf16[4,8,16,128]{3,2,1,0:T(8,128)(2,1)}, bf16[768,128]{1,0:T(8,128)(2,1)S(1)}, f32[16,128]{1,0:T(8,128)S(1)}) custom-call(s32[13]{0:T(128)} %parent_hbm.1, s32[5]{0:T(128)} %pages_hbm.1, s32[5]{0:T(128)} %owner_hbm.1, bf16[80,128]{1,0:T(8,128)(2,1)} %bitcast.8, bf16[512,128]{1,0:T(8,128)(2,1)} %bitcast.6, bf16[256,128]{1,0:T(8,128)(2,1)} %bitcast.7), custom_call_target="tpu_custom_call" | custom-call | flops 49999998976 | bytes 1000000 | tf_op jit(solution)/shard_map/pallas_call | solution.py:287
  1.5 3.0 %collective-permute-start = (bf16[768,128]{1,0:T(8,128)(2,1)S(1)}, bf16[768,128]{1,0:T(8,128)(2,1)S(1)}, u32[]{:S(2)}, u32[]{:S(2)}) collective-permute-start(bf16[768,128]{1,0:T(8,128)(2,1)S(1)} %get-tuple-element.19.refs_0_), channel_id=1, source_target_pairs={{0,2},{1,3},{2,0},{3,1},{4,6},{5,7},{6,4},{7,5},{8,10},{9,11},{10,... | collective-permute-start | bytes 589832 | tf_op jit(solution)/shard_map/ppermute | solution.py:280
  4.5 4.9 %all-to-all-start = ((bf16[32,16,128]{2,1,0:T(8,128)(2,1)}), bf16[32,16,128]{2,1,0:T(8,128)(2,1)S(1)}, u32[]{:S(2)}, u32[]{:S(2)}) async-start(bf16[32,16,128]{2,1,0:T(8,128)(2,1)} %bitcast.3), calls=%async_computation | async-start | bytes 262144 | tf_op jit(solution)/shard_map/all_to_all | solution.py:309
  9.5 0.0 copy-start
  9.5 0.0 collective-permute-done.refs_1_
  9.5 0.3 %collective-permute-start.1 = (bf16[768,128]{1,0:T(8,128)(2,1)S(1)}, bf16[768,128]{1,0:T(8,128)(2,1)S(1)}, u32[]{:S(2)}, u32[]{:S(2)}) collective-permute-start(bf16[768,128]{1,0:T(8,128)(2,1)S(1)} %get-tuple-element.20.rest_0_), channel_id=1, source_target_pairs={{0,1},{1,0},{2,3},{3,2},{4,5},{5,4},{6,7},{7,6},{8,9},{9,8},{10,11... | collective-permute-start | bytes 589832 | tf_op jit(solution)/shard_map/ppermute | solution.py:280
  9.8 0.3 %collective-permute-start.2 = (bf16[768,128]{1,0:T(8,128)(2,1)S(1)}, bf16[768,128]{1,0:T(8,128)(2,1)S(1)}, u32[]{:S(2)}, u32[]{:S(2)}) collective-permute-start(bf16[768,128]{1,0:T(8,128)(2,1)S(1)} %get-tuple-element.21.rest_2_), channel_id=1, source_target_pairs={{0,1},{1,0},{2,3},{3,2},{4,5},{5,4},{6,7},{7,6},{8,9},{9,8},{10,11... | collective-permute-start | bytes 589832 | tf_op jit(solution)/shard_map/ppermute | solution.py:280
  10.7 0.3 %collective-permute-done.1.rest_1_ = bf16[768,128]{1,0:T(8,128)(2,1)S(1)} collective-permute-done((bf16[768,128]{1,0:T(8,128)(2,1)S(1)}, bf16[768,128]{1,0:T(8,128)(2,1)S(1)}, u32[]{:S(2)}, u32[]{:S(2)}) %collective-permute-start.1) | collective-permute-done | bytes 196640 | tf_op jit(solution)/shard_map/ppermute | solution.py:280
  11.0 0.3 %collective-permute-done.2.rest_3_ = bf16[768,128]{1,0:T(8,128)(2,1)S(1)} collective-permute-done((bf16[768,128]{1,0:T(8,128)(2,1)S(1)}, bf16[768,128]{1,0:T(8,128)(2,1)S(1)}, u32[]{:S(2)}, u32[]{:S(2)}) %collective-permute-start.2) | collective-permute-done | bytes 196640 | tf_op jit(solution)/shard_map/ppermute | solution.py:280
  11.3 0.0 copy-done
  11.3 2.5 %shard_map.84 = (f32[4,512,128]{2,1,0:T(8,128)S(1)}, f32[4,512,128]{2,1,0:T(8,128)S(1)}) custom-call(s32[1]{0:T(128)S(6)} %copy.17.leaf_len_ref, bf16[32,64,128]{2,1,0:T(8,128)(2,1)S(1)} %copy-done, bf16[768,128]{1,0:T(8,128)(2,1)S(1)} %get-tuple-element.20.rest_0_, bf16[768,128]{1,0:T(8,128)(2,1)S(1)} %collective-permute-done.1.rest_1_, ...), custom_call_target="tpu_custom_call" | custom-call | flops 1000000 | bytes 100000 | tf_op jit(solution)/shard_map/pallas_call | solution.py:316
  13.8 3.4 %all-to-all-done = bf16[32,16,128]{2,1,0:T(8,128)(2,1)S(1)} async-done(((bf16[32,16,128]{2,1,0:T(8,128)(2,1)}), bf16[32,16,128]{2,1,0:T(8,128)(2,1)S(1)}, u32[]{:S(2)}, u32[]{:S(2)}) %all-to-all-start) | async-done | bytes 131104 | tf_op jit(solution)/shard_map/all_to_all | solution.py:309
  17.2 0.1 collective-permute-start.3
  17.3 0.6 %shard_map.86 = (f32[2,512,256]{2,1,0:T(8,128)S(1)}, f32[2,512,256]{2,1,0:T(8,128)S(1)}, f32[8,128]{1,0:T(8,128)S(1)}, f32[2,512,128]{2,1,0:T(8,128)S(1)}) custom-call(bf16[32,64,128]{2,1,0:T(8,128)(2,1)S(1)} %copy-done, f32[16,128]{1,0:T(8,128)S(1)} %get-tuple-element.18.bias_ref, f32[4,512,128]{2,1,0:T(8,128)S(1)} %get-tuple-element.22.other_ref, ...), custom_call_target="tpu_custom_call" | custom-call | flops 1000000 | bytes 100000 | tf_op jit(solution)/shard_map/pallas_call | solution.py:329
  17.9 0.6 %collective-permute-done.3.theirs_ref = bf16[4,8,16,128]{3,2,1,0:T(8,128)(2,1)S(1)} collective-permute-done((bf16[4,8,16,128]{3,2,1,0:T(8,128)(2,1)S(1)}, bf16[4,8,16,128]{3,2,1,0:T(8,128)(2,1)S(1)}, u32[]{:S(2)}, u32[]{:S(2)}) %collective-permute-start.3) | collective-permute-done | bytes 131104 | tf_op jit(solution)/shard_map/ppermute | solution.py:280
  18.6 1.3 %shard_map.87 = bf16[32,64,128]{2,1,0:T(8,128)(2,1)} custom-call(bf16[32,64,128]{2,1,0:T(8,128)(2,1)S(1)} %copy-done, f32[16,128]{1,0:T(8,128)S(1)} %get-tuple-element.18.bias_ref, f32[4,512,128]{2,1,0:T(8,128)S(1)} %get-tuple-element.22.other_ref, f32[4,512,128]{2,1,0:T(8,128)S(1)} %get-tuple-element.25.level_ref, ...), custom_call_target="tpu_custom_call" | custom-call | tf_op jit(solution)/shard_map/pallas_call | solution.py:339
  (2 shorter events, 0.0 us)
Async XLA Ops:
  1.5 7.9 %collective-permute-start = (bf16[768,128]{1,0:T(8,128)(2,1)S(1)}, bf16[768,128]{1,0:T(8,128)(2,1)S(1)}, u32[]{:S(2)}, u32[]{:S(2)}) collective-permute-start(bf16[768,128]{1,0:T(8,128)(2,1)S(1)} %get-tuple-element.19.refs_0_), channel_id=1, source_target_pairs={{0,2},{1,3},{2,0},{3,1},{4,6},{5,7},{6,4},{7,5},{8,10},{9,11},{10,... | collective-permute-start | bytes 589832 | tf_op jit(solution)/shard_map/ppermute | solution.py:280
  4.5 12.7 %all-to-all-start = ((bf16[32,16,128]{2,1,0:T(8,128)(2,1)}), bf16[32,16,128]{2,1,0:T(8,128)(2,1)S(1)}, u32[]{:S(2)}, u32[]{:S(2)}) async-start(bf16[32,16,128]{2,1,0:T(8,128)(2,1)} %bitcast.3), calls=%async_computation | async-start | bytes 262144 | tf_op jit(solution)/shard_map/all_to_all | solution.py:309
  9.5 1.8 %copy-start = (bf16[32,64,128]{2,1,0:T(8,128)(2,1)S(1)}, bf16[32,64,128]{2,1,0:T(8,128)(2,1)}, u32[]{:S(2)}) copy-start(bf16[32,64,128]{2,1,0:T(8,128)(2,1)} %q_ref.5) | copy-start | bytes 1572868
  9.5 1.5 %collective-permute-start.1 = (bf16[768,128]{1,0:T(8,128)(2,1)S(1)}, bf16[768,128]{1,0:T(8,128)(2,1)S(1)}, u32[]{:S(2)}, u32[]{:S(2)}) collective-permute-start(bf16[768,128]{1,0:T(8,128)(2,1)S(1)} %get-tuple-element.20.rest_0_), channel_id=1, source_target_pairs={{0,1},{1,0},{2,3},{3,2},{4,5},{5,4},{6,7},{7,6},{8,9},{9,8},{10,11... | collective-permute-start | bytes 589832 | tf_op jit(solution)/shard_map/ppermute | solution.py:280
  9.8 1.5 %collective-permute-start.2 = (bf16[768,128]{1,0:T(8,128)(2,1)S(1)}, bf16[768,128]{1,0:T(8,128)(2,1)S(1)}, u32[]{:S(2)}, u32[]{:S(2)}) collective-permute-start(bf16[768,128]{1,0:T(8,128)(2,1)S(1)} %get-tuple-element.21.rest_2_), channel_id=1, source_target_pairs={{0,1},{1,0},{2,3},{3,2},{4,5},{5,4},{6,7},{7,6},{8,9},{9,8},{10,11... | collective-permute-start | bytes 589832 | tf_op jit(solution)/shard_map/ppermute | solution.py:280
  17.2 1.3 %collective-permute-start.3 = (bf16[4,8,16,128]{3,2,1,0:T(8,128)(2,1)S(1)}, bf16[4,8,16,128]{3,2,1,0:T(8,128)(2,1)S(1)}, u32[]{:S(2)}, u32[]{:S(2)}) collective-permute-start(bf16[4,8,16,128]{3,2,1,0:T(8,128)(2,1)S(1)} %get-tuple-element.26.pool_ref.mine_ref), channel_id=1, source_target_pairs={{0,1},{1,0},{2,3},{3,2},{4,5},{5,4},{6,7},{7,6},{8,9},{9,8},{10,11... | collective-permute-start | bytes 393224 | tf_op jit(solution)/shard_map/ppermute | solution.py:280

commit v13 on v11

--- a/solution.py
+++ b/solution.py
@@ -38,8 +38,10 @@
         (fresh_hbm, local_ref.at[pl.ds(leaf_rows, fresh_rows)]),
     ]
     fetches = [pltpu.make_async_copy(*pair, sems.at[i]) for i, pair in enumerate(pairs)]
-    for fetch in fetches:
+    for fetch in fetches[:4]:
         fetch.start()
+    for fetch in fetches[4:]:
+        fetch.start(priority=1)
     node_count = pool_ref.shape[0] // (2 * page)
     copies, requests = out_hbm.shape[:2]
     fetches[0].wait()
@@ -232,7 +234,7 @@
             stage_ref[step] = part.astype(jnp.bfloat16).reshape(tokens, group, dim)
             target = out_hbm.at[:, place_of(step, group)]
             copies.append(pltpu.make_async_copy(stage_ref.at[step], target, sems.at[step]))
-            copies[-1].start()
+            copies[-1].start(priority=i)
         return copies
 
     scores = [above_level(pair, q_ref, bias_ref[8:9], level_ref, theirs_ref) for pair in PAIRS]

time: 20.1 us -> 20.1 us (level)
  no operation moved by 1% of the time
where the time goes in v13:
time: 20.1 us; the launch traced here: 19.9 us
  starting transfers between devices  8.61 us (43%)
  Pallas kernels  5.91 us (29%)
  waiting for transfers between devices  4.65 us (23%)
  between operations  0.71 us (4%)
    all_to_all x1, starting transfers between devices, per_device(): lax.all_to_all(sent.reshape(tp * stripes, 2 * page, dim), ('tp', 'pool'),...  4.92 us
    ppermute x4, starting transfers between devices, per_device(): lax.ppermute(array, 'tp', [(i, i ^ bit) for i in range(tp)])  3.69 us
    all_to_all x1, waiting for transfers between devices, per_device(): lax.all_to_all(sent.reshape(tp * stripes, 2 * page, dim), ('tp', 'pool'),...  3.43 us
    pallas_call x1, Pallas kernels, per_device(): pl.pallas_call(functools.partial(own_kernel, page=page), out_shape=[jax.S...  2.48 us
    pallas_call x1, Pallas kernels, per_device(): pl.pallas_call(functools.partial(select_kernel, page), out_shape=[jax.Sha...  1.52 us
    pallas_call x1, Pallas kernels, per_device(): pl.pallas_call(second_half_kernel, out_shape=jax.ShapeDtypeStruct(queries...  1.34 us
    ppermute x4, waiting for transfers between devices, per_device(): lax.ppermute(array, 'tp', [(i, i ^ bit) for i in range(tp)])  1.22 us
    pallas_call x1, Pallas kernels, per_device(): pl.pallas_call(first_half_kernel, out_shape=[jax.ShapeDtypeStruct((len(PA...  0.57 us
  transfers between devices with their start and end apart: 5, of which 4 were waited for; matrix products, arithmetic and copies ran while one was open for 0% of the time, Pallas kernels for 15%

profile of v13, /device:TPU:0, one launch (start us, length us, event | category | flops | bytes accessed | tf_op | source)
XLA Modules:
  0.0 19.9 jit_solution(17545824177620347185)
XLA Ops:
  0.0 1.5 %shard_map.82 = (bf16[4,8,16,128]{3,2,1,0:T(8,128)(2,1)}, bf16[768,128]{1,0:T(8,128)(2,1)S(1)}, f32[16,128]{1,0:T(8,128)S(1)}) custom-call(s32[13]{0:T(128)} %parent_hbm.1, s32[5]{0:T(128)} %pages_hbm.1, s32[5]{0:T(128)} %owner_hbm.1, bf16[80,128]{1,0:T(8,128)(2,1)} %bitcast.8, bf16[512,128]{1,0:T(8,128)(2,1)} %bitcast.6, bf16[256,128]{1,0:T(8,128)(2,1)} %bitcast.7), custom_call_target="tpu_custom_call" | custom-call | flops 49999998976 | bytes 1000000 | tf_op jit(solution)/shard_map/pallas_call | solution.py:285
  1.5 3.0 %collective-permute-start = (bf16[768,128]{1,0:T(8,128)(2,1)S(1)}, bf16[768,128]{1,0:T(8,128)(2,1)S(1)}, u32[]{:S(2)}, u32[]{:S(2)}) collective-permute-start(bf16[768,128]{1,0:T(8,128)(2,1)S(1)} %get-tuple-element.18.refs_0_), channel_id=1, source_target_pairs={{0,2},{1,3},{2,0},{3,1},{4,6},{5,7},{6,4},{7,5},{8,10},{9,11},{10,... | collective-permute-start | bytes 589832 | tf_op jit(solution)/shard_map/ppermute | solution.py:278
  4.5 4.9 %all-to-all-start = ((bf16[32,16,128]{2,1,0:T(8,128)(2,1)}), bf16[32,16,128]{2,1,0:T(8,128)(2,1)S(1)}, u32[]{:S(2)}, u32[]{:S(2)}) async-start(bf16[32,16,128]{2,1,0:T(8,128)(2,1)} %bitcast.3), calls=%async_computation | async-start | bytes 262144 | tf_op jit(solution)/shard_map/all_to_all | solution.py:307
  9.5 0.0 copy-start
  9.5 0.0 collective-permute-done.refs_1_
  9.5 0.3 %collective-permute-start.1 = (bf16[768,128]{1,0:T(8,128)(2,1)S(1)}, bf16[768,128]{1,0:T(8,128)(2,1)S(1)}, u32[]{:S(2)}, u32[]{:S(2)}) collective-permute-start(bf16[768,128]{1,0:T(8,128)(2,1)S(1)} %get-tuple-element.19.rest_0_), channel_id=1, source_target_pairs={{0,1},{1,0},{2,3},{3,2},{4,5},{5,4},{6,7},{7,6},{8,9},{9,8},{10,11... | collective-permute-start | bytes 589832 | tf_op jit(solution)/shard_map/ppermute | solution.py:278
  9.8 0.3 %collective-permute-start.2 = (bf16[768,128]{1,0:T(8,128)(2,1)S(1)}, bf16[768,128]{1,0:T(8,128)(2,1)S(1)}, u32[]{:S(2)}, u32[]{:S(2)}) collective-permute-start(bf16[768,128]{1,0:T(8,128)(2,1)S(1)} %get-tuple-element.20.rest_2_), channel_id=1, source_target_pairs={{0,1},{1,0},{2,3},{3,2},{4,5},{5,4},{6,7},{7,6},{8,9},{9,8},{10,11... | collective-permute-start | bytes 589832 | tf_op jit(solution)/shard_map/ppermute | solution.py:278
  10.7 0.3 %collective-permute-done.1.rest_1_ = bf16[768,128]{1,0:T(8,128)(2,1)S(1)} collective-permute-done((bf16[768,128]{1,0:T(8,128)(2,1)S(1)}, bf16[768,128]{1,0:T(8,128)(2,1)S(1)}, u32[]{:S(2)}, u32[]{:S(2)}) %collective-permute-start.1) | collective-permute-done | bytes 196640 | tf_op jit(solution)/shard_map/ppermute | solution.py:278
  11.0 0.3 %collective-permute-done.2.rest_3_ = bf16[768,128]{1,0:T(8,128)(2,1)S(1)} collective-permute-done((bf16[768,128]{1,0:T(8,128)(2,1)S(1)}, bf16[768,128]{1,0:T(8,128)(2,1)S(1)}, u32[]{:S(2)}, u32[]{:S(2)}) %collective-permute-start.2) | collective-permute-done | bytes 196640 | tf_op jit(solution)/shard_map/ppermute | solution.py:278
  11.3 0.0 copy-done
  11.3 2.5 %shard_map.84 = (f32[4,512,128]{2,1,0:T(8,128)S(1)}, f32[4,512,128]{2,1,0:T(8,128)S(1)}) custom-call(s32[1]{0:T(128)S(6)} %copy.17.leaf_len_ref, bf16[32,64,128]{2,1,0:T(8,128)(2,1)S(1)} %copy-done, bf16[768,128]{1,0:T(8,128)(2,1)S(1)} %get-tuple-element.19.rest_0_, bf16[768,128]{1,0:T(8,128)(2,1)S(1)} %collective-permute-done.1.rest_1_, ...), custom_call_target="tpu_custom_call" | custom-call | flops 1000000 | bytes 100000 | tf_op jit(solution)/shard_map/pallas_call | solution.py:314
  13.8 3.4 %all-to-all-done = bf16[32,16,128]{2,1,0:T(8,128)(2,1)S(1)} async-done(((bf16[32,16,128]{2,1,0:T(8,128)(2,1)}), bf16[32,16,128]{2,1,0:T(8,128)(2,1)S(1)}, u32[]{:S(2)}, u32[]{:S(2)}) %all-to-all-start) | async-done | bytes 131104 | tf_op jit(solution)/shard_map/all_to_all | solution.py:307
  17.2 0.1 collective-permute-start.3
  17.3 0.6 %shard_map.86 = (f32[2,512,256]{2,1,0:T(8,128)S(1)}, f32[2,512,256]{2,1,0:T(8,128)S(1)}, f32[8,128]{1,0:T(8,128)S(1)}) custom-call(bf16[32,64,128]{2,1,0:T(8,128)(2,1)S(1)} %copy-done, f32[16,128]{1,0:T(8,128)S(1)} %get-tuple-element.17.bias_ref, f32[4,512,128]{2,1,0:T(8,128)S(1)} %get-tuple-element.21.other_ref, ...), custom_call_target="tpu_custom_call" | custom-call | flops 1000000 | bytes 100000 | tf_op jit(solution)/shard_map/pallas_call | solution.py:327
  17.9 0.7 %collective-permute-done.3.theirs_ref = bf16[4,8,16,128]{3,2,1,0:T(8,128)(2,1)S(1)} collective-permute-done((bf16[4,8,16,128]{3,2,1,0:T(8,128)(2,1)S(1)}, bf16[4,8,16,128]{3,2,1,0:T(8,128)(2,1)S(1)}, u32[]{:S(2)}, u32[]{:S(2)}) %collective-permute-start.3) | collective-permute-done | bytes 131104 | tf_op jit(solution)/shard_map/ppermute | solution.py:278
  18.6 1.3 %shard_map.87 = bf16[32,64,128]{2,1,0:T(8,128)(2,1)} custom-call(bf16[32,64,128]{2,1,0:T(8,128)(2,1)S(1)} %copy-done, f32[16,128]{1,0:T(8,128)S(1)} %get-tuple-element.17.bias_ref, f32[4,512,128]{2,1,0:T(8,128)S(1)} %get-tuple-element.21.other_ref, f32[4,512,128]{2,1,0:T(8,128)S(1)} %get-tuple-element.24.level_ref, ...), custom_call_target="tpu_custom_call" | custom-call | tf_op jit(solution)/shard_map/pallas_call | solution.py:336
  (2 shorter events, 0.0 us)
Async XLA Ops:
  1.5 7.9 %collective-permute-start = (bf16[768,128]{1,0:T(8,128)(2,1)S(1)}, bf16[768,128]{1,0:T(8,128)(2,1)S(1)}, u32[]{:S(2)}, u32[]{:S(2)}) collective-permute-start(bf16[768,128]{1,0:T(8,128)(2,1)S(1)} %get-tuple-element.18.refs_0_), channel_id=1, source_target_pairs={{0,2},{1,3},{2,0},{3,1},{4,6},{5,7},{6,4},{7,5},{8,10},{9,11},{10,... | collective-permute-start | bytes 589832 | tf_op jit(solution)/shard_map/ppermute | solution.py:278
  4.5 12.7 %all-to-all-start = ((bf16[32,16,128]{2,1,0:T(8,128)(2,1)}), bf16[32,16,128]{2,1,0:T(8,128)(2,1)S(1)}, u32[]{:S(2)}, u32[]{:S(2)}) async-start(bf16[32,16,128]{2,1,0:T(8,128)(2,1)} %bitcast.3), calls=%async_computation | async-start | bytes 262144 | tf_op jit(solution)/shard_map/all_to_all | solution.py:307
  9.5 1.8 %copy-start = (bf16[32,64,128]{2,1,0:T(8,128)(2,1)S(1)}, bf16[32,64,128]{2,1,0:T(8,128)(2,1)}, u32[]{:S(2)}) copy-start(bf16[32,64,128]{2,1,0:T(8,128)(2,1)} %q_ref.5) | copy-start | bytes 1572868
  9.5 1.5 %collective-permute-start.1 = (bf16[768,128]{1,0:T(8,128)(2,1)S(1)}, bf16[768,128]{1,0:T(8,128)(2,1)S(1)}, u32[]{:S(2)}, u32[]{:S(2)}) collective-permute-start(bf16[768,128]{1,0:T(8,128)(2,1)S(1)} %get-tuple-element.19.rest_0_), channel_id=1, source_target_pairs={{0,1},{1,0},{2,3},{3,2},{4,5},{5,4},{6,7},{7,6},{8,9},{9,8},{10,11... | collective-permute-start | bytes 589832 | tf_op jit(solution)/shard_map/ppermute | solution.py:278
  9.8 1.5 %collective-permute-start.2 = (bf16[768,128]{1,0:T(8,128)(2,1)S(1)}, bf16[768,128]{1,0:T(8,128)(2,1)S(1)}, u32[]{:S(2)}, u32[]{:S(2)}) collective-permute-start(bf16[768,128]{1,0:T(8,128)(2,1)S(1)} %get-tuple-element.20.rest_2_), channel_id=1, source_target_pairs={{0,1},{1,0},{2,3},{3,2},{4,5},{5,4},{6,7},{7,6},{8,9},{9,8},{10,11... | collective-permute-start | bytes 589832 | tf_op jit(solution)/shard_map/ppermute | solution.py:278
  17.2 1.3 %collective-permute-start.3 = (bf16[4,8,16,128]{3,2,1,0:T(8,128)(2,1)S(1)}, bf16[4,8,16,128]{3,2,1,0:T(8,128)(2,1)S(1)}, u32[]{:S(2)}, u32[]{:S(2)}) collective-permute-start(bf16[4,8,16,128]{3,2,1,0:T(8,128)(2,1)S(1)} %get-tuple-element.25.pool_ref.mine_ref), channel_id=1, source_target_pairs={{0,1},{1,0},{2,3},{3,2},{4,5},{5,4},{6,7},{7,6},{8,9},{9,8},{10,11... | collective-permute-start | bytes 393224 | tf_op jit(solution)/shard_map/ppermute | solution.py:278

commit v14 on v11

--- a/solution.py
+++ b/solution.py
@@ -38,11 +38,13 @@
         (fresh_hbm, local_ref.at[pl.ds(leaf_rows, fresh_rows)]),
     ]
     fetches = [pltpu.make_async_copy(*pair, sems.at[i]) for i, pair in enumerate(pairs)]
-    for fetch in fetches:
+    for fetch in fetches[:4]:
         fetch.start()
     node_count = pool_ref.shape[0] // (2 * page)
     copies, requests = out_hbm.shape[:2]
     fetches[0].wait()
+    for fetch in fetches[4:]:
+        fetch.start()
     rows_ref[...] = pool_ref[...].astype(jnp.float32)
     root = [rows_ref[pl.ds(kind, page, stride=2)] for kind in range(2)]
     fetches[1].wait()
@@ -235,10 +237,10 @@
             copies[-1].start()
         return copies
 
-    scores = [above_level(pair, q_ref, bias_ref[8:9], level_ref, theirs_ref) for pair in PAIRS]
     writes, weights = [], []
     for i, pair in enumerate(PAIRS):
-        weights.append(jnp.exp2(scores[i]).astype(jnp.bfloat16))
+        scores = above_level(pair, q_ref, bias_ref[8:9], level_ref, theirs_ref)
+        weights.append(jnp.exp2(scores).astype(jnp.bfloat16))
         sums, totals = weigh_pair(pair, weights[-1], theirs_ref)
         writes += write(pair, over(sums + sums_ref[i], totals + totals_ref[i]))
     peak = jnp.maximum(jnp.max(functools.reduce(jnp.maximum, weights).astype(jnp.float32)), jnp.max(peak_ref[...]))

time: 20.1 us -> 20.5 us (1.020)
  Pallas kernels: 5.91 us -> 6.25 us
where the time goes in v14:
time: 20.5 us; the launch traced here: 20.2 us
  starting transfers between devices  8.61 us (42%)
  Pallas kernels  6.25 us (30%)
  waiting for transfers between devices  4.64 us (23%)
  between operations  0.71 us (3%)
    all_to_all x1, starting transfers between devices, per_device(): lax.all_to_all(sent.reshape(tp * stripes, 2 * page, dim), ('tp', 'pool'),...  4.92 us
    ppermute x4, starting transfers between devices, per_device(): lax.ppermute(array, 'tp', [(i, i ^ bit) for i in range(tp)])  3.69 us
    all_to_all x1, waiting for transfers between devices, per_device(): lax.all_to_all(sent.reshape(tp * stripes, 2 * page, dim), ('tp', 'pool'),...  3.41 us
    pallas_call x1, Pallas kernels, per_device(): pl.pallas_call(functools.partial(own_kernel, page=page), out_shape=[jax.S...  2.49 us
    pallas_call x1, Pallas kernels, per_device(): pl.pallas_call(functools.partial(select_kernel, page), out_shape=[jax.Sha...  1.69 us
    pallas_call x1, Pallas kernels, per_device(): pl.pallas_call(second_half_kernel, out_shape=jax.ShapeDtypeStruct(queries...  1.49 us
    ppermute x4, waiting for transfers between devices, per_device(): lax.ppermute(array, 'tp', [(i, i ^ bit) for i in range(tp)])  1.22 us
    pallas_call x1, Pallas kernels, per_device(): pl.pallas_call(first_half_kernel, out_shape=[jax.ShapeDtypeStruct((len(PA...  0.57 us
  transfers between devices with their start and end apart: 5, of which 4 were waited for; matrix products, arithmetic and copies ran while one was open for 0% of the time, Pallas kernels for 15%

profile of v14, /device:TPU:0, one launch (start us, length us, event | category | flops | bytes accessed | tf_op | source)
XLA Modules:
  0.0 20.2 jit_solution(1837987458561759881)
XLA Ops:
  0.0 1.7 %shard_map.82 = (bf16[4,8,16,128]{3,2,1,0:T(8,128)(2,1)}, bf16[768,128]{1,0:T(8,128)(2,1)S(1)}, f32[16,128]{1,0:T(8,128)S(1)}) custom-call(s32[13]{0:T(128)} %parent_hbm.1, s32[5]{0:T(128)} %pages_hbm.1, s32[5]{0:T(128)} %owner_hbm.1, bf16[80,128]{1,0:T(8,128)(2,1)} %bitcast.8, bf16[512,128]{1,0:T(8,128)(2,1)} %bitcast.6, bf16[256,128]{1,0:T(8,128)(2,1)} %bitcast.7), custom_call_target="tpu_custom_call" | custom-call | flops 49999998976 | bytes 1000000 | tf_op jit(solution)/shard_map/pallas_call | solution.py:285
  1.7 3.0 %collective-permute-start = (bf16[768,128]{1,0:T(8,128)(2,1)S(1)}, bf16[768,128]{1,0:T(8,128)(2,1)S(1)}, u32[]{:S(2)}, u32[]{:S(2)}) collective-permute-start(bf16[768,128]{1,0:T(8,128)(2,1)S(1)} %get-tuple-element.18.refs_0_), channel_id=1, source_target_pairs={{0,2},{1,3},{2,0},{3,1},{4,6},{5,7},{6,4},{7,5},{8,10},{9,11},{10,... | collective-permute-start | bytes 589832 | tf_op jit(solution)/shard_map/ppermute | solution.py:278
  4.7 4.9 %all-to-all-start = ((bf16[32,16,128]{2,1,0:T(8,128)(2,1)}), bf16[32,16,128]{2,1,0:T(8,128)(2,1)S(1)}, u32[]{:S(2)}, u32[]{:S(2)}) async-start(bf16[32,16,128]{2,1,0:T(8,128)(2,1)} %bitcast.3), calls=%async_computation | async-start | bytes 262144 | tf_op jit(solution)/shard_map/all_to_all | solution.py:307
  9.6 0.0 copy-start
  9.6 0.0 collective-permute-done.refs_1_
  9.7 0.3 %collective-permute-start.1 = (bf16[768,128]{1,0:T(8,128)(2,1)S(1)}, bf16[768,128]{1,0:T(8,128)(2,1)S(1)}, u32[]{:S(2)}, u32[]{:S(2)}) collective-permute-start(bf16[768,128]{1,0:T(8,128)(2,1)S(1)} %get-tuple-element.19.rest_0_), channel_id=1, source_target_pairs={{0,1},{1,0},{2,3},{3,2},{4,5},{5,4},{6,7},{7,6},{8,9},{9,8},{10,11... | collective-permute-start | bytes 589832 | tf_op jit(solution)/shard_map/ppermute | solution.py:278
  10.0 0.3 %collective-permute-start.2 = (bf16[768,128]{1,0:T(8,128)(2,1)S(1)}, bf16[768,128]{1,0:T(8,128)(2,1)S(1)}, u32[]{:S(2)}, u32[]{:S(2)}) collective-permute-start(bf16[768,128]{1,0:T(8,128)(2,1)S(1)} %get-tuple-element.20.rest_2_), channel_id=1, source_target_pairs={{0,1},{1,0},{2,3},{3,2},{4,5},{5,4},{6,7},{7,6},{8,9},{9,8},{10,11... | collective-permute-start | bytes 589832 | tf_op jit(solution)/shard_map/ppermute | solution.py:278
  10.9 0.3 %collective-permute-done.1.rest_1_ = bf16[768,128]{1,0:T(8,128)(2,1)S(1)} collective-permute-done((bf16[768,128]{1,0:T(8,128)(2,1)S(1)}, bf16[768,128]{1,0:T(8,128)(2,1)S(1)}, u32[]{:S(2)}, u32[]{:S(2)}) %collective-permute-start.1) | collective-permute-done | bytes 196640 | tf_op jit(solution)/shard_map/ppermute | solution.py:278
  11.2 0.3 %collective-permute-done.2.rest_3_ = bf16[768,128]{1,0:T(8,128)(2,1)S(1)} collective-permute-done((bf16[768,128]{1,0:T(8,128)(2,1)S(1)}, bf16[768,128]{1,0:T(8,128)(2,1)S(1)}, u32[]{:S(2)}, u32[]{:S(2)}) %collective-permute-start.2) | collective-permute-done | bytes 196640 | tf_op jit(solution)/shard_map/ppermute | solution.py:278
  11.5 0.0 copy-done
  11.5 2.5 %shard_map.84 = (f32[4,512,128]{2,1,0:T(8,128)S(1)}, f32[4,512,128]{2,1,0:T(8,128)S(1)}) custom-call(s32[1]{0:T(128)S(6)} %copy.17.leaf_len_ref, bf16[32,64,128]{2,1,0:T(8,128)(2,1)S(1)} %copy-done, bf16[768,128]{1,0:T(8,128)(2,1)S(1)} %get-tuple-element.19.rest_0_, bf16[768,128]{1,0:T(8,128)(2,1)S(1)} %collective-permute-done.1.rest_1_, ...), custom_call_target="tpu_custom_call" | custom-call | flops 1000000 | bytes 100000 | tf_op jit(solution)/shard_map/pallas_call | solution.py:314
  14.0 3.4 %all-to-all-done = bf16[32,16,128]{2,1,0:T(8,128)(2,1)S(1)} async-done(((bf16[32,16,128]{2,1,0:T(8,128)(2,1)}), bf16[32,16,128]{2,1,0:T(8,128)(2,1)S(1)}, u32[]{:S(2)}, u32[]{:S(2)}) %all-to-all-start) | async-done | bytes 131104 | tf_op jit(solution)/shard_map/all_to_all | solution.py:307
  17.4 0.1 collective-permute-start.3
  17.5 0.6 %shard_map.86 = (f32[2,512,256]{2,1,0:T(8,128)S(1)}, f32[2,512,256]{2,1,0:T(8,128)S(1)}, f32[8,128]{1,0:T(8,128)S(1)}) custom-call(bf16[32,64,128]{2,1,0:T(8,128)(2,1)S(1)} %copy-done, f32[16,128]{1,0:T(8,128)S(1)} %get-tuple-element.17.bias_ref, f32[4,512,128]{2,1,0:T(8,128)S(1)} %get-tuple-element.21.other_ref, ...), custom_call_target="tpu_custom_call" | custom-call | flops 1000000 | bytes 100000 | tf_op jit(solution)/shard_map/pallas_call | solution.py:327
  18.1 0.7 %collective-permute-done.3.theirs_ref = bf16[4,8,16,128]{3,2,1,0:T(8,128)(2,1)S(1)} collective-permute-done((bf16[4,8,16,128]{3,2,1,0:T(8,128)(2,1)S(1)}, bf16[4,8,16,128]{3,2,1,0:T(8,128)(2,1)S(1)}, u32[]{:S(2)}, u32[]{:S(2)}) %collective-permute-start.3) | collective-permute-done | bytes 131104 | tf_op jit(solution)/shard_map/ppermute | solution.py:278
  18.7 1.5 %shard_map.87 = bf16[32,64,128]{2,1,0:T(8,128)(2,1)} custom-call(bf16[32,64,128]{2,1,0:T(8,128)(2,1)S(1)} %copy-done, f32[16,128]{1,0:T(8,128)S(1)} %get-tuple-element.17.bias_ref, f32[4,512,128]{2,1,0:T(8,128)S(1)} %get-tuple-element.21.other_ref, f32[4,512,128]{2,1,0:T(8,128)S(1)} %get-tuple-element.24.level_ref, ...), custom_call_target="tpu_custom_call" | custom-call | tf_op jit(solution)/shard_map/pallas_call | solution.py:336
  (2 shorter events, 0.0 us)
Async XLA Ops:
  1.7 7.9 %collective-permute-start = (bf16[768,128]{1,0:T(8,128)(2,1)S(1)}, bf16[768,128]{1,0:T(8,128)(2,1)S(1)}, u32[]{:S(2)}, u32[]{:S(2)}) collective-permute-start(bf16[768,128]{1,0:T(8,128)(2,1)S(1)} %get-tuple-element.18.refs_0_), channel_id=1, source_target_pairs={{0,2},{1,3},{2,0},{3,1},{4,6},{5,7},{6,4},{7,5},{8,10},{9,11},{10,... | collective-permute-start | bytes 589832 | tf_op jit(solution)/shard_map/ppermute | solution.py:278
  4.7 12.7 %all-to-all-start = ((bf16[32,16,128]{2,1,0:T(8,128)(2,1)}), bf16[32,16,128]{2,1,0:T(8,128)(2,1)S(1)}, u32[]{:S(2)}, u32[]{:S(2)}) async-start(bf16[32,16,128]{2,1,0:T(8,128)(2,1)} %bitcast.3), calls=%async_computation | async-start | bytes 262144 | tf_op jit(solution)/shard_map/all_to_all | solution.py:307
  9.6 1.8 %copy-start = (bf16[32,64,128]{2,1,0:T(8,128)(2,1)S(1)}, bf16[32,64,128]{2,1,0:T(8,128)(2,1)}, u32[]{:S(2)}) copy-start(bf16[32,64,128]{2,1,0:T(8,128)(2,1)} %q_ref.5) | copy-start | bytes 1572868
  9.7 1.5 %collective-permute-start.1 = (bf16[768,128]{1,0:T(8,128)(2,1)S(1)}, bf16[768,128]{1,0:T(8,128)(2,1)S(1)}, u32[]{:S(2)}, u32[]{:S(2)}) collective-permute-start(bf16[768,128]{1,0:T(8,128)(2,1)S(1)} %get-tuple-element.19.rest_0_), channel_id=1, source_target_pairs={{0,1},{1,0},{2,3},{3,2},{4,5},{5,4},{6,7},{7,6},{8,9},{9,8},{10,11... | collective-permute-start | bytes 589832 | tf_op jit(solution)/shard_map/ppermute | solution.py:278
  10.0 1.5 %collective-permute-start.2 = (bf16[768,128]{1,0:T(8,128)(2,1)S(1)}, bf16[768,128]{1,0:T(8,128)(2,1)S(1)}, u32[]{:S(2)}, u32[]{:S(2)}) collective-permute-start(bf16[768,128]{1,0:T(8,128)(2,1)S(1)} %get-tuple-element.20.rest_2_), channel_id=1, source_target_pairs={{0,1},{1,0},{2,3},{3,2},{4,5},{5,4},{6,7},{7,6},{8,9},{9,8},{10,11... | collective-permute-start | bytes 589832 | tf_op jit(solution)/shard_map/ppermute | solution.py:278
  17.4 1.3 %collective-permute-start.3 = (bf16[4,8,16,128]{3,2,1,0:T(8,128)(2,1)S(1)}, bf16[4,8,16,128]{3,2,1,0:T(8,128)(2,1)S(1)}, u32[]{:S(2)}, u32[]{:S(2)}) collective-permute-start(bf16[4,8,16,128]{3,2,1,0:T(8,128)(2,1)S(1)} %get-tuple-element.25.pool_ref.mine_ref), channel_id=1, source_target_pairs={{0,1},{1,0},{2,3},{3,2},{4,5},{5,4},{6,7},{7,6},{8,9},{9,8},{10,11... | collective-permute-start | bytes 393224 | tf_op jit(solution)/shard_map/ppermute | solution.py:278

commit v15 on v11

--- a/solution.py
+++ b/solution.py
@@ -236,10 +236,10 @@
         return copies
 
     scores = [above_level(pair, q_ref, bias_ref[8:9], level_ref, theirs_ref) for pair in PAIRS]
-    writes, weights = [], []
-    for i, pair in enumerate(PAIRS):
-        weights.append(jnp.exp2(scores[i]).astype(jnp.bfloat16))
-        sums, totals = weigh_pair(pair, weights[-1], theirs_ref)
+    weights = [jnp.exp2(score).astype(jnp.bfloat16) for score in scores]
+    found = [weigh_pair(pair, weights[i], theirs_ref) for i, pair in enumerate(PAIRS)]
+    writes = []
+    for i, (pair, (sums, totals)) in enumerate(zip(PAIRS, found)):
         writes += write(pair, over(sums + sums_ref[i], totals + totals_ref[i]))
     peak = jnp.maximum(jnp.max(functools.reduce(jnp.maximum, weights).astype(jnp.float32)), jnp.max(peak_ref[...]))
     for copy in writes:

time: 20.1 us -> 20.1 us (level)
  no operation moved by 1% of the time
where the time goes in v15:
time: 20.1 us; the launch traced here: 19.9 us
  starting transfers between devices  8.61 us (43%)
  Pallas kernels  5.91 us (29%)
  waiting for transfers between devices  4.65 us (23%)
  between operations  0.71 us (4%)
    all_to_all x1, starting transfers between devices, per_device(): lax.all_to_all(sent.reshape(tp * stripes, 2 * page, dim), ('tp', 'pool'),...  4.92 us
    ppermute x4, starting transfers between devices, per_device(): lax.ppermute(array, 'tp', [(i, i ^ bit) for i in range(tp)])  3.69 us
    all_to_all x1, waiting for transfers between devices, per_device(): lax.all_to_all(sent.reshape(tp * stripes, 2 * page, dim), ('tp', 'pool'),...  3.43 us
    pallas_call x1, Pallas kernels, per_device(): pl.pallas_call(functools.partial(own_kernel, page=page), out_shape=[jax.S...  2.48 us
    pallas_call x1, Pallas kernels, per_device(): pl.pallas_call(functools.partial(select_kernel, page), out_shape=[jax.Sha...  1.52 us
    pallas_call x1, Pallas kernels, per_device(): pl.pallas_call(second_half_kernel, out_shape=jax.ShapeDtypeStruct(queries...  1.34 us
    ppermute x4, waiting for transfers between devices, per_device(): lax.ppermute(array, 'tp', [(i, i ^ bit) for i in range(tp)])  1.22 us
    pallas_call x1, Pallas kernels, per_device(): pl.pallas_call(first_half_kernel, out_shape=[jax.ShapeDtypeStruct((len(PA...  0.57 us
  transfers between devices with their start and end apart: 5, of which 4 were waited for; matrix products, arithmetic and copies ran while one was open for 0% of the time, Pallas kernels for 15%

profile of v15, /device:TPU:0, one launch (start us, length us, event | category | flops | bytes accessed | tf_op | source)
XLA Modules:
  0.0 19.9 jit_solution(9065362107499404102)
XLA Ops:
  0.0 1.5 %shard_map.82 = (bf16[4,8,16,128]{3,2,1,0:T(8,128)(2,1)}, bf16[768,128]{1,0:T(8,128)(2,1)S(1)}, f32[16,128]{1,0:T(8,128)S(1)}) custom-call(s32[13]{0:T(128)} %parent_hbm.1, s32[5]{0:T(128)} %pages_hbm.1, s32[5]{0:T(128)} %owner_hbm.1, bf16[80,128]{1,0:T(8,128)(2,1)} %bitcast.8, bf16[512,128]{1,0:T(8,128)(2,1)} %bitcast.6, bf16[256,128]{1,0:T(8,128)(2,1)} %bitcast.7), custom_call_target="tpu_custom_call" | custom-call | flops 49999998976 | bytes 1000000 | tf_op jit(solution)/shard_map/pallas_call | solution.py:283
  1.5 3.0 %collective-permute-start = (bf16[768,128]{1,0:T(8,128)(2,1)S(1)}, bf16[768,128]{1,0:T(8,128)(2,1)S(1)}, u32[]{:S(2)}, u32[]{:S(2)}) collective-permute-start(bf16[768,128]{1,0:T(8,128)(2,1)S(1)} %get-tuple-element.18.refs_0_), channel_id=1, source_target_pairs={{0,2},{1,3},{2,0},{3,1},{4,6},{5,7},{6,4},{7,5},{8,10},{9,11},{10,... | collective-permute-start | bytes 589832 | tf_op jit(solution)/shard_map/ppermute | solution.py:276
  4.5 4.9 %all-to-all-start = ((bf16[32,16,128]{2,1,0:T(8,128)(2,1)}), bf16[32,16,128]{2,1,0:T(8,128)(2,1)S(1)}, u32[]{:S(2)}, u32[]{:S(2)}) async-start(bf16[32,16,128]{2,1,0:T(8,128)(2,1)} %bitcast.3), calls=%async_computation | async-start | bytes 262144 | tf_op jit(solution)/shard_map/all_to_all | solution.py:305
  9.5 0.0 copy-start
  9.5 0.0 collective-permute-done.refs_1_
  9.5 0.3 %collective-permute-start.1 = (bf16[768,128]{1,0:T(8,128)(2,1)S(1)}, bf16[768,128]{1,0:T(8,128)(2,1)S(1)}, u32[]{:S(2)}, u32[]{:S(2)}) collective-permute-start(bf16[768,128]{1,0:T(8,128)(2,1)S(1)} %get-tuple-element.19.rest_0_), channel_id=1, source_target_pairs={{0,1},{1,0},{2,3},{3,2},{4,5},{5,4},{6,7},{7,6},{8,9},{9,8},{10,11... | collective-permute-start | bytes 589832 | tf_op jit(solution)/shard_map/ppermute | solution.py:276
  9.8 0.3 %collective-permute-start.2 = (bf16[768,128]{1,0:T(8,128)(2,1)S(1)}, bf16[768,128]{1,0:T(8,128)(2,1)S(1)}, u32[]{:S(2)}, u32[]{:S(2)}) collective-permute-start(bf16[768,128]{1,0:T(8,128)(2,1)S(1)} %get-tuple-element.20.rest_2_), channel_id=1, source_target_pairs={{0,1},{1,0},{2,3},{3,2},{4,5},{5,4},{6,7},{7,6},{8,9},{9,8},{10,11... | collective-permute-start | bytes 589832 | tf_op jit(solution)/shard_map/ppermute | solution.py:276
  10.7 0.3 %collective-permute-done.1.rest_1_ = bf16[768,128]{1,0:T(8,128)(2,1)S(1)} collective-permute-done((bf16[768,128]{1,0:T(8,128)(2,1)S(1)}, bf16[768,128]{1,0:T(8,128)(2,1)S(1)}, u32[]{:S(2)}, u32[]{:S(2)}) %collective-permute-start.1) | collective-permute-done | bytes 196640 | tf_op jit(solution)/shard_map/ppermute | solution.py:276
  11.0 0.3 %collective-permute-done.2.rest_3_ = bf16[768,128]{1,0:T(8,128)(2,1)S(1)} collective-permute-done((bf16[768,128]{1,0:T(8,128)(2,1)S(1)}, bf16[768,128]{1,0:T(8,128)(2,1)S(1)}, u32[]{:S(2)}, u32[]{:S(2)}) %collective-permute-start.2) | collective-permute-done | bytes 196640 | tf_op jit(solution)/shard_map/ppermute | solution.py:276
  11.3 0.0 copy-done
  11.3 2.5 %shard_map.84 = (f32[4,512,128]{2,1,0:T(8,128)S(1)}, f32[4,512,128]{2,1,0:T(8,128)S(1)}) custom-call(s32[1]{0:T(128)S(6)} %copy.17.leaf_len_ref, bf16[32,64,128]{2,1,0:T(8,128)(2,1)S(1)} %copy-done, bf16[768,128]{1,0:T(8,128)(2,1)S(1)} %get-tuple-element.19.rest_0_, bf16[768,128]{1,0:T(8,128)(2,1)S(1)} %collective-permute-done.1.rest_1_, ...), custom_call_target="tpu_custom_call" | custom-call | flops 1000000 | bytes 100000 | tf_op jit(solution)/shard_map/pallas_call | solution.py:312
  13.8 3.4 %all-to-all-done = bf16[32,16,128]{2,1,0:T(8,128)(2,1)S(1)} async-done(((bf16[32,16,128]{2,1,0:T(8,128)(2,1)}), bf16[32,16,128]{2,1,0:T(8,128)(2,1)S(1)}, u32[]{:S(2)}, u32[]{:S(2)}) %all-to-all-start) | async-done | bytes 131104 | tf_op jit(solution)/shard_map/all_to_all | solution.py:305
  17.2 0.1 collective-permute-start.3
  17.3 0.6 %shard_map.86 = (f32[2,512,256]{2,1,0:T(8,128)S(1)}, f32[2,512,256]{2,1,0:T(8,128)S(1)}, f32[8,128]{1,0:T(8,128)S(1)}) custom-call(bf16[32,64,128]{2,1,0:T(8,128)(2,1)S(1)} %copy-done, f32[16,128]{1,0:T(8,128)S(1)} %get-tuple-element.17.bias_ref, f32[4,512,128]{2,1,0:T(8,128)S(1)} %get-tuple-element.21.other_ref, ...), custom_call_target="tpu_custom_call" | custom-call | flops 1000000 | bytes 100000 | tf_op jit(solution)/shard_map/pallas_call | solution.py:325
  17.9 0.7 %collective-permute-done.3.theirs_ref = bf16[4,8,16,128]{3,2,1,0:T(8,128)(2,1)S(1)} collective-permute-done((bf16[4,8,16,128]{3,2,1,0:T(8,128)(2,1)S(1)}, bf16[4,8,16,128]{3,2,1,0:T(8,128)(2,1)S(1)}, u32[]{:S(2)}, u32[]{:S(2)}) %collective-permute-start.3) | collective-permute-done | bytes 131104 | tf_op jit(solution)/shard_map/ppermute | solution.py:276
  18.6 1.3 %shard_map.87 = bf16[32,64,128]{2,1,0:T(8,128)(2,1)} custom-call(bf16[32,64,128]{2,1,0:T(8,128)(2,1)S(1)} %copy-done, f32[16,128]{1,0:T(8,128)S(1)} %get-tuple-element.17.bias_ref, f32[4,512,128]{2,1,0:T(8,128)S(1)} %get-tuple-element.21.other_ref, f32[4,512,128]{2,1,0:T(8,128)S(1)} %get-tuple-element.24.level_ref, ...), custom_call_target="tpu_custom_call" | custom-call | tf_op jit(solution)/shard_map/pallas_call | solution.py:334
  (2 shorter events, 0.0 us)
Async XLA Ops:
  1.5 7.9 %collective-permute-start = (bf16[768,128]{1,0:T(8,128)(2,1)S(1)}, bf16[768,128]{1,0:T(8,128)(2,1)S(1)}, u32[]{:S(2)}, u32[]{:S(2)}) collective-permute-start(bf16[768,128]{1,0:T(8,128)(2,1)S(1)} %get-tuple-element.18.refs_0_), channel_id=1, source_target_pairs={{0,2},{1,3},{2,0},{3,1},{4,6},{5,7},{6,4},{7,5},{8,10},{9,11},{10,... | collective-permute-start | bytes 589832 | tf_op jit(solution)/shard_map/ppermute | solution.py:276
  4.5 12.7 %all-to-all-start = ((bf16[32,16,128]{2,1,0:T(8,128)(2,1)}), bf16[32,16,128]{2,1,0:T(8,128)(2,1)S(1)}, u32[]{:S(2)}, u32[]{:S(2)}) async-start(bf16[32,16,128]{2,1,0:T(8,128)(2,1)} %bitcast.3), calls=%async_computation | async-start | bytes 262144 | tf_op jit(solution)/shard_map/all_to_all | solution.py:305
  9.5 1.8 %copy-start = (bf16[32,64,128]{2,1,0:T(8,128)(2,1)S(1)}, bf16[32,64,128]{2,1,0:T(8,128)(2,1)}, u32[]{:S(2)}) copy-start(bf16[32,64,128]{2,1,0:T(8,128)(2,1)} %q_ref.5) | copy-start | bytes 1572868
  9.5 1.5 %collective-permute-start.1 = (bf16[768,128]{1,0:T(8,128)(2,1)S(1)}, bf16[768,128]{1,0:T(8,128)(2,1)S(1)}, u32[]{:S(2)}, u32[]{:S(2)}) collective-permute-start(bf16[768,128]{1,0:T(8,128)(2,1)S(1)} %get-tuple-element.19.rest_0_), channel_id=1, source_target_pairs={{0,1},{1,0},{2,3},{3,2},{4,5},{5,4},{6,7},{7,6},{8,9},{9,8},{10,11... | collective-permute-start | bytes 589832 | tf_op jit(solution)/shard_map/ppermute | solution.py:276
  9.8 1.5 %collective-permute-start.2 = (bf16[768,128]{1,0:T(8,128)(2,1)S(1)}, bf16[768,128]{1,0:T(8,128)(2,1)S(1)}, u32[]{:S(2)}, u32[]{:S(2)}) collective-permute-start(bf16[768,128]{1,0:T(8,128)(2,1)S(1)} %get-tuple-element.20.rest_2_), channel_id=1, source_target_pairs={{0,1},{1,0},{2,3},{3,2},{4,5},{5,4},{6,7},{7,6},{8,9},{9,8},{10,11... | collective-permute-start | bytes 589832 | tf_op jit(solution)/shard_map/ppermute | solution.py:276
  17.2 1.3 %collective-permute-start.3 = (bf16[4,8,16,128]{3,2,1,0:T(8,128)(2,1)S(1)}, bf16[4,8,16,128]{3,2,1,0:T(8,128)(2,1)S(1)}, u32[]{:S(2)}, u32[]{:S(2)}) collective-permute-start(bf16[4,8,16,128]{3,2,1,0:T(8,128)(2,1)S(1)} %get-tuple-element.25.pool_ref.mine_ref), channel_id=1, source_target_pairs={{0,1},{1,0},{2,3},{3,2},{4,5},{5,4},{6,7},{7,6},{8,9},{9,8},{10,11... | collective-permute-start | bytes 393224 | tf_op jit(solution)/shard_map/ppermute | solution.py:276
